TPU v7x, 128 devices: a whole 4x4x4 slice. The times are simulated.
128 devices in a mesh: row: 8 (over x, core), col: 16 (over z, y).
Axes of the slice: x: 4, y: 4, z: 4, core: 2. Of those that a mesh axis runs over, the one named last changes fastest.
Arguments:
- jac_cam: float32 [8, 18, 16384], P(None, None, ('row', 'col')), may hold values from -4 to 4
- jac_pt: float32 [8, 6, 16384], P(None, None, ('row', 'col')), may hold values from -6 to 6
- resid: float32 [8, 2, 16384], P(None, None, ('row', 'col')), may hold values from -6 to 6
- point_damp: float32 [3, 16384], P(None, ('row', 'col')), may hold values from 0.2 to 2
- cam_damp: float32 [16, 576], P('col'), may hold values from 0.5 to 4
- obs_cluster: int32 [16384, 8], P(('row', 'col')), may hold values from 0 to 15, all different within a row; in each aligned block of 128 rows (0 to 127, 128 to 255, ...) at most 96 rows name the same one
- obs_slot: int32 [8, 16384], P(None, ('row', 'col')), may hold values from 0 to 63
Outputs:
- schur: float32 [16, 16, 576, 576], P('row', 'col')
- step: float32 [9216], replicated
- residual: float32 [9216], replicated
- direction: float32 [9216], replicated
Inputs may be any that keep to these rules, and one draw needn't show every extreme that they name: `obs_cluster`: the 8 observations of a point lie in 8 different clusters. Among the 128 points of one device (aligned blocks of rows), no cluster is named by more than 96 points, and in every draw some cluster is named by exactly 96 points of some device.
All inputs are finite; a program needn't handle non-finite values.
Results may differ from a plain program's by a relative error of at most 0.0003.
Values sent between devices are 32-bit elements; how exact they have to be, the bound alone decides.
No kernel may reach another device: no remote copies, remote signals or barrier semaphores. Data moves between devices by JAX's collectives and lax.ppermute only.
A program may use at most 192 MiB of HBM per device.

v0:
```python
import jax
import jax.numpy as jnp
from jax import lax
from jax.sharding import PartitionSpec as P

KOBS = 8


def point_factors(jac_cam, jac_pt, resid, point_damp):
    cam_rows = jac_cam.reshape(KOBS, 2, 9, -1)
    pnt_rows = jac_pt.reshape(KOBS, 2, 3, -1)

    def inner(first, second):
        return jnp.sum(pnt_rows[:, :, first, :] * pnt_rows[:, :, second, :], axis=(0, 1))

    diag_aa = inner(0, 0) + point_damp[0]
    diag_bb = inner(1, 1) + point_damp[1]
    diag_cc = inner(2, 2) + point_damp[2]
    lower_aa = jnp.sqrt(diag_aa)
    lower_ba = inner(1, 0) / lower_aa
    lower_ca = inner(2, 0) / lower_aa
    lower_bb = jnp.sqrt(diag_bb - lower_ba * lower_ba)
    lower_cb = (inner(2, 1) - lower_ca * lower_ba) / lower_bb
    lower_cc = jnp.sqrt(diag_cc - lower_ca * lower_ca - lower_cb * lower_cb)

    def solve_lower(vec_a, vec_b, vec_c):
        out_a = vec_a / lower_aa
        out_b = (vec_b - lower_ba * out_a) / lower_bb
        out_c = (vec_c - lower_ca * out_a - lower_cb * out_b) / lower_cc
        return [out_a, out_b, out_c]

    whiten = solve_lower(pnt_rows[:, :, 0, :], pnt_rows[:, :, 1, :], pnt_rows[:, :, 2, :])
    coupled = [jnp.sum(cam_rows * part[:, :, None, :], axis=1) for part in whiten]
    grads = [jnp.sum(pnt_rows[:, :, member, :] * resid, axis=(0, 1)) for member in range(3)]
    reduced = solve_lower(grads[0], grads[1], grads[2])
    factor = jnp.stack([cam_rows[:, 0], cam_rows[:, 1]] + coupled, axis=1)
    shaped = [jnp.broadcast_to(part, resid[:, 0].shape) for part in reduced]
    targets = jnp.stack([-resid[:, 0], -resid[:, 1]] + shaped, axis=1)
    return (factor, targets)


def spread(weights, values):
    return jnp.einsum("csg,sfg->cfg", weights, values, precision=lax.Precision.HIGHEST)


def shards(jac_cam, jac_pt, resid, point_damp, cam_damp, obs_cluster, obs_slot):
    highest = lax.Precision.HIGHEST
    n_row = lax.axis_size("row")
    n_col = lax.axis_size("col")
    per_row = n_col // n_row
    tile = cam_damp.shape[1]
    cams = tile // 9
    points = jac_cam.shape[2]
    capacity = min(points, 3 * points * KOBS // (2 * n_col))
    width = per_row * capacity
    fields = 97
    factor, targets = point_factors(jac_cam, jac_pt, resid, point_damp)
    clusters = obs_cluster.T
    labels = jnp.arange(n_col, dtype=jnp.int32)
    named_count = jnp.sum(
        (clusters[:, :, None] == labels[None, None, :]).astype(jnp.float32), axis=0
    )
    order = jnp.arange(points, dtype=jnp.int32)
    earlier = (order[None, :] < order[:, None]).astype(jnp.float32)
    before = jnp.dot(earlier, named_count, precision=highest)
    rank_rows = jnp.stack(
        [
            jnp.sum(jnp.where(clusters[member][:, None] == labels[None, :], before, 0.0), axis=1)
            for member in range(KOBS)
        ]
    )
    slot_target = clusters.astype(jnp.float32) * capacity + rank_rows
    total_slots = n_col * capacity
    slot_ids = jnp.arange(total_slots, dtype=jnp.float32)
    placing = (slot_target.reshape(-1)[:, None] == slot_ids[None, :]).astype(jnp.float32)
    slot_float = obs_slot.astype(jnp.float32)
    own_rows = jnp.concatenate(
        [factor.reshape(KOBS, 45, points), targets, slot_float[:, None, :]], axis=1
    )
    own_slots = jnp.dot(
        own_rows.transpose(1, 0, 2).reshape(51, KOBS * points), placing, precision=highest
    )
    shared = jnp.concatenate(
        [factor.reshape(KOBS * 45, points), slot_float, clusters.astype(jnp.float32)], axis=0
    )
    point_place = jnp.sum(placing.reshape(KOBS, points, total_slots), axis=0)
    shared_slots = jnp.dot(shared, point_place, precision=highest)
    other_rows = shared_slots[: KOBS * 45].reshape(KOBS, 45, total_slots)
    other_slot = shared_slots[KOBS * 45 : KOBS * 46][:, None, :]
    other_cluster = shared_slots[KOBS * 46 :]
    column_ids = labels.astype(jnp.float32)
    routing = (other_cluster[None, :, :] == column_ids[:, None, None]).astype(jnp.float32)
    present = jnp.sum(routing, axis=1)
    packed = jnp.concatenate(
        [
            own_slots[None, 0:45] * present[:, None, :],
            spread(routing, other_rows),
            own_slots[None, 45:51] * present[:, None, :],
            spread(routing, other_slot),
        ],
        axis=1,
    )
    outgoing = packed.reshape(n_col, fields, n_row, width).transpose(2, 0, 1, 3)
    incoming = lax.all_to_all(
        outgoing.reshape(n_row * n_col, fields, width),
        ("row", "col"),
        split_axis=0,
        concat_axis=0,
        tiled=True,
    )
    sources = n_row * n_col
    incoming = incoming.reshape(sources, fields, per_row, capacity)
    my_row = lax.axis_index("row")
    my_col = lax.axis_index("col")
    damp_col = cam_damp[0]
    tiles = []
    rhs_part = jnp.zeros((tile,), jnp.float32)
    diag_part = jnp.zeros((tile,), jnp.float32)
    minus = jnp.full((3,), -1.0, jnp.float32)
    cam_ids = jnp.arange(cams, dtype=jnp.int32)
    for member in range(per_row):
        cluster_id = my_row * per_row + member
        on_diag = (cluster_id == my_col).astype(jnp.float32)
        block = incoming[:, :, member, :]
        row_side = block[:, 0:45].reshape(sources, 5, 9, capacity)
        col_side = block[:, 45:90].reshape(sources, 5, 9, capacity)
        weights = block[:, 90:95]
        left = block[:, 95].astype(jnp.int32)
        right = block[:, 96].astype(jnp.int32)
        signs = jnp.concatenate([jnp.stack([on_diag, on_diag]), minus])
        product = jnp.sum(
            row_side[:, :, :, None, :]
            * signs[None, :, None, None, None]
            * col_side[:, :, None, :, :],
            axis=1,
        )
        product_rows = product.transpose(0, 3, 1, 2).reshape(-1, 81)
        where = (left * cams + right).reshape(-1)
        flat = jnp.zeros((cams * cams, 81), jnp.float32).at[where].add(product_rows)
        tile_block = flat.reshape(cams, cams, 9, 9).transpose(0, 2, 1, 3).reshape(tile, tile)
        tile_block = tile_block + on_diag * jnp.diag(damp_col)
        rhs_term = jnp.sum(row_side * weights[:, :, None, :], axis=1)
        rhs_rows = rhs_term.transpose(0, 2, 1).reshape(-1, 9)
        cam_pick = (left.reshape(-1)[None, :] == cam_ids[:, None]).astype(jnp.float32)
        rhs_flat = jnp.dot(cam_pick, rhs_rows, precision=highest)
        rhs_part = rhs_part + on_diag * rhs_flat.reshape(tile)
        diag_part = diag_part + on_diag * jnp.diagonal(tile_block)
        tiles.append(tile_block)
    rhs_col, diag_col = lax.psum((rhs_part, diag_part), "row")
    rhs, precond = (
        lax.all_gather(rhs_col, "col", axis=0, tiled=True),
        lax.all_gather(diag_col, "col", axis=0, tiled=True),
    )
    start = rhs / precond
    rz_first = jnp.sum(rhs * start)
    own_piece = lax.dynamic_slice_in_dim(start, my_col * tile, tile)
    local = jnp.concatenate(
        [jnp.dot(block_tile, own_piece, precision=highest) for block_tile in tiles]
    )
    summed = lax.psum(local, "col")
    image = lax.all_gather(summed, "row", axis=0, tiled=True)
    alpha = rz_first / jnp.sum(start * image)
    step = alpha * start
    residual = rhs - alpha * image
    second_z = residual / precond
    beta = jnp.sum(residual * second_z) / rz_first
    direction = second_z + beta * start
    schur = jnp.stack(tiles)[:, None, :, :]
    return (schur, step, residual, direction)


def solution(mesh):
    placed = (
        P(None, None, ("row", "col")),
        P(None, None, ("row", "col")),
        P(None, None, ("row", "col")),
        P(None, ("row", "col")),
        P("col", None),
        P(("row", "col"), None),
        P(None, ("row", "col")),
    )
    return jax.shard_map(
        shards,
        mesh=mesh,
        in_specs=placed,
        out_specs=(P("row", "col", None, None), P(), P(), P()),
        check_vma=False,
    )
```

profile of v0, /device:TPU:24, one launch (start us, length us, event | category | flops | bytes accessed | tf_op | source)
XLA Modules:
  0.0 794.6 jit_solution(17134670752762577608)
XLA Ops:
  7.2 1.0 slice_bitcast_fusion.10
  10.3 0.8 rsqrt_multiply_fusion
  12.7 0.9 multiply_reduce_fusion.6
  13.6 0.9 pad_maximum_fusion.1
  16.2 2.0 fusion.25
  18.2 1.5 slice.161
  20.5 2.3 fusion.3
  22.8 2.0 reshape.415
  24.9 4.4 copy.127
  29.5 8.3 %fusion.2 = f32[16,1536]{0,1:T(8,128)S(1)} fusion(f32[16]{0:T(128)S(1)} %iota_convert_fusion, f32[8,1536]{0,1:T(8,128)S(1)} %copy.126), kind=kLoop, calls=%fused_computation.11 | loop fusion | flops 565248 | bytes 147520 | tf_op jit(solution)/shard_map/reduce_sum | solution.py:93
  37.9 15.8 %fusion.4 = f32[16,45,1536]{1,0,2:T(8,128)} fusion(f32[8,45,1536]{1,0,2:T(8,128)} %copy.127, f32[16]{0:T(128)S(1)} %iota_convert_fusion, f32[8,1536]{0,1:T(8,128)S(1)} %copy.126), kind=kOutput, calls=%fused_computation.21 | convolution fusion | flops 106364928 | bytes 6684736 | tf_op jit(solution)/shard_map/csg,sfg->cfg/dot_general | solution.py:43
  54.3 9.8 %broadcast_multiply_fusion.1 = f32[16,45,1536]{1,0,2:T(8,128)} fusion(f32[16,1536]{0,1:T(8,128)S(1)} %fusion.2, f32[45,1536]{0,1:T(8,128)S(1)} %copy.124), kind=kLoop, calls=%fused_computation.14 | loop fusion | flops 1105920 | bytes 4798464 | tf_op jit(solution)/shard_map/mul | solution.py:96
  64.1 9.7 %broadcast_multiply_fusion = f32[16,6,1536]{1,0,2:T(8,128)} fusion(f32[16,1536]{0,1:T(8,128)S(1)} %fusion.2, f32[6,1536]{0,1:T(8,128)S(1)} %copy.128), kind=kLoop, calls=%fused_computation.13 | loop fusion | flops 147456 | bytes 724992 | tf_op jit(solution)/shard_map/mul | solution.py:98
  74.1 8.4 %select_reduce_fusion = f32[1536,16]{1,0:T(8,128)S(1)} fusion(f32[1536,8]{1,0:T(8,128)S(1)} %copy.159, f32[16]{0:T(128)S(1)} %iota_convert_fusion, f32[8,1536]{0,1:T(8,128)S(1)} %copy.126), kind=kLoop, calls=%fused_computation.12 | loop fusion | flops 565248 | bytes 196672
  82.5 11.1 %copy.129 = f32[1536,1,16]{1,2,0:T(8,128)} copy(f32[1536,1,16]{2,0,1:T(8,128)S(1)} %bitcast.202) | data formatting | bytes 196608 | tf_op jit(solution)/shard_map/csg,sfg->cfg/dot_general | solution.py:43
  93.6 23.9 %pad_maximum_fusion = f32[16,97,1536]{1,0,2:T(8,128)} fusion(f32[16,1,1536]{1,0,2:T(8,128)} %bitcast.191, f32[16,6,1536]{1,0,2:T(8,128)} %broadcast_multiply_fusion, f32[16,45,1536]{1,0,2:T(8,128)} %fusion.4, f32[16,45,1536]{1,0,2:T(8,128)} %broadcast_multiply_fusion.1), kind=kLoop, calls=%fused_computation.6 | loop fusion | flops 7151616 | bytes 19070976 | tf_op jit(solution)/shard_map/concatenate | solution.py:94
  117.6 12.8 %copy.130 = f32[16,97,8,192]{1,3,0,2:T(8,128)} copy(f32[16,97,8,192]{1,0,3,2:T(8,128)} %bitcast.192) | data formatting | bytes 19070976 | tf_op jit(solution)/shard_map/reshape | solution.py:103
  130.4 10.7 %all-to-all-start = ((f32[128,97,192]{1,2,0:T(8,128)}), f32[128,97,192]{1,2,0:T(8,128)}, u32[]{:S(2)}, u32[]{:S(2)}) async-start(f32[128,97,192]{1,2,0:T(8,128)} %bitcast.190), calls=%async_computation | async-start | bytes 25165824 | tf_op jit(solution)/shard_map/all_to_all | solution.py:104
  142.9 152.8 %all-to-all-done = f32[128,97,192]{1,2,0:T(8,128)} async-done(((f32[128,97,192]{1,2,0:T(8,128)}), f32[128,97,192]{1,2,0:T(8,128)}, u32[]{:S(2)}, u32[]{:S(2)}) %all-to-all-start) | async-done | bytes 9535520 | tf_op jit(solution)/shard_map/all_to_all | solution.py:104
  295.7 12.0 %copy.131 = f32[128,97,192]{0,2,1:T(8,128)} copy(f32[128,97,192]{1,2,0:T(8,128)} %all-to-all-done) | data formatting | bytes 19070976 | tf_op jit(solution)/shard_map/all_to_all | solution.py:104
  307.7 4.7 slice_bitcast_fusion.1
  312.4 3.0 fusion.47
  316.1 1.2 multiply_reduce_fusion.2
  317.3 3.6 multiply_reduce_fusion
  320.9 5.9 copy.138
  326.8 6.6 reshape.453
  333.4 6.2 copy.139
  339.9 68.0 %scatter_custom_fusion.1 = f32[4096,81]{1,0:T(8,128)S(1)} fusion(s32[12288]{0:T(1024)S(1)} %bitcast.220, f32[12288,81]{1,0:T(8,128)} %copy.139, f32[]{:T(128)} %constant.13.clone.1), kind=kCustom, calls=%fused_computation.51 | custom fusion | flops 995328 | bytes 1327616 | tf_op jit(solution)/shard_map/scatter-add | solution.py:139
  407.9 1.9 copy.140
  409.8 2.2 reshape.423
  412.1 9.9 %copy.141 = f32[64,9,64,9]{3,2,1,0:T(8,128)} copy(f32[64,9,64,9]{2,0,3,1:T(8,128)S(1)} %bitcast.196) | data formatting | bytes 2654208 | tf_op jit(solution)/shard_map/transpose | solution.py:140
  421.9 14.7 %reshape.428 = f32[576,576]{1,0:T(8,128)} reshape(f32[64,9,64,9]{3,2,1,0:T(8,128)} %copy.141) | data formatting | bytes 2654208 | tf_op jit(solution)/shard_map/reshape | solution.py:140
  436.6 14.8 %reshape.424 = f32[1,576,576]{2,1,0:T(8,128)} reshape(f32[64,9,64,9]{3,2,1,0:T(8,128)} %copy.141) | data formatting | bytes 2654208 | tf_op jit(solution)/shard_map/reshape | solution.py:140
  451.5 1.2 multiply_reduce_fusion.3
  453.3 3.6 multiply_reduce_fusion.1
  456.8 5.9 copy.133
  462.7 6.6 reshape.445
  469.3 6.2 copy.134
  475.8 67.3 %scatter_custom_fusion = f32[4096,81]{1,0:T(8,128)S(1)} fusion(s32[12288]{0:T(1024)S(1)} %bitcast.221, f32[12288,81]{1,0:T(8,128)} %copy.134, f32[]{:T(128)} %constant.13.clone.1), kind=kCustom, calls=%fused_computation.53 | custom fusion | flops 995328 | bytes 1327616 | tf_op jit(solution)/shard_map/scatter-add | solution.py:139
  543.1 1.9 copy.135
  545.0 2.2 reshape.420
  547.3 9.9 %copy.136 = f32[64,9,64,9]{3,2,1,0:T(8,128)} copy(f32[64,9,64,9]{2,0,3,1:T(8,128)S(1)} %bitcast.197) | data formatting | bytes 2654208 | tf_op jit(solution)/shard_map/transpose | solution.py:140
  557.2 14.7 %reshape.427 = f32[576,576]{1,0:T(8,128)} reshape(f32[64,9,64,9]{3,2,1,0:T(8,128)} %copy.136) | data formatting | bytes 2654208 | tf_op jit(solution)/shard_map/reshape | solution.py:140
  571.9 14.7 %reshape.421 = f32[1,576,576]{2,1,0:T(8,128)} reshape(f32[64,9,64,9]{3,2,1,0:T(8,128)} %copy.136) | data formatting | bytes 2654208 | tf_op jit(solution)/shard_map/reshape | solution.py:140
  586.6 2.1 fusion.16
  588.7 4.9 gather_fusion
  593.6 4.9 gather_fusion.1
  599.3 1.2 copy.143
  600.6 1.3 reshape.425
  601.9 0.9 copy.144
  603.5 1.2 copy.145
  604.7 1.3 reshape.426
  606.1 2.7 fusion.20
  608.8 2.8 fusion.19
  611.8 38.8 %all-reduce.3 = (f32[576]{0:T(1024)S(1)}, f32[576]{0:T(1024)S(1)}) all-reduce(f32[576]{0:T(1024)S(1)} %add.165, f32[576]{0:T(1024)S(1)} %multiply_add_fusion.1), channel_id=1, replica_groups=mesh['row'=8,'col'=16] {'row'}, use_global_device_ids=true, to_apply=%region_29.30 | all-reduce | flops 1152 | bytes 9216 | tf_op jit(solution)/shard_map/psum | solution.py:149
  652.1 2.1 fusion.14
  654.2 1.8 maximum_bitcast_fusion
  656.0 76.5 %all-reduce.6.cloned.1.call-done = (f32[9216]{0:T(1024)}, f32[9216]{0:T(1024)}) async-done(((f32[9216]{0:T(1024)}, f32[9216]{0:T(1024)}), (f32[9216]{0:T(1024)}, f32[9216]{0:T(1024)})) %all-reduce.6.cloned.1.call-update) | async-done | bytes 73744
  732.5 0.9 div.100
  733.5 1.4 convolution_reduce_fusion.1
  734.9 1.4 convolution_reduce_fusion
  736.4 32.8 %psum.23 = f32[1152]{0:T(1024)S(1)} all-reduce(f32[1152]{0:T(1024)S(1)} %pad_maximum_fusion.2), channel_id=1, replica_groups=mesh['row'=8,'col'=16] {'col'}, use_global_device_ids=true, to_apply=%region_32.33 | all-reduce | flops 1152 | bytes 9216 | tf_op jit(solution)/shard_map/psum | solution.py:160
  769.2 13.1 %all-gather = f32[8,1,1152]{2,1,0:T(1,128)S(1)} all-gather(f32[1,1,1152]{2,1,0:T(1,128)S(1)} %reshape.463), channel_id=1, replica_groups=mesh['row'=8,'col'=16] {'row'}, dimensions={0}, use_global_device_ids=true | all-gather | bytes 41472 | tf_op jit(solution)/shard_map/all_gather | solution.py:161
  784.3 1.2 multiply_reduce_fusion.7
  (85 shorter events, 14.9 us)
Async XLA Ops:
  7.2 9.1 %copy-start.8 = (s32[8,128]{1,0:T(8,128)S(1)}, s32[8,128]{1,0:T(8,128)}, u32[]{:S(2)}) copy-start(s32[8,128]{1,0:T(8,128)} %param.13) | copy-start | bytes 12292
  22.8 2.1 copy-start.2
  37.8 15.8 %slice-start = ((f32[51,1536]{1,0:T(8,128)}), f32[45,1536]{1,0:T(8,128)S(1)}, s32[]{:S(2)}) async-start(f32[51,1536]{1,0:T(8,128)} %copy-done.2), calls=%async_computation.2 | async-start | bytes 589824 | tf_op jit(solution)/shard_map/slice | solution.py:96
  64.1 9.7 %copy-start.4 = (f32[1536,8]{0,1:T(8,128)S(1)}, f32[1536,8]{0,1:T(8,128)}, u32[]{:S(2)}) copy-start(f32[1536,8]{0,1:T(8,128)} %get-tuple-element.66) | copy-start | bytes 147460
  130.4 10.7 %copy-start.9 = (f32[1,576]{1,0:T(1,128)S(1)}, f32[1,576]{1,0:T(1,128)}, u32[]{:S(2)}) copy-start(f32[1,576]{1,0:T(1,128)} %param.11) | copy-start | bytes 6916
  130.4 10.8 %copy-start.10 = (u32[128]{0:T(128)S(1)}, u32[128]{0:T(128)}, u32[]{:S(2)}) copy-start(u32[128]{0:T(128)} %constant.70) | copy-start | bytes 1540
  130.4 165.4 %all-to-all-start = ((f32[128,97,192]{1,2,0:T(8,128)}), f32[128,97,192]{1,2,0:T(8,128)}, u32[]{:S(2)}, u32[]{:S(2)}) async-start(f32[128,97,192]{1,2,0:T(8,128)} %bitcast.190), calls=%async_computation | async-start | bytes 25165824 | tf_op jit(solution)/shard_map/all_to_all | solution.py:104
  141.0 591.5 %all-reduce.6.cloned.1.call-start = ((), (), s32[]{:S(2)}) async-start(), calls=%async_computation.1 | async-start | bytes 147456
  436.6 14.9 %copy-start.1 = (f32[128,45,96]{0,2,1:T(8,128)S(1)}, f32[128,45,96]{0,2,1:T(8,128)}, u32[]{:S(2)}) copy-start(f32[128,45,96]{0,2,1:T(8,128)} %get-tuple-element.61) | copy-start | bytes 6635524
  451.5 1.8 copy-start
  651.2 0.6 copy-start.7
  651.5 0.6 copy-start.6
  732.5 49.8 %copy-start.3 = (f32[9216]{0:T(1024)S(1)}, f32[9216]{0:T(1024)}, u32[]{:S(2)}) copy-start(f32[9216]{0:T(1024)} %get-tuple-element.42) | copy-start | bytes 110596
  732.5 51.8 %copy-start.5 = (f32[9216]{0:T(1024)S(1)}, f32[9216]{0:T(1024)}, u32[]{:S(2)}) copy-start(f32[9216]{0:T(1024)} %get-tuple-element.43) | copy-start | bytes 110596
Sparse Core Ops, SparseCore 0:
  652.2 80.2 all-reduce.5
where the time goes:
time: 809 us; the launch traced here: 795 us
  waiting for transfers between devices  229 us (28%)
  other arithmetic  223 us (28%)
  local copies, waits for them, and re-layouts  200 us (25%)
  blocking collectives  84.7 us (10%)
  matrix products  28.6 us (4%)
  between operations  18.2 us (2%)
  starting transfers between devices  10.7 us (1%)
    all_to_all x1, waiting for transfers between devices, shards(): lax.all_to_all(outgoing.reshape(n_row * n_col, fields, width), ('row', 'c...  153 us
    scatter-add x2, other arithmetic, shards(): flat = jnp.zeros((cams * cams, 81), jnp.float32).at[where].add(product_rows)  135 us
    unnamed x2, waiting for transfers between devices  76.6 us
    reshape x6, local copies, waits for them, and re-layouts, shards(): flat.reshape(cams, cams, 9, 9).transpose(0, 2, 1, 3).reshape(tile, tile)  63.4 us
    psum x1, blocking collectives, shards(): rhs_col, diag_col = lax.psum((rhs_part, diag_part), 'row')  38.8 us
    psum x1, blocking collectives, shards(): summed = lax.psum(local, 'col')  32.8 us
    reshape x4, local copies, waits for them, and re-layouts, shards(): product_rows = product.transpose(0, 3, 1, 2).reshape(-1, 81)  25.6 us
    concatenate x1, other arithmetic, shards(): jnp.concatenate([own_slots[None, 0:45] * present[:, None, :], spread(rout...  23.9 us
  transfers between devices with their start and end apart: 2, of which 2 were waited for; matrix products, arithmetic and copies ran while one was open for 1% of the time, Pallas kernels for 0%

commit v1 on v0

v1 whole, which is shorter than its diff:
```python
import functools

import jax
import jax.numpy as jnp
from jax import lax
from jax.experimental import pallas as pl
from jax.experimental.pallas import tpu as pltpu
from jax.sharding import PartitionSpec as P

KOBS = 8
NCL = 16
CAP = 96
CAM = 64
TILE = 576
NROW = 8
NDEV = 128
PTS = 128
AXES = ("row", "col")
BF = jnp.bfloat16
F32 = jnp.float32
NT = (((1,), (1,)), ((), ()))
MIB = 1 << 20


def iota(shape, dim):
    return lax.broadcasted_iota(jnp.int32, shape, dim)


def whitened(jp, rs, damp):
    def inner(a, b):
        return jnp.sum(jp[0][a] * jp[0][b] + jp[1][a] * jp[1][b], axis=0, keepdims=True)

    laa = jnp.sqrt(inner(0, 0) + damp[0:1])
    lba = inner(1, 0) / laa
    lca = inner(2, 0) / laa
    lbb = jnp.sqrt(inner(1, 1) + damp[1:2] - lba * lba)
    lcb = (inner(2, 1) - lca * lba) / lbb
    lcc = jnp.sqrt(inner(2, 2) + damp[2:3] - lca * lca - lcb * lcb)

    def solve(a, b, c):
        x = a / laa
        y = (b - lba * x) / lbb
        return [x, y, (c - lca * x - lcb * y) / lcc]

    u = [solve(*jp[m]) for m in range(2)]
    grad = [
        jnp.sum(jp[0][a] * rs[0] + jp[1][a] * rs[1], axis=0, keepdims=True) for a in range(3)
    ]
    w = solve(*grad)
    q = [u[m][0] * w[0] + u[m][1] * w[1] + u[m][2] * w[2] - rs[m] for m in range(2)]
    return u, q


def load_point(jp_ref, rs_ref, damp_ref):
    jp = [[jp_ref[m * 3 + a] for a in range(3)] for m in range(2)]
    rs = [rs_ref[m] for m in range(2)]
    return whitened(jp, rs, damp_ref[...])


def pack_kernel(jc_ref, jp_ref, rs_ref, damp_ref, cl_ref, slot_ref, out_ref, fields, dense):
    u, _ = load_point(jp_ref, rs_ref, damp_ref)
    j0, j1 = jc_ref[0], jc_ref[9]
    top = jnp.maximum(jnp.abs(j0), jnp.abs(j1))
    some = top > 0.0
    safe = jnp.where(some, top, 1.0)
    x, y = j0 / safe, j1 / safe
    length = jnp.where(some, jnp.sqrt(x * x + y * y), 1.0)
    cs = jnp.where(some, x / length, 1.0)
    sn = jnp.where(some, y / length, 0.0)
    for i in range(9):
        a, b = jc_ref[i], jc_ref[9 + i]
        fields[i] = cs * a + sn * b
        if i:
            fields[8 + i] = cs * b - sn * a
    for a in range(3):
        fields[17 + a] = cs * u[0][a] + sn * u[1][a]
        fields[20 + a] = cs * u[1][a] - sn * u[0][a]
    fields[23] = slot_ref[...].astype(F32)
    named = []
    for e in range(2):
        ids = 2 * iota((NROW, PTS), 0) + e
        hits = [jnp.broadcast_to(cl_ref[k : k + 1, :], (NROW, PTS)) == ids for k in range(KOBS)]
        for f in range(24):
            value = jnp.full((NROW, PTS), -1.0 if f == 23 else 0.0, F32)
            for k in range(KOBS):
                row = jnp.broadcast_to(fields[f, k : k + 1, :], (NROW, PTS))
                value = jnp.where(hits[k], row, value)
            dense[f, e] = value
        named.append(dense[23, e] >= 0.0)
    present = jnp.concatenate([n.astype(F32) for n in named], axis=0).astype(BF)
    upto = (iota((PTS, PTS), 1) <= iota((PTS, PTS), 0)).astype(F32).astype(BF)
    counts = lax.dot_general(upto, present, NT, preferred_element_type=F32)
    lane = iota((NROW, PTS), 1)
    lane_f = iota((PTS, PTS), 1).astype(F32)
    ones = jnp.ones((NROW, PTS), BF)
    row_id = iota((NROW, PTS), 0)
    for c in range(NCL):
        ec, rc = c % 2, c // 2
        col = ec * NROW + rc
        before = (jnp.broadcast_to(counts[:, col : col + 1], (PTS, PTS)) <= lane_f).astype(F32)
        found = jnp.dot(ones, before.astype(BF), preferred_element_type=F32)
        valid = found < float(PTS)
        pick = jnp.minimum(found, float(PTS - 1)).astype(jnp.int32)

        def take(f, e):
            return jnp.take_along_axis(dense[f, e], pick, axis=1)

        side = [[take(f, e) for f in range(24)] for e in range(2)]
        mine = [jnp.broadcast_to(side[ec][f][rc : rc + 1, :], (NROW, PTS)) for f in range(24)]
        mid = []
        for e in range(2):
            on = jnp.where(2 * row_id + e == c, 1.0, 0.0)
            for m in range(2):
                for n in range(2):
                    v = sum(side[e][17 + 3 * m + a] * mine[17 + 3 * n + a] for a in range(3))
                    mid.append(on - v if m == n else -v)
        rows = []
        for part in (side[0], side[1], mine):
            rows += part[0:9] + part[9:16]
        extra = [side[0][16], side[1][16], mine[16], side[0][23], side[1][23]]
        extra.append(jnp.where(valid, mine[23], -1.0))
        zero = jnp.zeros((NROW, PTS), F32)
        extra += [zero, zero] + mid
        for v in range(3):
            for q in range(16):
                moved = extra[q] if q in (6, 7) else pltpu.roll(extra[q], 96 - 32 * v, 1)
                full = jnp.where(lane < CAP, rows[v * 16 + q], moved)
                out_ref[:, c, v * 16 + q, :] = full


def pack(jc, jp, rs, damp, cl, slot):
    return pl.pallas_call(
        pack_kernel,
        out_shape=jax.ShapeDtypeStruct((NROW, NCL, 48, PTS), F32),
        scratch_shapes=[
            pltpu.VMEM((24, KOBS, PTS), F32),
            pltpu.VMEM((24, 2, NROW, PTS), F32),
        ],
        compiler_params=pltpu.CompilerParams(vmem_limit_bytes=40 * MIB),
        cost_estimate=pl.CostEstimate(flops=10**7, bytes_accessed=4 * 10**6, transcendentals=0),
        name="pack",
    )(jc, jp, rs, damp, cl, slot)


SRC = 8
LANES = SRC * CAP
GROUP = 3


def spread_kernel(flag_ref, in_ref, damp_ref, out_ref, acc, rows_ref, prod, stage):
    step = pl.program_id(0)

    @pl.when(step == 0)
    def _():
        acc[...] = jnp.zeros_like(acc)

    for half in range(SRC // 4):
        pieces = []
        for s in range(4):
            block = in_ref[half * 4 + s]
            lane16 = iota((16, PTS), 1)
            rest = jnp.where(
                lane16 < 32,
                pltpu.roll(block[0:16], 32, 1),
                jnp.where(lane16 < 64, pltpu.roll(block[16:32], 64, 1), pltpu.roll(block[32:48], 96, 1)),
            )
            pieces.append(jnp.concatenate([block, rest], axis=0))
        lane = iota((64, PTS), 1)
        r1, r2, r3 = pltpu.roll(pieces[1], 96, 1), pltpu.roll(pieces[2], 64, 1), pltpu.roll(pieces[3], 32, 1)
        base = half * 384
        rows_ref[:, base : base + 128] = jnp.where(lane < 96, pieces[0], r1)
        rows_ref[:, base + 128 : base + 256] = jnp.where(lane < 64, r1, r2)
        rows_ref[:, base + 256 : base + 384] = jnp.where(lane < 32, r2, r3)

    def bcast(row, n):
        return jnp.broadcast_to(row, (n, LANES))

    first = iota((8, LANES), 0) == 0
    cam0 = rows_ref[32:40]
    cam1 = jnp.where(first, 0.0, rows_ref[40:48])
    slot_c = rows_ref[53:54].astype(jnp.int32)
    for e in range(2):
        a0 = rows_ref[16 * e : 16 * e + 8]
        a1 = jnp.where(first, 0.0, rows_ref[16 * e + 8 : 16 * e + 16])
        last0 = rows_ref[16 * e + 8 : 16 * e + 9]
        last1 = rows_ref[48 + e : 49 + e]
        t, t_last = [], []
        for m in range(2):
            m0 = rows_ref[56 + 4 * e + 2 * m : 57 + 4 * e + 2 * m]
            m1 = rows_ref[57 + 4 * e + 2 * m : 58 + 4 * e + 2 * m]
            t.append(bcast(m0, 8) * cam0 + bcast(m1, 8) * cam1)
            t_last.append(m0 * rows_ref[40:41] + m1 * rows_ref[50:51])

        def split(value):
            high = value.astype(BF).astype(F32)
            return high, value - high

        for j in range(9):
            t0 = t[0][j : j + 1] if j < 8 else t_last[0]
            t1 = t[1][j : j + 1] if j < 8 else t_last[1]
            high, low = split(a0 * bcast(t0, 8) + a1 * bcast(t1, 8))
            prod[0, j, 0:8] = high
            prod[1, j, 0:8] = low
            high, low = split(last0 * t0 + last1 * t1)
            prod[0, j, 8:9] = high
            prod[1, j, 8:9] = low

        slot_a = rows_ref[51 + e : 52 + e].astype(jnp.int32)
        both = jnp.minimum(slot_a, slot_c) >= 0
        code = jnp.where(both, (slot_a >> 4) * CAM + slot_c, -1)
        onehot = (bcast(code, 256) == iota((256, LANES), 0)).astype(F32).astype(BF)
        mask = (bcast(slot_a & 15, 16) == iota((16, LANES), 0)).astype(F32).astype(BF)
        for g in range(9 // GROUP):
            parts = []
            for h in range(2):
                for j in range(g * GROUP, (g + 1) * GROUP):
                    for i in range(9):
                        parts.append(bcast(prod[h, j, i : i + 1], 16).astype(BF) * mask)
            left = jnp.concatenate(parts, axis=0)
            got = lax.dot_general(left, onehot, NT, preferred_element_type=F32)
            n = GROUP * 144
            acc[e, g * n : (g + 1) * n, :] += got[:n] + got[n:]

    @pl.when(step == pl.num_programs(0) - 1)
    def _():
        source = iota((640, 640), 0)
        place = iota((640, 640), 1) == 9 * (source % CAM) + source // CAM
        place = (place & (source < TILE)).astype(F32).astype(BF)
        lane = iota((144, PTS), 1)
        for e in range(2):
            for u in range(4):
                base = (u // 2) * 128
                tiles = []
                for jj in range(5):
                    even = acc[e, 288 * jj : 288 * jj + 144, base : base + 128]
                    if u % 2:
                        even = pltpu.roll(even, 64, 1)
                    if jj < 4:
                        odd = acc[e, 288 * jj + 144 : 288 * jj + 288, base : base + 128]
                        if u % 2 == 0:
                            odd = pltpu.roll(odd, 64, 1)
                        even = jnp.where(lane < CAM, even, odd)
                    tiles.append(even)
                wide = jnp.concatenate(tiles, axis=1)
                high = wide.astype(BF)
                low = (wide - high.astype(F32)).astype(BF)
                got = jnp.dot(high, place, preferred_element_type=F32)
                got += jnp.dot(low, place, preferred_element_type=F32)
                for tile in range(5):
                    for i in range(9):
                        piece = got[16 * i : 16 * i + 16, 128 * tile : 128 * tile + 128]
                        stage[pl.ds(TILE * tile + 144 * u + i, 16, stride=9), :] = piece
            for tile in range(5):
                wide = min(128, TILE - 128 * tile)
                block = stage[TILE * tile : TILE * tile + TILE, 0:wide]
                out_ref[e, :, 128 * tile : 128 * tile + wide] = block

            @pl.when(flag_ref[e] == 1)
            def _():
                same = iota((TILE, TILE), 0) == iota((TILE, TILE), 1)
                out_ref[e] += jnp.where(same, jnp.broadcast_to(damp_ref[...], (TILE, TILE)), 0.0)


def spread(flags, incoming, damp):
    steps = NDEV // SRC
    return pl.pallas_call(
        spread_kernel,
        grid=(steps,),
        in_specs=[
            pl.BlockSpec(memory_space=pltpu.SMEM),
            pl.BlockSpec((SRC, 48, PTS), lambda s: (s, 0, 0)),
            pl.BlockSpec((1, TILE), lambda s: (0, 0)),
        ],
        out_specs=pl.BlockSpec((2, TILE, TILE), lambda s: (0, 0, 0)),
        out_shape=jax.ShapeDtypeStruct((2, TILE, TILE), F32),
        scratch_shapes=[
            pltpu.VMEM((2, 1296, 256), F32),
            pltpu.VMEM((64, LANES), F32),
            pltpu.VMEM((2, 9, 16, LANES), F32),
            pltpu.VMEM((5 * TILE, 128), F32),
        ],
        compiler_params=pltpu.CompilerParams(vmem_limit_bytes=48 * MIB),
        cost_estimate=pl.CostEstimate(flops=4 * 10**10, bytes_accessed=6 * 10**6, transcendentals=0),
        name="spread",
    )(flags, incoming, damp)


def three(value):
    a = value.astype(BF)
    rest = value - a.astype(F32)
    b = rest.astype(BF)
    c = (rest - b.astype(F32)).astype(BF)
    return jnp.concatenate([a, b, c], axis=0)


NCAM = NCL * CAM


def camera_hits(cl_ref, slot_ref, k):
    code = cl_ref[k : k + 1, :] * CAM + slot_ref[k : k + 1, :]
    hit = jnp.broadcast_to(code, (NCAM, PTS)) == iota((NCAM, PTS), 0)
    return hit.astype(F32).astype(BF)


def sums_kernel(jc_ref, jp_ref, rs_ref, damp_ref, cl_ref, slot_ref, out_ref):
    u, q = load_point(jp_ref, rs_ref, damp_ref)
    m00 = 1.0 - (u[0][0] * u[0][0] + u[0][1] * u[0][1] + u[0][2] * u[0][2])
    m11 = 1.0 - (u[1][0] * u[1][0] + u[1][1] * u[1][1] + u[1][2] * u[1][2])
    m01 = -2.0 * (u[0][0] * u[1][0] + u[0][1] * u[1][1] + u[0][2] * u[1][2])
    terms = []
    for i in range(9):
        a, b = jc_ref[i], jc_ref[9 + i]
        terms.append(a * q[0] + b * q[1])
    for i in range(9):
        a, b = jc_ref[i], jc_ref[9 + i]
        terms.append(a * a * m00 + a * b * m01 + b * b * m11)
    total = jnp.zeros((72, NCAM), F32)
    pad = jnp.zeros((6, PTS), F32)
    for k in range(KOBS):
        stacked = jnp.concatenate([v[k : k + 1] for v in terms] + [pad], axis=0)
        total += lax.dot_general(
            three(stacked), camera_hits(cl_ref, slot_ref, k), NT, preferred_element_type=F32
        )
    out_ref[...] = (total[0:24] + total[24:48] + total[48:72])[0:18]


def image_kernel(first_ref, jc_ref, jp_ref, rs_ref, damp_ref, cl_ref, slot_ref, out_ref):
    u, _ = load_point(jp_ref, rs_ref, damp_ref)
    pad = jnp.zeros((7, NCAM), F32)
    first = three(jnp.concatenate([first_ref[...], pad], axis=0))
    hits = [camera_hits(cl_ref, slot_ref, k) for k in range(KOBS)]
    seen = [[], []]
    for k in range(KOBS):
        got = jnp.dot(first, hits[k], preferred_element_type=F32)
        x = got[0:16] + got[16:32] + got[32:48]
        for m in range(2):
            row = sum(jc_ref[9 * m + i][k : k + 1] * x[i : i + 1] for i in range(9))
            seen[m].append(row)
    y = [jnp.concatenate(rows, axis=0) for rows in seen]
    z = [jnp.sum(u[0][a] * y[0] + u[1][a] * y[1], axis=0, keepdims=True) for a in range(3)]
    v = [y[m] - (u[m][0] * z[0] + u[m][1] * z[1] + u[m][2] * z[2]) for m in range(2)]
    terms = [jc_ref[i] * v[0] + jc_ref[9 + i] * v[1] for i in range(9)]
    total = jnp.zeros((48, NCAM), F32)
    pad = jnp.zeros((7, PTS), F32)
    for k in range(KOBS):
        stacked = jnp.concatenate([t[k : k + 1] for t in terms] + [pad], axis=0)
        total += lax.dot_general(three(stacked), hits[k], NT, preferred_element_type=F32)
    out_ref[...] = (total[0:16] + total[16:32] + total[32:48])[0:9]


def small_call(body, rows, name, *args):
    return pl.pallas_call(
        body,
        out_shape=jax.ShapeDtypeStruct((rows, NCAM), F32),
        compiler_params=pltpu.CompilerParams(vmem_limit_bytes=32 * MIB),
        cost_estimate=pl.CostEstimate(flops=3 * 10**8, bytes_accessed=10**6, transcendentals=0),
        name=name,
    )(*args)


def finish_kernel(rhs_ref, diag_ref, image_ref, step_ref, res_ref, dir_ref):
    rhs, diag, image = rhs_ref[...], diag_ref[...], image_ref[...]
    start = rhs / diag
    rz = jnp.sum(rhs * start)
    alpha = rz / jnp.sum(start * image)
    residual = rhs - alpha * image
    second = residual / diag
    beta = jnp.sum(residual * second) / rz
    step_ref[...] = alpha * start
    res_ref[...] = residual
    dir_ref[...] = second + beta * start


def total_sum(value):
    shape = value.shape
    flat = value.reshape(-1, 128)
    for bit in (16, 32, 64, 1, 2, 4, 8):
        pairs = [(d, d ^ bit) for d in range(NDEV)]
        flat = flat + lax.ppermute(flat, AXES, pairs)
    return flat.reshape(shape)


def shards(jac_cam, jac_pt, resid, point_damp, cam_damp, obs_cluster, obs_slot):
    my_row = lax.axis_index("row")
    my_col = lax.axis_index("col")
    jc = jac_cam.transpose(1, 0, 2)
    jp = jac_pt.transpose(1, 0, 2)
    rs = resid.transpose(1, 0, 2)
    cl = obs_cluster.T
    packed = pack(jc, jp, rs, point_damp, cl, obs_slot)
    incoming = lax.all_to_all(
        packed.reshape(NDEV, 48, PTS), AXES, split_axis=0, concat_axis=0, tiled=True
    )
    here = (jnp.arange(NCL) == my_col) & (my_row == 0)
    damp = cam_damp.reshape(CAM, 9).T
    damp = (damp[:, None, :] * here.astype(F32)[None, :, None]).reshape(9, NCAM)

    sums = small_call(sums_kernel, 18, "sums", jc, jp, rs, point_damp, cl, obs_slot)
    sums = total_sum(sums + jnp.concatenate([jnp.zeros_like(damp), damp], axis=0))
    rhs, diag = sums[0:9], sums[9:18]
    first = rhs / diag
    image = small_call(
        image_kernel, 9, "image", first, jc, jp, rs, point_damp, cl, obs_slot
    )
    image = total_sum(image + damp * first)
    step, residual, direction = pl.pallas_call(
        finish_kernel,
        out_shape=[jax.ShapeDtypeStruct((9, NCAM), F32)] * 3,
        name="finish",
    )(rhs, diag, image)
    flags = (2 * my_row + jnp.arange(2) == my_col).astype(jnp.int32)
    schur = spread(flags, incoming, cam_damp)

    def order(value):
        return value.T.reshape(-1)

    return (schur[:, None], order(step), order(residual), order(direction))


def solution(mesh):
    placed = (
        P(None, None, AXES),
        P(None, None, AXES),
        P(None, None, AXES),
        P(None, AXES),
        P("col", None),
        P(AXES, None),
        P(None, AXES),
    )
    return jax.shard_map(
        shards,
        mesh=mesh,
        in_specs=placed,
        out_specs=(P("row", "col", None, None), P(), P(), P()),
        check_vma=False,
    )
```

time: 809 us -> 184 us (0.23); the launches traced: 795 us -> 184 us
  other arithmetic: 223 us -> 0.22 us
  local copies, waits for them, and re-layouts: 200 us -> 17.1 us
  waiting for transfers between devices: 229 us -> 74.2 us
  blocking collectives: 84.7 us -> 0 us
  Pallas kernels: 0 us -> 62.1 us
  matrix products: 28.6 us -> 0 us
  starting transfers between devices: 10.7 us -> 29.2 us
  between operations: 18.2 us -> 0.86 us
    all_to_all x1, waiting for transfers between devices: 153 us -> 0.01 us  [shards(): lax.all_to_all(packed.reshape(NDEV, 48, PTS), AXES, split_axis=0, concat_...]
    scatter-add x2 -> x0, other arithmetic: 135 us -> none  [shards(): flat = jnp.zeros((cams * cams, 81), jnp.float32).at[where].add(product_rows)]
    reshape x16 -> x7, local copies, waits for them, and re-layouts: 111 us -> 6.82 us  [the longest x3 6.02 us: order(): return value.T.reshape(-1)]
    unnamed x2 -> x0, waiting for transfers between devices: 76.6 us -> none
    ppermute x0 -> x14, waiting for transfers between devices: none -> 74.2 us  [total_sum(): flat = flat + lax.ppermute(flat, AXES, pairs)]
    psum x2 -> x0, blocking collectives: 71.6 us -> none  [the longest x1 38.8 us: shards(): rhs_col, diag_col = lax.psum((rhs_part, diag_part), 'row')]
    pallas_call x0 -> x5, Pallas kernels: none -> 62.1 us  [the longest x1 50.2 us: spread(): pl.pallas_call(spread_kernel, grid=(steps,), in_specs=[pl.BlockSpec(memor...]
    dot_general x8 -> x0, matrix products: 28.6 us -> none  [the longest x1 15.8 us: spread(): jnp.einsum('csg,sfg->cfg', weights, values, precision=lax.Precision.HIGHEST)]
  transfers between devices with their start and end apart: 2 -> 15, of which waited for: 2 -> 14; matrix products, arithmetic and copies ran while one was open for 1% -> 7% of each run, Pallas kernels for 0% -> 2%
where the time goes in v1:
time: 184 us
  waiting for transfers between devices  74.2 us (40%)
  Pallas kernels  62.1 us (34%)
  starting transfers between devices  29.2 us (16%)
  local copies, waits for them, and re-layouts  17.1 us (9%)
    ppermute x14, waiting for transfers between devices, total_sum(): flat = flat + lax.ppermute(flat, AXES, pairs)  74.2 us
    pallas_call x1, Pallas kernels, spread(): pl.pallas_call(spread_kernel, grid=(steps,), in_specs=[pl.BlockSpec(memor...  50.2 us
    ppermute x14, starting transfers between devices, total_sum(): flat = flat + lax.ppermute(flat, AXES, pairs)  18.9 us
    all_to_all x1, starting transfers between devices, shards(): lax.all_to_all(packed.reshape(NDEV, 48, PTS), AXES, split_axis=0, concat_...  10.3 us
    pallas_call x1, Pallas kernels, pack(): pl.pallas_call(pack_kernel, out_shape=jax.ShapeDtypeStruct((NROW, NCL, 48...  7.58 us
    reshape x3, local copies, waits for them, and re-layouts, order(): return value.T.reshape(-1)  6.02 us
    transpose x3, local copies, waits for them, and re-layouts, order(): return value.T.reshape(-1)  5.56 us
    unnamed x27, local copies, waits for them, and re-layouts  4.41 us
  transfers between devices with their start and end apart: 15, of which 14 were waited for; matrix products, arithmetic and copies ran while one was open for 7% of the time, Pallas kernels for 2%

profile of v1, /device:TPU:24, one launch (start us, length us, event | category | flops | bytes accessed | tf_op | source)
XLA Modules:
  0.0 183.6 jit_solution(17703433649852594613)
XLA Ops:
  0.6 0.7 copy.21
  1.3 0.9 copy-done
  2.2 0.7 copy-done.2
  3.0 0.7 copy-done.4
  3.6 0.7 copy-done.6
  4.3 0.7 copy-done.9
  5.0 7.6 %pack.1 = f32[8,16,48,128]{3,2,1,0:T(8,128)} custom-call(f32[18,8,128]{2,1,0:T(8,128)S(1)} %bitcast.14, f32[6,8,128]{2,1,0:T(8,128)S(1)} %bitcast.20, f32[2,8,128]{2,1,0:T(8,128)S(1)} %bitcast.17, f32[3,128]{1,0:T(4,128)S(1)} %copy-done.9, s32[8,128]{1,0:T(8,128)S(1)} %bitcast.23, s32[8,128]{1,0:T(8,128)S(1)} %copy-done.6), custom_call_target="tpu_custom_call" | custom-call | flops 10000000 | bytes 4000000 | tf_op jit(solution)/shard_map/pack/pallas_call | solution.py:132
  12.6 0.0 copy-start.7
  12.6 0.0 copy-start.10
  12.6 10.3 %all-to-all-start = ((f32[128,48,128]{2,1,0:T(8,128)}), f32[128,48,128]{2,1,0:T(8,128)S(1)}, u32[]{:S(2)}, u32[]{:S(2)}) async-start(f32[128,48,128]{2,1,0:T(8,128)} %bitcast.4), calls=%async_computation | async-start | bytes 6291456 | tf_op jit(solution)/shard_map/all_to_all | solution.py:391
  22.9 0.0 copy-done.8
  22.9 0.1 reshape.46
  23.1 0.1 copy.15
  23.2 0.1 mul.24
  23.3 0.1 mul.25
  23.3 0.1 mul.26
  23.4 0.0 copy-done.1
  23.4 0.0 copy-done.3
  23.4 0.0 copy-done.5
  23.4 0.0 copy-done.7
  23.4 0.0 copy-done.10
  23.4 0.9 sums.1
  24.4 0.2 collective-permute-start
  24.6 1.1 collective-permute-done
  25.8 1.6 collective-permute-start.1
  27.3 32.7 %collective-permute-done.1 = f32[144,128]{1,0:T(8,128)S(1)} collective-permute-done((f32[144,128]{1,0:T(8,128)S(1)}, f32[144,128]{1,0:T(8,128)S(1)}, u32[]{:S(2)}, u32[]{:S(2)}) %collective-permute-start.1) | collective-permute-done | bytes 73760 | tf_op jit(solution)/shard_map/ppermute | solution.py:379
  60.0 2.8 %collective-permute-start.2 = (f32[144,128]{1,0:T(8,128)S(1)}, f32[144,128]{1,0:T(8,128)S(1)}, u32[]{:S(2)}, u32[]{:S(2)}) collective-permute-start(f32[144,128]{1,0:T(8,128)S(1)} %add.60), channel_id=1, source_target_pairs={{0,64},{1,65},{2,66},{3,67},{4,68},{5,69},{6,70},{7,71},{8,72},{9,... | collective-permute-start | bytes 221192 | tf_op jit(solution)/shard_map/ppermute | solution.py:379
  62.8 3.1 %collective-permute-done.2 = f32[144,128]{1,0:T(8,128)S(1)} collective-permute-done((f32[144,128]{1,0:T(8,128)S(1)}, f32[144,128]{1,0:T(8,128)S(1)}, u32[]{:S(2)}, u32[]{:S(2)}) %collective-permute-start.2) | collective-permute-done | bytes 73760 | tf_op jit(solution)/shard_map/ppermute | solution.py:379
  66.0 0.9 collective-permute-start.3
  66.8 4.2 %collective-permute-done.3 = f32[144,128]{1,0:T(8,128)S(1)} collective-permute-done((f32[144,128]{1,0:T(8,128)S(1)}, f32[144,128]{1,0:T(8,128)S(1)}, u32[]{:S(2)}, u32[]{:S(2)}) %collective-permute-start.3) | collective-permute-done | bytes 73760 | tf_op jit(solution)/shard_map/ppermute | solution.py:379
  71.1 0.8 collective-permute-start.4
  71.9 5.1 %collective-permute-done.4 = f32[144,128]{1,0:T(8,128)S(1)} collective-permute-done((f32[144,128]{1,0:T(8,128)S(1)}, f32[144,128]{1,0:T(8,128)S(1)}, u32[]{:S(2)}, u32[]{:S(2)}) %collective-permute-start.4) | collective-permute-done | bytes 73760 | tf_op jit(solution)/shard_map/ppermute | solution.py:379
  77.0 1.9 %collective-permute-start.5 = (f32[144,128]{1,0:T(8,128)S(1)}, f32[144,128]{1,0:T(8,128)S(1)}, u32[]{:S(2)}, u32[]{:S(2)}) collective-permute-start(f32[144,128]{1,0:T(8,128)S(1)} %add.63), channel_id=1, source_target_pairs={{0,4},{1,5},{2,6},{3,7},{4,0},{5,1},{6,2},{7,3},{8,12},{9,13},{10,... | collective-permute-start | bytes 221192 | tf_op jit(solution)/shard_map/ppermute | solution.py:379
  79.0 3.1 %collective-permute-done.5 = f32[144,128]{1,0:T(8,128)S(1)} collective-permute-done((f32[144,128]{1,0:T(8,128)S(1)}, f32[144,128]{1,0:T(8,128)S(1)}, u32[]{:S(2)}, u32[]{:S(2)}) %collective-permute-start.5) | collective-permute-done | bytes 73760 | tf_op jit(solution)/shard_map/ppermute | solution.py:379
  82.1 2.6 %collective-permute-start.6 = (f32[144,128]{1,0:T(8,128)S(1)}, f32[144,128]{1,0:T(8,128)S(1)}, u32[]{:S(2)}, u32[]{:S(2)}) collective-permute-start(f32[144,128]{1,0:T(8,128)S(1)} %add.64), channel_id=1, source_target_pairs={{0,8},{1,9},{2,10},{3,11},{4,12},{5,13},{6,14},{7,15},{8,0},{9,1},... | collective-permute-start | bytes 221192 | tf_op jit(solution)/shard_map/ppermute | solution.py:379
  84.7 3.3 %collective-permute-done.6 = f32[144,128]{1,0:T(8,128)S(1)} collective-permute-done((f32[144,128]{1,0:T(8,128)S(1)}, f32[144,128]{1,0:T(8,128)S(1)}, u32[]{:S(2)}, u32[]{:S(2)}) %collective-permute-start.6) | collective-permute-done | bytes 73760 | tf_op jit(solution)/shard_map/ppermute | solution.py:379
  88.0 0.0 copy-start.11
  88.1 0.0 copy-start.12
  88.1 1.6 image.1
  89.8 0.1 collective-permute-start.7
  89.9 1.2 collective-permute-done.7
  91.1 0.6 collective-permute-start.8
  91.7 3.4 %collective-permute-done.8 = f32[72,128]{1,0:T(8,128)S(1)} collective-permute-done((f32[72,128]{1,0:T(8,128)S(1)}, f32[72,128]{1,0:T(8,128)S(1)}, u32[]{:S(2)}, u32[]{:S(2)}) %collective-permute-start.8) | collective-permute-done | bytes 36896 | tf_op jit(solution)/shard_map/ppermute | solution.py:379
  95.1 2.8 %collective-permute-start.9 = (f32[72,128]{1,0:T(8,128)S(1)}, f32[72,128]{1,0:T(8,128)S(1)}, u32[]{:S(2)}, u32[]{:S(2)}) collective-permute-start(f32[72,128]{1,0:T(8,128)S(1)} %add.68), channel_id=1, source_target_pairs={{0,64},{1,65},{2,66},{3,67},{4,68},{5,69},{6,70},{7,71},{8,72},{9,... | collective-permute-start | bytes 110600 | tf_op jit(solution)/shard_map/ppermute | solution.py:379
  97.8 2.7 %collective-permute-done.9 = f32[72,128]{1,0:T(8,128)S(1)} collective-permute-done((f32[72,128]{1,0:T(8,128)S(1)}, f32[72,128]{1,0:T(8,128)S(1)}, u32[]{:S(2)}, u32[]{:S(2)}) %collective-permute-start.9) | collective-permute-done | bytes 36896 | tf_op jit(solution)/shard_map/ppermute | solution.py:379
  100.5 0.0 collective-permute-start.10
  100.5 3.9 %collective-permute-done.10 = f32[72,128]{1,0:T(8,128)S(1)} collective-permute-done((f32[72,128]{1,0:T(8,128)S(1)}, f32[72,128]{1,0:T(8,128)S(1)}, u32[]{:S(2)}, u32[]{:S(2)}) %collective-permute-start.10) | collective-permute-done | bytes 36896 | tf_op jit(solution)/shard_map/ppermute | solution.py:379
  104.5 0.1 collective-permute-start.11
  104.6 5.3 %collective-permute-done.11 = f32[72,128]{1,0:T(8,128)S(1)} collective-permute-done((f32[72,128]{1,0:T(8,128)S(1)}, f32[72,128]{1,0:T(8,128)S(1)}, u32[]{:S(2)}, u32[]{:S(2)}) %collective-permute-start.11) | collective-permute-done | bytes 36896 | tf_op jit(solution)/shard_map/ppermute | solution.py:379
  110.0 1.9 %collective-permute-start.12 = (f32[72,128]{1,0:T(8,128)S(1)}, f32[72,128]{1,0:T(8,128)S(1)}, u32[]{:S(2)}, u32[]{:S(2)}) collective-permute-start(f32[72,128]{1,0:T(8,128)S(1)} %add.71), channel_id=1, source_target_pairs={{0,4},{1,5},{2,6},{3,7},{4,0},{5,1},{6,2},{7,3},{8,12},{9,13},{10,... | collective-permute-start | bytes 110600 | tf_op jit(solution)/shard_map/ppermute | solution.py:379
  111.8 2.1 %collective-permute-done.12 = f32[72,128]{1,0:T(8,128)S(1)} collective-permute-done((f32[72,128]{1,0:T(8,128)S(1)}, f32[72,128]{1,0:T(8,128)S(1)}, u32[]{:S(2)}, u32[]{:S(2)}) %collective-permute-start.12) | collective-permute-done | bytes 36896 | tf_op jit(solution)/shard_map/ppermute | solution.py:379
  113.9 2.6 %collective-permute-start.13 = (f32[72,128]{1,0:T(8,128)S(1)}, f32[72,128]{1,0:T(8,128)S(1)}, u32[]{:S(2)}, u32[]{:S(2)}) collective-permute-start(f32[72,128]{1,0:T(8,128)S(1)} %add.72), channel_id=1, source_target_pairs={{0,8},{1,9},{2,10},{3,11},{4,12},{5,13},{6,14},{7,15},{8,0},{9,1},... | collective-permute-start | bytes 110600 | tf_op jit(solution)/shard_map/ppermute | solution.py:379
  116.5 2.9 %collective-permute-done.13 = f32[72,128]{1,0:T(8,128)S(1)} collective-permute-done((f32[72,128]{1,0:T(8,128)S(1)}, f32[72,128]{1,0:T(8,128)S(1)}, u32[]{:S(2)}, u32[]{:S(2)}) %collective-permute-start.13) | collective-permute-done | bytes 36896 | tf_op jit(solution)/shard_map/ppermute | solution.py:379
  119.4 0.6 reshape.49.image_ref
  120.0 0.0 copy-done.11
  120.1 1.8 %finish.1 = (f32[9,1024]{1,0:T(8,128)}, f32[9,1024]{1,0:T(8,128)}, f32[9,1024]{1,0:T(8,128)}) custom-call(f32[9,1024]{1,0:T(8,128)} %copy-done.11, f32[9,1024]{1,0:T(8,128)} %copy-done.12, f32[9,1024]{1,0:T(8,128)} %reshape.49.image_ref), custom_call_target="tpu_custom_call" | custom-call | tf_op jit(solution)/shard_map/finish/pallas_call | solution.py:406
  121.9 1.9 %copy.16 = f32[1024,9]{1,0:T(8,128)} copy(f32[1024,9]{0,1:T(8,128)} %bitcast.29) | data formatting | bytes 73728 | tf_op jit(solution)/shard_map/transpose | solution.py:415
  123.8 2.0 %reshape.50 = f32[9216]{0:T(1024)} reshape(f32[1024,9]{1,0:T(8,128)} %copy.16) | data formatting | bytes 73728 | tf_op jit(solution)/shard_map/reshape | solution.py:415
  125.8 1.9 %copy.17 = f32[1024,9]{1,0:T(8,128)} copy(f32[1024,9]{0,1:T(8,128)} %bitcast.28) | data formatting | bytes 73728 | tf_op jit(solution)/shard_map/transpose | solution.py:415
  127.6 2.0 %reshape.51 = f32[9216]{0:T(1024)} reshape(f32[1024,9]{1,0:T(8,128)} %copy.17) | data formatting | bytes 73728 | tf_op jit(solution)/shard_map/reshape | solution.py:415
  129.6 1.9 %copy.18 = f32[1024,9]{1,0:T(8,128)} copy(f32[1024,9]{0,1:T(8,128)} %bitcast.27) | data formatting | bytes 73728 | tf_op jit(solution)/shard_map/transpose | solution.py:415
  131.5 2.0 %reshape.52 = f32[9216]{0:T(1024)} reshape(f32[1024,9]{1,0:T(8,128)} %copy.18) | data formatting | bytes 73728 | tf_op jit(solution)/shard_map/reshape | solution.py:415
  133.5 0.0 all-to-all-done.in_ref
  133.5 50.2 %spread.1 = f32[2,576,576]{2,1,0:T(8,128)} custom-call(s32[2]{0:T(128)S(1)} %compare_convert_fusion.flag_ref, f32[128,48,128]{2,1,0:T(8,128)S(1)} %all-to-all-done.in_ref, f32[1,576]{1,0:T(1,128)S(1)} %copy-done.8), custom_call_target="tpu_custom_call" | custom-call | flops 40000000000 | bytes 6000000 | tf_op jit(solution)/shard_map/spread/pallas_call | solution.py:266
  (37 shorter events, 0.3 us)
Async XLA Ops:
  1.3 0.9 copy-start
  2.2 0.7 copy-start.2
  3.0 0.7 copy-start.4
  3.6 0.7 copy-start.6
  4.3 0.7 copy-start.9
  12.6 10.3 %copy-start.8 = (f32[1,576]{1,0:T(1,128)S(1)}, f32[1,576]{1,0:T(1,128)}, u32[]{:S(2)}) copy-start(f32[1,576]{1,0:T(1,128)} %damp_ref.5) | copy-start | bytes 6916
  12.6 10.8 %copy-start.1 = (f32[8,18,128]{2,0,1:T(8,128)S(1)}, f32[8,18,128]{2,0,1:T(8,128)}, u32[]{:S(2)}) copy-start(f32[8,18,128]{2,0,1:T(8,128)} %param.7) | copy-start | bytes 221188
  12.6 10.8 %copy-start.3 = (f32[8,6,128]{2,0,1:T(8,128)S(1)}, f32[8,6,128]{2,0,1:T(8,128)}, u32[]{:S(2)}) copy-start(f32[8,6,128]{2,0,1:T(8,128)} %param.8) | copy-start | bytes 73732
  12.6 10.8 %copy-start.5 = (s32[128,8]{0,1:T(8,128)S(1)}, s32[128,8]{0,1:T(8,128)}, u32[]{:S(2)}) copy-start(s32[128,8]{0,1:T(8,128)} %param.12) | copy-start | bytes 12292
  12.6 10.8 %copy-start.7 = (s32[8,128]{1,0:T(8,128)S(1)}, s32[8,128]{1,0:T(8,128)}, u32[]{:S(2)}) copy-start(s32[8,128]{1,0:T(8,128)} %slot_ref.5) | copy-start | bytes 12292
  12.6 10.8 %copy-start.10 = (f32[3,128]{1,0:T(4,128)S(1)}, f32[3,128]{1,0:T(4,128)}, u32[]{:S(2)}) copy-start(f32[3,128]{1,0:T(4,128)} %damp_ref.7) | copy-start | bytes 4612
  12.6 120.9 %all-to-all-start = ((f32[128,48,128]{2,1,0:T(8,128)}), f32[128,48,128]{2,1,0:T(8,128)S(1)}, u32[]{:S(2)}, u32[]{:S(2)}) async-start(f32[128,48,128]{2,1,0:T(8,128)} %bitcast.4), calls=%async_computation | async-start | bytes 6291456 | tf_op jit(solution)/shard_map/all_to_all | solution.py:391
  24.4 1.3 collective-permute-start
  25.8 34.2 %collective-permute-start.1 = (f32[144,128]{1,0:T(8,128)S(1)}, f32[144,128]{1,0:T(8,128)S(1)}, u32[]{:S(2)}, u32[]{:S(2)}) collective-permute-start(f32[144,128]{1,0:T(8,128)S(1)} %add.59), channel_id=1, source_target_pairs={{0,32},{1,33},{2,34},{3,35},{4,36},{5,37},{6,38},{7,39},{8,40},{9,... | collective-permute-start | bytes 221192 | tf_op jit(solution)/shard_map/ppermute | solution.py:379
  60.0 5.9 %collective-permute-start.2 = (f32[144,128]{1,0:T(8,128)S(1)}, f32[144,128]{1,0:T(8,128)S(1)}, u32[]{:S(2)}, u32[]{:S(2)}) collective-permute-start(f32[144,128]{1,0:T(8,128)S(1)} %add.60), channel_id=1, source_target_pairs={{0,64},{1,65},{2,66},{3,67},{4,68},{5,69},{6,70},{7,71},{8,72},{9,... | collective-permute-start | bytes 221192 | tf_op jit(solution)/shard_map/ppermute | solution.py:379
  66.0 5.1 %collective-permute-start.3 = (f32[144,128]{1,0:T(8,128)S(1)}, f32[144,128]{1,0:T(8,128)S(1)}, u32[]{:S(2)}, u32[]{:S(2)}) collective-permute-start(f32[144,128]{1,0:T(8,128)S(1)} %add.61), channel_id=1, source_target_pairs={{0,1},{1,0},{2,3},{3,2},{4,5},{5,4},{6,7},{7,6},{8,9},{9,8},{10,11... | collective-permute-start | bytes 221192 | tf_op jit(solution)/shard_map/ppermute | solution.py:379
  71.1 5.9 %collective-permute-start.4 = (f32[144,128]{1,0:T(8,128)S(1)}, f32[144,128]{1,0:T(8,128)S(1)}, u32[]{:S(2)}, u32[]{:S(2)}) collective-permute-start(f32[144,128]{1,0:T(8,128)S(1)} %add.62), channel_id=1, source_target_pairs={{0,2},{1,3},{2,0},{3,1},{4,6},{5,7},{6,4},{7,5},{8,10},{9,11},{10,... | collective-permute-start | bytes 221192 | tf_op jit(solution)/shard_map/ppermute | solution.py:379
  77.0 5.0 %collective-permute-start.5 = (f32[144,128]{1,0:T(8,128)S(1)}, f32[144,128]{1,0:T(8,128)S(1)}, u32[]{:S(2)}, u32[]{:S(2)}) collective-permute-start(f32[144,128]{1,0:T(8,128)S(1)} %add.63), channel_id=1, source_target_pairs={{0,4},{1,5},{2,6},{3,7},{4,0},{5,1},{6,2},{7,3},{8,12},{9,13},{10,... | collective-permute-start | bytes 221192 | tf_op jit(solution)/shard_map/ppermute | solution.py:379
  82.1 5.9 %collective-permute-start.6 = (f32[144,128]{1,0:T(8,128)S(1)}, f32[144,128]{1,0:T(8,128)S(1)}, u32[]{:S(2)}, u32[]{:S(2)}) collective-permute-start(f32[144,128]{1,0:T(8,128)S(1)} %add.64), channel_id=1, source_target_pairs={{0,8},{1,9},{2,10},{3,11},{4,12},{5,13},{6,14},{7,15},{8,0},{9,1},... | collective-permute-start | bytes 221192 | tf_op jit(solution)/shard_map/ppermute | solution.py:379
  88.0 32.0 %copy-start.11 = (f32[9,1024]{1,0:T(8,128)}, f32[9,1024]{1,0:T(8,128)S(1)}, u32[]{:S(2)}) copy-start(f32[9,1024]{1,0:T(8,128)S(1)} %slice.13.rhs_ref) | copy-start | bytes 110596
  88.1 32.0 %copy-start.12 = (f32[9,1024]{1,0:T(8,128)}, f32[9,1024]{1,0:T(8,128)S(1)}, u32[]{:S(2)}) copy-start(f32[9,1024]{1,0:T(8,128)S(1)} %slice.15.diag_ref) | copy-start | bytes 110596
  89.8 1.3 collective-permute-start.7
  91.1 4.0 %collective-permute-start.8 = (f32[72,128]{1,0:T(8,128)S(1)}, f32[72,128]{1,0:T(8,128)S(1)}, u32[]{:S(2)}, u32[]{:S(2)}) collective-permute-start(f32[72,128]{1,0:T(8,128)S(1)} %add.67), channel_id=1, source_target_pairs={{0,32},{1,33},{2,34},{3,35},{4,36},{5,37},{6,38},{7,39},{8,40},{9,... | collective-permute-start | bytes 110600 | tf_op jit(solution)/shard_map/ppermute | solution.py:379
  95.1 5.5 %collective-permute-start.9 = (f32[72,128]{1,0:T(8,128)S(1)}, f32[72,128]{1,0:T(8,128)S(1)}, u32[]{:S(2)}, u32[]{:S(2)}) collective-permute-start(f32[72,128]{1,0:T(8,128)S(1)} %add.68), channel_id=1, source_target_pairs={{0,64},{1,65},{2,66},{3,67},{4,68},{5,69},{6,70},{7,71},{8,72},{9,... | collective-permute-start | bytes 110600 | tf_op jit(solution)/shard_map/ppermute | solution.py:379
  100.5 4.0 %collective-permute-start.10 = (f32[72,128]{1,0:T(8,128)S(1)}, f32[72,128]{1,0:T(8,128)S(1)}, u32[]{:S(2)}, u32[]{:S(2)}) collective-permute-start(f32[72,128]{1,0:T(8,128)S(1)} %add.69), channel_id=1, source_target_pairs={{0,1},{1,0},{2,3},{3,2},{4,5},{5,4},{6,7},{7,6},{8,9},{9,8},{10,11... | collective-permute-start | bytes 110600 | tf_op jit(solution)/shard_map/ppermute | solution.py:379
  104.5 5.5 %collective-permute-start.11 = (f32[72,128]{1,0:T(8,128)S(1)}, f32[72,128]{1,0:T(8,128)S(1)}, u32[]{:S(2)}, u32[]{:S(2)}) collective-permute-start(f32[72,128]{1,0:T(8,128)S(1)} %add.70), channel_id=1, source_target_pairs={{0,2},{1,3},{2,0},{3,1},{4,6},{5,7},{6,4},{7,5},{8,10},{9,11},{10,... | collective-permute-start | bytes 110600 | tf_op jit(solution)/shard_map/ppermute | solution.py:379
  110.0 4.0 %collective-permute-start.12 = (f32[72,128]{1,0:T(8,128)S(1)}, f32[72,128]{1,0:T(8,128)S(1)}, u32[]{:S(2)}, u32[]{:S(2)}) collective-permute-start(f32[72,128]{1,0:T(8,128)S(1)} %add.71), channel_id=1, source_target_pairs={{0,4},{1,5},{2,6},{3,7},{4,0},{5,1},{6,2},{7,3},{8,12},{9,13},{10,... | collective-permute-start | bytes 110600 | tf_op jit(solution)/shard_map/ppermute | solution.py:379
  113.9 5.5 %collective-permute-start.13 = (f32[72,128]{1,0:T(8,128)S(1)}, f32[72,128]{1,0:T(8,128)S(1)}, u32[]{:S(2)}, u32[]{:S(2)}) collective-permute-start(f32[72,128]{1,0:T(8,128)S(1)} %add.72), channel_id=1, source_target_pairs={{0,8},{1,9},{2,10},{3,11},{4,12},{5,13},{6,14},{7,15},{8,0},{9,1},... | collective-permute-start | bytes 110600 | tf_op jit(solution)/shard_map/ppermute | solution.py:379

commit v2 on v0

v2 whole, which is shorter than its diff:
```python
import functools

import jax
import jax.numpy as jnp
from jax import lax
from jax.experimental import pallas as pl
from jax.experimental.pallas import tpu as pltpu
from jax.sharding import PartitionSpec as P

KOBS = 8
NCL = 16
CAP = 96
CAM = 64
TILE = 576
NROW = 8
NDEV = 128
PTS = 128
AXES = ("row", "col")
BF = jnp.bfloat16
F32 = jnp.float32
NT = (((1,), (1,)), ((), ()))
MIB = 1 << 20
SRC = 16
LANES = SRC * CAP
GROUP = 3
ANY = pl.BlockSpec(memory_space=pl.ANY)


def iota(shape, dim):
    return lax.broadcasted_iota(jnp.int32, shape, dim)


def whole(*shape):
    return pl.BlockSpec(shape, lambda *_: (0,) * len(shape))


def settings(micros, mib):
    return dict(
        compiler_params=pltpu.CompilerParams(vmem_limit_bytes=mib * MIB),
        cost_estimate=pl.CostEstimate(
            flops=micros * 10**9, bytes_accessed=10**6, transcendentals=0
        ),
    )


def lanes_of(row, n):
    return jnp.broadcast_to(row, (n, row.shape[1]))


def whitened(jp, rs, damp):
    def inner(a, b):
        return jnp.sum(jp[0][a] * jp[0][b] + jp[1][a] * jp[1][b], axis=0, keepdims=True)

    laa = jnp.sqrt(inner(0, 0) + damp[0:1])
    lba = inner(1, 0) / laa
    lca = inner(2, 0) / laa
    lbb = jnp.sqrt(inner(1, 1) + damp[1:2] - lba * lba)
    lcb = (inner(2, 1) - lca * lba) / lbb
    lcc = jnp.sqrt(inner(2, 2) + damp[2:3] - lca * lca - lcb * lcb)

    def solve(a, b, c):
        x = a / laa
        y = (b - lba * x) / lbb
        return [x, y, (c - lca * x - lcb * y) / lcc]

    u = [solve(*jp[m]) for m in range(2)]
    grad = [
        jnp.sum(jp[0][a] * rs[0] + jp[1][a] * rs[1], axis=0, keepdims=True) for a in range(3)
    ]
    w = solve(*grad)
    q = [u[m][0] * w[0] + u[m][1] * w[1] + u[m][2] * w[2] - rs[m] for m in range(2)]
    return u, q


def three(value):
    a = value.astype(BF)
    rest = value - a.astype(F32)
    b = rest.astype(BF)
    return jnp.concatenate([a, b, (rest - b.astype(F32)).astype(BF)], axis=0)


def chosen(dense, pair, ec):
    upto = (iota((PTS, PTS), 1) <= iota((PTS, PTS), 0)).astype(F32).astype(BF)
    lane = iota((PTS, PTS), 1).astype(F32)
    present = (dense[23, ec, pl.ds(pair, 1), :] >= 0.0).astype(F32)
    present = lanes_of(present, PTS).astype(BF)
    counts = lax.dot_general(upto, present, NT, preferred_element_type=F32)
    before = (counts <= lane).astype(F32).astype(BF)
    return jnp.dot(jnp.ones((NROW, PTS), BF), before, preferred_element_type=F32)


def points_kernel(jc, jp, rs, damp, cl_ref, slot_ref, dense, found_ref, fields):
    cl, slot = cl_ref[...], slot_ref[...]
    u, q = whitened(
        [[jp[m * 3 + a] for a in range(3)] for m in range(2)],
        [rs[:, m, :] for m in range(2)],
        damp[...],
    )
    j0, j1 = jc[0], jc[9]
    top = jnp.maximum(jnp.abs(j0), jnp.abs(j1))
    some = top > 0.0
    safe = jnp.where(some, top, 1.0)
    x, y = j0 / safe, j1 / safe
    length = jnp.where(some, jnp.sqrt(x * x + y * y), 1.0)
    cs = jnp.where(some, x / length, 1.0)
    sn = jnp.where(some, y / length, 0.0)
    for i in range(9):
        a, b = jc[i], jc[9 + i]
        fields[i] = cs * a + sn * b
        if i:
            fields[8 + i] = cs * b - sn * a
    turned = [[], []]
    for a in range(3):
        turned[0].append(cs * u[0][a] + sn * u[1][a])
        turned[1].append(cs * u[1][a] - sn * u[0][a])
        fields[17 + a] = turned[0][a]
        fields[20 + a] = turned[1][a]
    fields[23] = slot.astype(F32)
    fields[24] = cs * q[0] + sn * q[1]
    fields[25] = cs * q[1] - sn * q[0]
    fields[26] = 1.0 - sum(v * v for v in turned[0])
    fields[27] = -2.0 * sum(v * w for v, w in zip(*turned))
    fields[28] = 1.0 - sum(v * v for v in turned[1])
    for e in range(2):
        ids = 2 * iota((NROW, PTS), 0) + e
        hits = [lanes_of(cl[k : k + 1], NROW) == ids for k in range(KOBS)]
        for f in range(29):
            value = jnp.full((NROW, PTS), -1.0 if f == 23 else 0.0, F32)
            for k in range(KOBS):
                value = jnp.where(hits[k], lanes_of(fields[f, k : k + 1, :], NROW), value)
            dense[f, e] = value
    for r in range(NROW):
        for e in range(2):
            found_ref[2 * r + e] = chosen(dense, r, e)


def points(*args):
    shapes = [(29, 2, NROW, PTS), (NCL, NROW, PTS)]
    return pl.pallas_call(
        points_kernel,
        grid=(1,),
        in_specs=[whole(*a.shape) for a in args],
        out_specs=[whole(*shape) for shape in shapes],
        out_shape=[jax.ShapeDtypeStruct(shape, F32) for shape in shapes],
        scratch_shapes=[pltpu.VMEM((29, KOBS, PTS), F32)],
        name="points",
        **settings(4, 60),
    )(*args)


def mixed(side, mine, on):
    out = []
    for m in range(2):
        for n in range(2):
            v = sum(side[17 + 3 * m + a] * mine[17 + 3 * n + a] for a in range(3))
            out.append(on - v if m == n else -v)
    return out


def pack_kernel(dense, found_ref, out_ref, kept):
    pair = pl.program_id(0)
    lane = iota((NROW, PTS), 1)
    zero = jnp.zeros((NROW, PTS), F32)
    for ec in range(2):
        found = found_ref[2 * pair + ec]
        pick = jnp.minimum(found, float(PTS - 1)).astype(jnp.int32)
        side = [
            [jnp.take_along_axis(dense[f, e], pick, axis=1) for f in range(24)] for e in range(2)
        ]
        for f in range(29):
            if f < 24:
                kept[f] = side[ec][f]
            else:
                kept[f] = jnp.take_along_axis(dense[f, ec], pick, axis=1)
        mine = [lanes_of(kept[f, pl.ds(pair, 1), :], NROW) for f in range(29)]
        rows = side[0][0:16] + side[1][0:16] + mine[0:16]
        rows += [side[0][16], side[1][16], mine[16], side[0][23], side[1][23]]
        rows.append(jnp.where(found < float(PTS), mine[23], -1.0))
        rows += mine[24:26]
        extra = []
        for e in range(2):
            same = jnp.where(iota((NROW, PTS), 0) == pair, float(e == ec), 0.0)
            extra += mixed(side[e], mine, same)
        extra += mine[26:29]
        for at, row in enumerate(rows):
            v, x = at // 16, at % 16
            rest = pltpu.roll(extra[x], 96 - 32 * v, 1) if v < 3 and x < 11 else zero
            out_ref[:, ec, at, :] = jnp.where(lane < CAP, row, rest)


def pack(dense, found):
    return pl.pallas_call(
        pack_kernel,
        grid=(NROW,),
        in_specs=[whole(29, 2, NROW, PTS), whole(NCL, NROW, PTS)],
        out_specs=pl.BlockSpec((NROW, 2, SENT, PTS), lambda g: (0, g, 0, 0)),
        out_shape=jax.ShapeDtypeStruct((NROW, NCL, SENT, PTS), F32),
        scratch_shapes=[pltpu.VMEM((29, NROW, PTS), F32)],
        name="pack",
        **settings(8, 60),
    )(dense, found)


def exchange(value):
    return lax.all_to_all(value, AXES, split_axis=0, concat_axis=0, tiled=True)


ROWS = 72
SENT = 56


def lay(in_ref, rows_ref):
    lane = iota((16, PTS), 1)
    full = iota((ROWS, PTS), 1)
    for quarter in range(SRC // 4):
        pieces = []
        for s in range(4):
            block = in_ref[quarter * 4 + s]
            part = [pltpu.roll(block[16 * v : 16 * v + 16], 32 + 32 * v, 1) for v in range(3)]
            rest = jnp.where(lane < 32, part[0], jnp.where(lane < 64, part[1], part[2]))
            pieces.append(jnp.concatenate([block, rest], axis=0))
        r1, r2 = pltpu.roll(pieces[1], 96, 1), pltpu.roll(pieces[2], 64, 1)
        r3 = pltpu.roll(pieces[3], 32, 1)
        base = quarter * 384
        rows_ref[:, base : base + 128] = jnp.where(full < 96, pieces[0], r1)
        rows_ref[:, base + 128 : base + 256] = jnp.where(full < 64, r1, r2)
        rows_ref[:, base + 256 : base + 384] = jnp.where(full < 32, r2, r3)


def jacobian(rows_ref, which):
    at = 16 * which
    first = iota((8, LANES), 0) == 0
    a1 = jnp.where(first, 0.0, rows_ref[at + 8 : at + 16])
    return rows_ref[at : at + 8], a1, rows_ref[at + 8 : at + 9], rows_ref[48 + which : 49 + which]


def cg_kernel(flag_ref, in_ref, damp_ref, rows_ref, out_ref, keep, hits, sums, image):
    step = pl.program_id(0)
    steps = pl.num_programs(0)

    @pl.when(step == 0)
    def _():
        sums[...] = jnp.zeros_like(sums)

    lay(in_ref, rows_ref)
    a0, a1, l0, l1 = jacobian(rows_ref, 2)
    q0, q1 = rows_ref[54:55], rows_ref[55:56]
    m0, m1, m2 = rows_ref[64:65], rows_ref[65:66], rows_ref[66:67]
    terms = [
        a0 * lanes_of(q0, 8) + a1 * lanes_of(q1, 8),
        a0 * a0 * lanes_of(m0, 8) + a0 * a1 * lanes_of(m1, 8) + a1 * a1 * lanes_of(m2, 8),
        l0 * q0 + l1 * q1,
        l0 * l0 * m0 + l0 * l1 * m1 + l1 * l1 * m2,
        jnp.zeros((6, LANES), F32),
    ]
    slot = rows_ref[53:54].astype(jnp.int32)
    hit = (lanes_of(slot, 128) == iota((128, LANES), 0)).astype(F32).astype(BF)
    hits[step] = hit
    keep[step] = rows_ref[...]
    sums[...] += lax.dot_general(
        three(jnp.concatenate(terms, axis=0)), hit, NT, preferred_element_type=F32
    )

    @pl.when(step == steps - 1)
    def _():
        damp = damp_ref[...]
        total = sums[0:24] + sums[24:48] + sums[48:72] + damp
        sums[0:24] = total
        x8, x9 = total[0:8] / total[8:16], total[16:17] / total[17:18]
        x = three(jnp.concatenate([x8, x9, jnp.zeros((7, 128), F32)], axis=0))
        image[...] = jnp.zeros_like(image)

        @pl.loop(0, steps)
        def _(at):
            rows = keep.at[at]
            got = jnp.dot(x, hits[at], preferred_element_type=F32)
            got = got[0:16] + got[16:32] + got[32:48]
            a0, a1, l0, l1 = jacobian(rows, 2)
            v0 = jnp.sum(a0 * got[0:8], axis=0, keepdims=True) + l0 * got[8:9]
            v1 = jnp.sum(a1 * got[0:8], axis=0, keepdims=True) + l1 * got[8:9]
            for e in range(2):
                m = [rows[56 + 4 * e + n : 57 + 4 * e + n] for n in range(4)]
                z0, z1 = m[0] * v0 + m[1] * v1, m[2] * v0 + m[3] * v1
                a0, a1, l0, l1 = jacobian(rows, e)
                out8 = a0 * lanes_of(z0, 8) + a1 * lanes_of(z1, 8)
                terms = [out8, l0 * z0 + l1 * z1, jnp.zeros((7, LANES), F32)]
                slot = rows[51 + e : 52 + e].astype(jnp.int32)
                slot = jnp.where(slot >= 0, slot + CAM * e, -1)
                hit = (lanes_of(slot, 128) == iota((128, LANES), 0)).astype(F32).astype(BF)
                image[...] += lax.dot_general(
                    three(jnp.concatenate(terms, axis=0)), hit, NT, preferred_element_type=F32
                )

        y = image[0:16] + image[16:32] + image[32:48]
        own = iota((16, 128), 1) < CAM
        extra = jnp.concatenate([damp[8:16] * x8, damp[17:18] * x9, jnp.zeros((7, 128), F32)], axis=0)
        extra = jnp.where(own, extra, 0.0)
        y += jnp.where(flag_ref[0] == 1, extra, 0.0)
        y += jnp.where(flag_ref[1] == 1, pltpu.roll(extra, CAM, 1), 0.0)
        part = sums[pl.ds(3 * flag_ref[2], 3), :]
        block = jnp.concatenate([y[0:9], part, jnp.zeros((4, 128), F32)], axis=0)
        out_ref[...] = jnp.broadcast_to(block[None], (NDEV, 16, 128))


def cg_part(flags, incoming, damp):
    steps = NDEV // SRC
    return pl.pallas_call(
        cg_kernel,
        grid=(steps,),
        in_specs=[
            pl.BlockSpec(memory_space=pltpu.SMEM),
            pl.BlockSpec((SRC, SENT, PTS), lambda s: (s, 0, 0)),
            whole(24, 128),
        ],
        out_specs=[pl.BlockSpec((ROWS, LANES), lambda s: (0, s)), whole(NDEV, 16, 128)],
        out_shape=[
            jax.ShapeDtypeStruct((ROWS, steps * LANES), F32),
            jax.ShapeDtypeStruct((NDEV, 16, 128), F32),
        ],
        scratch_shapes=[
            pltpu.VMEM((steps, ROWS, LANES), F32),
            pltpu.VMEM((steps, 128, LANES), BF),
            pltpu.VMEM((72, 128), F32),
            pltpu.VMEM((48, 128), F32),
        ],
        name="cg",
        **settings(6, 60),
    )(flags, incoming, damp)


def split(value):
    high = value.astype(BF).astype(F32)
    return high, value - high


def add_products(e, rows_ref, prod, acc):
    a0, a1, last0, last1 = jacobian(rows_ref, e)
    cam0, cam1, cam_last0, cam_last1 = jacobian(rows_ref, 2)
    t, t_last = [], []
    for m in range(2):
        at = 56 + 4 * e + 2 * m
        m0, m1 = rows_ref[at : at + 1], rows_ref[at + 1 : at + 2]
        t.append(lanes_of(m0, 8) * cam0 + lanes_of(m1, 8) * cam1)
        t_last.append(m0 * cam_last0 + m1 * cam_last1)
    for j in range(9):
        t0 = t[0][j : j + 1] if j < 8 else t_last[0]
        t1 = t[1][j : j + 1] if j < 8 else t_last[1]
        high, low = split(a0 * lanes_of(t0, 8) + a1 * lanes_of(t1, 8))
        prod[0, j, 0:8] = high
        prod[1, j, 0:8] = low
        high, low = split(last0 * t0 + last1 * t1)
        prod[0, j, 8:9] = high
        prod[1, j, 8:9] = low
    slot_a = rows_ref[51 + e : 52 + e].astype(jnp.int32)
    slot_c = rows_ref[53:54].astype(jnp.int32)
    both = jnp.minimum(slot_a, slot_c) >= 0
    code = jnp.where(both, (slot_a >> 4) * CAM + slot_c, -1)
    onehot = (lanes_of(code, 256) == iota((256, LANES), 0)).astype(F32).astype(BF)
    mask = (lanes_of(slot_a & 15, 16) == iota((16, LANES), 0)).astype(F32).astype(BF)
    n = GROUP * 144
    for g in range(9 // GROUP):
        parts = []
        for h in range(2):
            for j in range(g * GROUP, (g + 1) * GROUP):
                for i in range(9):
                    parts.append(lanes_of(prod[h, j, i : i + 1], 16).astype(BF) * mask)
        left = jnp.concatenate(parts, axis=0)
        got = lax.dot_general(left, onehot, NT, preferred_element_type=F32)
        acc[e, g * n : (g + 1) * n, :] += got[:n] + got[n:]


def assemble(e, read, flag, damp_ref, out_ref, stage, wide_ref):
    source = iota((640, 640), 0)
    place = iota((640, 640), 1) == 9 * (source % CAM) + source // CAM
    place = (place & (source < TILE)).astype(F32).astype(BF)
    lane = iota((144, PTS), 1)
    for u in range(4):
        base = (u // 2) * 128
        tiles = []
        for jj in range(5):
            even = read(2 * jj, base)
            if u % 2:
                even = pltpu.roll(even, 64, 1)
            if jj < 4:
                odd = read(2 * jj + 1, base)
                if u % 2 == 0:
                    odd = pltpu.roll(odd, 64, 1)
                even = jnp.where(lane < CAM, even, odd)
            tiles.append(even)
        full = jnp.concatenate(tiles, axis=1)
        high = full.astype(BF)
        wide_ref[144 * u : 144 * u + 144] = high
        wide_ref[TILE + 144 * u : TILE + 144 * u + 144] = (full - high.astype(F32)).astype(BF)
    got = jnp.dot(wide_ref[...], place, preferred_element_type=F32)
    got = got[:TILE] + got[TILE:]
    for u in range(4):
        for tile in range(5):
            for i in range(9):
                at = 144 * u + 16 * i
                piece = got[at : at + 16, 128 * tile : 128 * tile + 128]
                stage[pl.ds(TILE * tile + 144 * u + i, 16, stride=9), :] = piece
    for tile in range(5):
        wide = min(128, TILE - 128 * tile)
        block = stage[TILE * tile : TILE * tile + TILE, 0:wide]
        out_ref[e, :, 128 * tile : 128 * tile + wide] = block

    @pl.when(flag == 1)
    def _():
        same = iota((TILE, TILE), 0) == iota((TILE, TILE), 1)
        out_ref[e] += jnp.where(same, jnp.broadcast_to(damp_ref[...], (TILE, TILE)), 0.0)


def spread_kernel(flag_ref, rows_ref, damp_ref, behind, out_ref, token, prod, acc, stage, wide_ref):
    step = pl.program_id(0)

    @pl.when(step == 0)
    def _():
        acc[...] = jnp.zeros_like(acc)

    for e in range(2):
        add_products(e, rows_ref, prod, acc)

    @pl.when(step == pl.num_programs(0) - 1)
    def _():
        for e in range(2):

            def read(j, base):
                return acc[e, 144 * j : 144 * j + 144, base : base + 128]

            assemble(e, read, flag_ref[e], damp_ref, out_ref, stage, wide_ref)
        token[...] = jnp.zeros_like(token)


def spread(flags, rows, damp, behind):
    return pl.pallas_call(
        spread_kernel,
        grid=(NDEV // SRC,),
        in_specs=[
            pl.BlockSpec(memory_space=pltpu.SMEM),
            pl.BlockSpec((ROWS, LANES), lambda s: (0, s)),
            whole(1, TILE),
            ANY,
        ],
        out_specs=[whole(2, TILE, TILE), whole(8, 128)],
        out_shape=[
            jax.ShapeDtypeStruct((2, TILE, TILE), F32),
            jax.ShapeDtypeStruct((8, 128), F32),
        ],
        scratch_shapes=[
            pltpu.VMEM((2, 9, 16, LANES), F32),
            pltpu.VMEM((2, 1296, 256), F32),
            pltpu.VMEM((5 * TILE, 128), F32),
            pltpu.VMEM((2 * TILE, 640), BF),
        ],
        name="spread",
        **settings(45, 60),
    )(flags, rows, damp, behind)


def finish_kernel(in_ref, behind, step_ref, res_ref, dir_ref):
    pieces = []
    for r in range(NROW):
        pieces.append(jnp.sum(in_ref[NCL * r : NCL * r + NCL], axis=0))
    lane = iota((16, 128), 1)
    image = jnp.concatenate([jnp.where(iota((16, 128), 0) < 9, p, 0.0) for p in pieces], axis=1)
    both = []
    for c in range(NCL):
        rows = jnp.concatenate([in_ref[NCL * r + c, 9:12, :] for r in range(6)], axis=0)
        both.append(rows)
    wide = iota((18, 128), 1)
    both = [
        jnp.where(wide < CAM, both[2 * g], pltpu.roll(both[2 * g + 1], CAM, 1))
        for g in range(NCL // 2)
    ]
    both = jnp.concatenate(both, axis=1)
    pad = jnp.zeros((7, NCL * CAM), F32)
    rhs = jnp.concatenate([both[0:8], both[16:17], pad], axis=0)
    diag = jnp.concatenate([both[8:16], both[17:18], pad + 1.0], axis=0)
    start = rhs / diag
    rz = jnp.sum(rhs * start)
    alpha = rz / jnp.sum(start * image)
    residual = rhs - alpha * image
    second = residual / diag
    beta = jnp.sum(residual * second) / rz
    values = (alpha * start, residual, second + beta * start)
    for r in range(9):
        at = 128 * r + lane
        camera = at // 9
        keep = at - 9 * camera == iota((16, 128), 0)
        camera = camera[0:8]
        for value, ref in zip(values, (step_ref, res_ref, dir_ref)):
            for g in range(NCL // 2):
                part = value[:, 128 * g : 128 * g + 128]
                top = jnp.take_along_axis(part[0:8], camera, axis=1)
                low = jnp.take_along_axis(part[8:16], camera, axis=1)
                found = jnp.where(keep, jnp.concatenate([top, low], axis=0), 0.0)
                ref[9 * g + r : 9 * g + r + 1, :] = jnp.sum(found, axis=0, keepdims=True)


def finish(incoming, behind):
    return pl.pallas_call(
        finish_kernel,
        grid=(1,),
        in_specs=[whole(NDEV, 16, 128), ANY],
        out_specs=[whole(72, 128)] * 3,
        out_shape=[jax.ShapeDtypeStruct((72, 128), F32)] * 3,
        name="finish",
        **settings(3, 60),
    )(incoming, behind)


def shards(jac_cam, jac_pt, resid, point_damp, cam_damp, obs_cluster, obs_slot):
    my_row = lax.axis_index("row")
    my_col = lax.axis_index("col")
    flags = (2 * my_row + jnp.arange(2) == my_col).astype(jnp.int32)
    flags = jnp.concatenate([flags, my_row[None].astype(jnp.int32)])
    damp = jnp.pad(cam_damp.reshape(CAM, 9).T, ((0, 0), (0, 128 - CAM)), constant_values=1.0)
    zeros = jnp.zeros((8, 128), F32)
    damp = jnp.concatenate([zeros, damp[0:8], zeros[0:1], damp[8:9], zeros[0:6]], axis=0)
    dense, found = points(
        jac_cam.transpose(1, 0, 2), jac_pt.transpose(1, 0, 2), resid, point_damp, obs_cluster.T,
        obs_slot,
    )
    incoming = exchange(pack(dense, found).reshape(NDEV, SENT, PTS))
    rows, share = cg_part(flags, incoming, damp)
    shares = exchange(share)
    tiles, token = spread(flags, rows, cam_damp, share)
    step, residual, direction = finish(shares, token)
    return (tiles[:, None], step.reshape(-1), residual.reshape(-1), direction.reshape(-1))


def solution(mesh):
    placed = (
        P(None, None, AXES),
        P(None, None, AXES),
        P(None, None, AXES),
        P(None, AXES),
        P("col", None),
        P(AXES, None),
        P(None, AXES),
    )
    return jax.shard_map(
        shards,
        mesh=mesh,
        in_specs=placed,
        out_specs=(P("row", "col", None, None), P(), P(), P()),
        check_vma=False,
    )
```

time: 809 us -> 136 us (0.17); the launches traced: 795 us -> 134 us
  other arithmetic: 223 us -> 0.61 us
  local copies, waits for them, and re-layouts: 200 us -> 2.99 us
  waiting for transfers between devices: 229 us -> 42.9 us
  blocking collectives: 84.7 us -> 0 us
  Pallas kernels: 0 us -> 70.9 us
  matrix products: 28.6 us -> 0 us
  between operations: 18.2 us -> 0.71 us
    scatter-add x2 -> x0, other arithmetic: 135 us -> none  [shards(): flat = jnp.zeros((cams * cams, 81), jnp.float32).at[where].add(product_rows)]
    reshape x16 -> x2, local copies, waits for them, and re-layouts: 111 us -> 0.2 us  [shards(): cam_damp.reshape(CAM, 9)]
    all_to_all x1 -> x2, waiting for transfers between devices: 153 us -> 42.9 us  [exchange(): return lax.all_to_all(value, AXES, split_axis=0, concat_axis=0, tiled=True)]
    unnamed x2 -> x0, waiting for transfers between devices: 76.6 us -> none
    psum x2 -> x0, blocking collectives: 71.6 us -> none  [the longest x1 38.8 us: shards(): rhs_col, diag_col = lax.psum((rhs_part, diag_part), 'row')]
    pallas_call x0 -> x5, Pallas kernels: none -> 70.9 us  [the longest x1 43.6 us: spread(): pl.pallas_call(spread_kernel, grid=(NDEV // SRC,), in_specs=[pl.BlockSpec...]
    transpose x6 -> x0, local copies, waits for them, and re-layouts: 34.1 us -> none  [the longest x2 19.8 us: shards(): flat.reshape(cams, cams, 9, 9).transpose(0, 2, 1, 3).reshape(tile, tile)]
    dot_general x8 -> x0, matrix products: 28.6 us -> none  [the longest x1 15.8 us: spread(): jnp.einsum('csg,sfg->cfg', weights, values, precision=lax.Precision.HIGHEST)]
  transfers between devices with their start and end apart: 2 -> 2, of which waited for: 2 -> 1; matrix products, arithmetic and copies ran while one was open for 1% -> 2% of each run, Pallas kernels for 0% -> 32%
where the time goes in v2:
time: 136 us; the launch traced here: 134 us
  Pallas kernels  70.9 us (52%)
  waiting for transfers between devices  42.9 us (32%)
  starting transfers between devices  16 us (12%)
  local copies, waits for them, and re-layouts  2.99 us (2%)
    pallas_call x1, Pallas kernels, spread(): pl.pallas_call(spread_kernel, grid=(NDEV // SRC,), in_specs=[pl.BlockSpec...  43.6 us
    all_to_all x2, waiting for transfers between devices, exchange(): return lax.all_to_all(value, AXES, split_axis=0, concat_axis=0, tiled=True)  42.9 us
    all_to_all x2, starting transfers between devices, exchange(): return lax.all_to_all(value, AXES, split_axis=0, concat_axis=0, tiled=True)  16 us
    pallas_call x1, Pallas kernels, cg_part(): pl.pallas_call(cg_kernel, grid=(steps,), in_specs=[pl.BlockSpec(memory_sp...  13.4 us
    pallas_call x1, Pallas kernels, pack(): pl.pallas_call(pack_kernel, grid=(NROW,), in_specs=[whole(29, 2, NROW, PT...  6.67 us
    pallas_call x1, Pallas kernels, points(): pl.pallas_call(points_kernel, grid=(1,), in_specs=[whole(*a.shape) for a...  4.48 us
    pallas_call x1, Pallas kernels, finish(): pl.pallas_call(finish_kernel, grid=(1,), in_specs=[whole(NDEV, 16, 128),...  2.79 us
  transfers between devices with their start and end apart: 2, of which 1 were waited for; matrix products, arithmetic and copies ran while one was open for 2% of the time, Pallas kernels for 32%

profile of v2, /device:TPU:24, one launch (start us, length us, event | category | flops | bytes accessed | tf_op | source)
XLA Modules:
  0.0 134.2 jit_solution(8524099092901133104)
XLA Ops:
  0.6 4.5 %points.1 = (f32[29,2,8,128]{3,2,1,0:T(8,128)}, f32[16,8,128]{2,1,0:T(8,128)}) custom-call(f32[18,8,128]{2,1,0:T(8,128)} %bitcast.15, f32[6,8,128]{2,1,0:T(8,128)} %bitcast.16, f32[8,2,128]{2,1,0:T(2,128)} %rs.1, f32[3,128]{1,0:T(4,128)} %damp.1, s32[8,128]{1,0:T(8,128)} %bitcast.17, s32[8,128]{1,0:T(8,128)} %slot_ref.1), custom_call_target="tpu_custom_call" | custom-call | flops 4000000000 | bytes 1000000 | tf_op jit(solution)/shard_map/points/pallas_call | solution.py:139
  5.1 6.7 %pack.1 = f32[8,16,56,128]{3,2,1,0:T(8,128)} custom-call(f32[29,2,8,128]{3,2,1,0:T(8,128)} %get-tuple-element.13.dense, f32[16,8,128]{2,1,0:T(8,128)} %get-tuple-element.14.found_ref), custom_call_target="tpu_custom_call" | custom-call | flops 8000000000 | bytes 1000000 | tf_op jit(solution)/shard_map/pack/pallas_call | solution.py:192
  11.8 0.0 copy-start.1
  11.8 10.7 %all-to-all-start = ((f32[128,56,128]{2,1,0:T(8,128)}), f32[128,56,128]{2,1,0:T(8,128)}, u32[]{:S(2)}, u32[]{:S(2)}) async-start(f32[128,56,128]{2,1,0:T(8,128)} %bitcast.12), calls=%async_computation | async-start | bytes 7340032 | tf_op jit(solution)/shard_map/all_to_all | solution.py:205
  22.5 0.0 copy-done.1
  22.5 0.1 reshape.24
  22.6 0.1 copy.12
  22.8 1.8 %concatenate.7.damp_ref = f32[24,128]{1,0:T(8,128)} concatenate(f32[8,128]{1,0:T(8,128)S(1)} %broadcast_in_dim.10, f32[8,128]{1,0:T(8,128)S(1)} %pad_slice_fusion.1, f32[1,128]{1,0:T(1,128)S(1)} %slice.13, f32[1,128]{1,0:T(1,128)S(1)} %pad_slice_fusion, f32[6,128]{1,0:T(8,128)S(1)} %slice.15), dimensions={0} | concatenate | bytes 24576 | tf_op jit(solution)/shard_map/concatenate | solution.py:519
  24.6 0.6 pad_add_fusion.flag_ref
  25.1 42.9 %all-to-all-done.in_ref = f32[128,56,128]{2,1,0:T(8,128)} async-done(((f32[128,56,128]{2,1,0:T(8,128)}), f32[128,56,128]{2,1,0:T(8,128)}, u32[]{:S(2)}, u32[]{:S(2)}) %all-to-all-start) | async-done | bytes 3670048 | tf_op jit(solution)/shard_map/all_to_all | solution.py:205
  68.1 13.4 %cg.1 = (f32[72,12288]{1,0:T(8,128)}, f32[128,16,128]{2,1,0:T(8,128)}) custom-call(s32[3]{0:T(128)} %pad_add_fusion.flag_ref, f32[128,56,128]{2,1,0:T(8,128)} %all-to-all-done.in_ref, f32[24,128]{1,0:T(8,128)} %concatenate.7.damp_ref), custom_call_target="tpu_custom_call" | custom-call | flops 6000000000 | bytes 1000000 | tf_op jit(solution)/shard_map/cg/pallas_call | solution.py:307
  81.5 5.4 %all-to-all-start.1 = ((f32[128,16,128]{2,1,0:T(8,128)}), f32[128,16,128]{2,1,0:T(8,128)S(1)}, u32[]{:S(2)}, u32[]{:S(2)}) async-start(f32[128,16,128]{2,1,0:T(8,128)} %get-tuple-element.16.behind), calls=%async_computation.1 | async-start | bytes 2097152 | tf_op jit(solution)/shard_map/all_to_all | solution.py:205
  86.8 43.6 %spread.1 = (f32[2,576,576]{2,1,0:T(8,128)}, f32[8,128]{1,0:T(8,128)}) custom-call(s32[3]{0:T(128)} %pad_add_fusion.flag_ref, f32[72,12288]{1,0:T(8,128)} %get-tuple-element.15.rows_ref, f32[1,576]{1,0:T(1,128)} %damp_ref.1, f32[128,16,128]{2,1,0:T(8,128)} %get-tuple-element.16.behind), custom_call_target="tpu_custom_call" | custom-call | flops 44999999488 | bytes 1000000 | tf_op jit(solution)/shard_map/spread/pallas_call | solution.py:435
  130.4 0.0 all-to-all-done.1.in_ref
  130.4 0.0 copy-start
  130.4 1.0 copy-done
  131.4 2.8 %finish.1 = (f32[72,128]{1,0:T(8,128)}, f32[72,128]{1,0:T(8,128)}, f32[72,128]{1,0:T(8,128)}) custom-call(f32[128,16,128]{2,1,0:T(8,128)} %copy-done, f32[8,128]{1,0:T(8,128)} %get-tuple-element.18.behind), custom_call_target="tpu_custom_call" | custom-call | flops 3000000000 | bytes 1000000 | tf_op jit(solution)/shard_map/finish/pallas_call | solution.py:501
  (7 shorter events, 0.1 us)
Async XLA Ops:
  11.8 10.7 %copy-start.1 = (f32[1,576]{1,0:T(1,128)S(1)}, f32[1,576]{1,0:T(1,128)}, u32[]{:S(2)}) copy-start(f32[1,576]{1,0:T(1,128)} %damp_ref.1) | copy-start | bytes 6916
  11.8 56.3 %all-to-all-start = ((f32[128,56,128]{2,1,0:T(8,128)}), f32[128,56,128]{2,1,0:T(8,128)}, u32[]{:S(2)}, u32[]{:S(2)}) async-start(f32[128,56,128]{2,1,0:T(8,128)} %bitcast.12), calls=%async_computation | async-start | bytes 7340032 | tf_op jit(solution)/shard_map/all_to_all | solution.py:205
  81.5 49.0 %all-to-all-start.1 = ((f32[128,16,128]{2,1,0:T(8,128)}), f32[128,16,128]{2,1,0:T(8,128)S(1)}, u32[]{:S(2)}, u32[]{:S(2)}) async-start(f32[128,16,128]{2,1,0:T(8,128)} %get-tuple-element.16.behind), calls=%async_computation.1 | async-start | bytes 2097152 | tf_op jit(solution)/shard_map/all_to_all | solution.py:205
  130.4 1.0 copy-start

commit v3 on v2

--- a/solution.py
+++ b/solution.py
@@ -17,10 +17,12 @@
 PTS = 128
 AXES = ("row", "col")
 BF = jnp.bfloat16
+F8 = jnp.float8_e4m3fn
 F32 = jnp.float32
 NT = (((1,), (1,)), ((), ()))
 MIB = 1 << 20
-SRC = 16
+SRC = 32
+PAIRS = 2
 LANES = SRC * CAP
 GROUP = 3
 ANY = pl.BlockSpec(memory_space=pl.ANY)
@@ -72,6 +74,12 @@
     return u, q
 
 
+def hot(code, n):
+    codes = lanes_of(code.astype(F32), n).astype(BF)
+    ids = iota((n, code.shape[1]), 0).astype(F32).astype(BF)
+    return jnp.where(codes == ids, jnp.ones((), BF), jnp.zeros((), BF))
+
+
 def three(value):
     a = value.astype(BF)
     rest = value - a.astype(F32)
@@ -79,17 +87,18 @@
     return jnp.concatenate([a, b, (rest - b.astype(F32)).astype(BF)], axis=0)
 
 
-def chosen(dense, pair, ec):
-    upto = (iota((PTS, PTS), 1) <= iota((PTS, PTS), 0)).astype(F32).astype(BF)
-    lane = iota((PTS, PTS), 1).astype(F32)
-    present = (dense[23, ec, pl.ds(pair, 1), :] >= 0.0).astype(F32)
-    present = lanes_of(present, PTS).astype(BF)
-    counts = lax.dot_general(upto, present, NT, preferred_element_type=F32)
-    before = (counts <= lane).astype(F32).astype(BF)
-    return jnp.dot(jnp.ones((NROW, PTS), BF), before, preferred_element_type=F32)
-
-
-def points_kernel(jc, jp, rs, damp, cl_ref, slot_ref, dense, found_ref, fields):
+def chosen(named):
+    upto = (iota((PTS, PTS), 0) <= iota((PTS, PTS), 1)).astype(F32).astype(BF)
+    counts = jnp.dot(named.astype(BF), upto, preferred_element_type=F32)
+    lane = iota(named.shape, 1)
+    at = jnp.zeros(named.shape, jnp.int32)
+    for jump in (64, 32, 16, 8, 4, 2, 1):
+        seen = jnp.take_along_axis(counts, at + (jump - 1), axis=1)
+        at = jnp.where(seen <= lane.astype(F32), at + jump, at)
+    return jnp.where(lane.astype(F32) < counts[:, PTS - 1 : PTS], at, PTS)
+
+
+def points_part(jc, jp, rs, damp, cl_ref, slot_ref, dense, found_ref, fields):
     cl, slot = cl_ref[...], slot_ref[...]
     u, q = whitened(
         [[jp[m * 3 + a] for a in range(3)] for m in range(2)],
@@ -129,23 +138,7 @@
             for k in range(KOBS):
                 value = jnp.where(hits[k], lanes_of(fields[f, k : k + 1, :], NROW), value)
             dense[f, e] = value
-    for r in range(NROW):
-        for e in range(2):
-            found_ref[2 * r + e] = chosen(dense, r, e)
-
-
-def points(*args):
-    shapes = [(29, 2, NROW, PTS), (NCL, NROW, PTS)]
-    return pl.pallas_call(
-        points_kernel,
-        grid=(1,),
-        in_specs=[whole(*a.shape) for a in args],
-        out_specs=[whole(*shape) for shape in shapes],
-        out_shape=[jax.ShapeDtypeStruct(shape, F32) for shape in shapes],
-        scratch_shapes=[pltpu.VMEM((29, KOBS, PTS), F32)],
-        name="points",
-        **settings(4, 60),
-    )(*args)
+        found_ref[e] = chosen((dense[23, e] >= 0.0).astype(F32))
 
 
 def mixed(side, mine, on):
@@ -157,25 +150,36 @@
     return out
 
 
-def pack_kernel(dense, found_ref, out_ref, kept):
-    pair = pl.program_id(0)
+def pack_kernel(jc, jp, rs, damp, cl, slot, out_ref, dense, found_ref, fields, kept):
+    step = pl.program_id(0)
+
+    @pl.when(step == 0)
+    def _():
+        points_part(jc, jp, rs, damp, cl, slot, dense, found_ref, fields)
+
+    for part in range(PAIRS):
+        pack_pair(step * PAIRS + part, part, out_ref, dense, found_ref, kept)
+
+
+def pack_pair(pair, part, out_ref, dense, found_ref, kept):
     lane = iota((NROW, PTS), 1)
     zero = jnp.zeros((NROW, PTS), F32)
+    flat = out_ref.reshape(NROW * 2 * PAIRS * SENT, PTS)
     for ec in range(2):
-        found = found_ref[2 * pair + ec]
-        pick = jnp.minimum(found, float(PTS - 1)).astype(jnp.int32)
+        found = lanes_of(found_ref[ec, pl.ds(pair, 1), :], NROW)
+        pick = jnp.minimum(found, PTS - 1)
         side = [
             [jnp.take_along_axis(dense[f, e], pick, axis=1) for f in range(24)] for e in range(2)
         ]
         for f in range(29):
             if f < 24:
-                kept[f] = side[ec][f]
+                kept[2 * part + ec, f] = side[ec][f]
             else:
-                kept[f] = jnp.take_along_axis(dense[f, ec], pick, axis=1)
-        mine = [lanes_of(kept[f, pl.ds(pair, 1), :], NROW) for f in range(29)]
+                kept[2 * part + ec, f] = jnp.take_along_axis(dense[f, ec], pick, axis=1)
+        mine = [lanes_of(kept[2 * part + ec, f, pl.ds(pair, 1), :], NROW) for f in range(29)]
         rows = side[0][0:16] + side[1][0:16] + mine[0:16]
         rows += [side[0][16], side[1][16], mine[16], side[0][23], side[1][23]]
-        rows.append(jnp.where(found < float(PTS), mine[23], -1.0))
+        rows.append(jnp.where(found < PTS, mine[23], -1.0))
         rows += mine[24:26]
         extra = []
         for e in range(2):
@@ -185,20 +189,26 @@
         for at, row in enumerate(rows):
             v, x = at // 16, at % 16
             rest = pltpu.roll(extra[x], 96 - 32 * v, 1) if v < 3 and x < 11 else zero
-            out_ref[:, ec, at, :] = jnp.where(lane < CAP, row, rest)
-
-
-def pack(dense, found):
+            at = SENT * (2 * part + ec) + at
+            flat[pl.ds(at, NROW, stride=2 * PAIRS * SENT), :] = jnp.where(lane < CAP, row, rest)
+
+
+def pack(*args):
     return pl.pallas_call(
         pack_kernel,
-        grid=(NROW,),
-        in_specs=[whole(29, 2, NROW, PTS), whole(NCL, NROW, PTS)],
-        out_specs=pl.BlockSpec((NROW, 2, SENT, PTS), lambda g: (0, g, 0, 0)),
+        grid=(NROW // PAIRS,),
+        in_specs=[whole(*a.shape) for a in args],
+        out_specs=pl.BlockSpec((NROW, 2 * PAIRS, SENT, PTS), lambda g: (0, g, 0, 0)),
         out_shape=jax.ShapeDtypeStruct((NROW, NCL, SENT, PTS), F32),
-        scratch_shapes=[pltpu.VMEM((29, NROW, PTS), F32)],
+        scratch_shapes=[
+            pltpu.VMEM((29, 2, NROW, PTS), F32),
+            pltpu.VMEM((2, NROW, PTS), jnp.int32),
+            pltpu.VMEM((29, KOBS, PTS), F32),
+            pltpu.VMEM((2 * PAIRS, 29, NROW, PTS), F32),
+        ],
         name="pack",
         **settings(8, 60),
-    )(dense, found)
+    )(*args)
 
 
 def exchange(value):
@@ -234,15 +244,21 @@
     return rows_ref[at : at + 8], a1, rows_ref[at + 8 : at + 9], rows_ref[48 + which : 49 + which]
 
 
-def cg_kernel(flag_ref, in_ref, damp_ref, rows_ref, out_ref, keep, hits, sums, image):
+def cg_kernel(
+    flag_ref, in_ref, damp_ref, rows_ref, out_ref, scale_ref, keep, hits, sums, image, largest
+):
     step = pl.program_id(0)
     steps = pl.num_programs(0)
 
     @pl.when(step == 0)
     def _():
         sums[...] = jnp.zeros_like(sums)
+        largest[...] = jnp.zeros_like(largest)
 
     lay(in_ref, rows_ref)
+    top = [jnp.max(jnp.abs(rows_ref[8 * v : 8 * v + 8]), axis=0, keepdims=True) for v in range(6)]
+    top.append(jnp.max(jnp.abs(rows_ref[48:51]), axis=0, keepdims=True))
+    largest[...] = jnp.maximum(largest[...], functools.reduce(jnp.maximum, top))
     a0, a1, l0, l1 = jacobian(rows_ref, 2)
     q0, q1 = rows_ref[54:55], rows_ref[55:56]
     m0, m1, m2 = rows_ref[64:65], rows_ref[65:66], rows_ref[66:67]
@@ -251,10 +267,10 @@
         a0 * a0 * lanes_of(m0, 8) + a0 * a1 * lanes_of(m1, 8) + a1 * a1 * lanes_of(m2, 8),
         l0 * q0 + l1 * q1,
         l0 * l0 * m0 + l0 * l1 * m1 + l1 * l1 * m2,
-        jnp.zeros((6, LANES), F32),
+        jnp.zeros((14, LANES), F32),
     ]
     slot = rows_ref[53:54].astype(jnp.int32)
-    hit = (lanes_of(slot, 128) == iota((128, LANES), 0)).astype(F32).astype(BF)
+    hit = hot(slot, 128)
     hits[step] = hit
     keep[step] = rows_ref[...]
     sums[...] += lax.dot_general(
@@ -264,13 +280,13 @@
     @pl.when(step == steps - 1)
     def _():
         damp = damp_ref[...]
-        total = sums[0:24] + sums[24:48] + sums[48:72] + damp
+        total = sums[0:24] + sums[32:56] + sums[64:88] + damp
         sums[0:24] = total
         x8, x9 = total[0:8] / total[8:16], total[16:17] / total[17:18]
         x = three(jnp.concatenate([x8, x9, jnp.zeros((7, 128), F32)], axis=0))
         image[...] = jnp.zeros_like(image)
 
-        @pl.loop(0, steps)
+        @pl.loop(0, steps, unroll=4)
         def _(at):
             rows = keep.at[at]
             got = jnp.dot(x, hits[at], preferred_element_type=F32)
@@ -286,7 +302,7 @@
                 terms = [out8, l0 * z0 + l1 * z1, jnp.zeros((7, LANES), F32)]
                 slot = rows[51 + e : 52 + e].astype(jnp.int32)
                 slot = jnp.where(slot >= 0, slot + CAM * e, -1)
-                hit = (lanes_of(slot, 128) == iota((128, LANES), 0)).astype(F32).astype(BF)
+                hit = hot(slot, 128)
                 image[...] += lax.dot_general(
                     three(jnp.concatenate(terms, axis=0)), hit, NT, preferred_element_type=F32
                 )
@@ -300,6 +316,9 @@
         part = sums[pl.ds(3 * flag_ref[2], 3), :]
         block = jnp.concatenate([y[0:9], part, jnp.zeros((4, 128), F32)], axis=0)
         out_ref[...] = jnp.broadcast_to(block[None], (NDEV, 16, 128))
+        top = jnp.maximum(jnp.max(largest[...], keepdims=True), 1e-15)
+        scale = jnp.broadcast_to(32768.0 / (top * top), (8, 128))
+        scale_ref[...] = jnp.where(iota((8, 128), 0) == 1, 1.0 / scale, scale)
 
 
 def cg_part(flags, incoming, damp):
@@ -312,34 +331,41 @@
             pl.BlockSpec((SRC, SENT, PTS), lambda s: (s, 0, 0)),
             whole(24, 128),
         ],
-        out_specs=[pl.BlockSpec((ROWS, LANES), lambda s: (0, s)), whole(NDEV, 16, 128)],
+        out_specs=[
+            pl.BlockSpec((ROWS, LANES), lambda s: (0, s)),
+            whole(NDEV, 16, 128),
+            whole(8, 128),
+        ],
         out_shape=[
             jax.ShapeDtypeStruct((ROWS, steps * LANES), F32),
             jax.ShapeDtypeStruct((NDEV, 16, 128), F32),
+            jax.ShapeDtypeStruct((8, 128), F32),
         ],
         scratch_shapes=[
             pltpu.VMEM((steps, ROWS, LANES), F32),
             pltpu.VMEM((steps, 128, LANES), BF),
-            pltpu.VMEM((72, 128), F32),
+            pltpu.VMEM((96, 128), F32),
             pltpu.VMEM((48, 128), F32),
+            pltpu.VMEM((1, LANES), F32),
         ],
         name="cg",
         **settings(6, 60),
     )(flags, incoming, damp)
 
 
-def split(value):
-    high = value.astype(BF).astype(F32)
-    return high, value - high
-
-
-def add_products(e, rows_ref, prod, acc):
+def add_products(e, rows_ref, scale_ref, prod, acc):
+    scale = scale_ref[0:1, 0:1]
+
+    def split(value):
+        high = value.astype(BF).astype(F32)
+        return high, value - high
+
     a0, a1, last0, last1 = jacobian(rows_ref, e)
     cam0, cam1, cam_last0, cam_last1 = jacobian(rows_ref, 2)
     t, t_last = [], []
     for m in range(2):
         at = 56 + 4 * e + 2 * m
-        m0, m1 = rows_ref[at : at + 1], rows_ref[at + 1 : at + 2]
+        m0, m1 = rows_ref[at : at + 1] * scale, rows_ref[at + 1 : at + 2] * scale
         t.append(lanes_of(m0, 8) * cam0 + lanes_of(m1, 8) * cam1)
         t_last.append(m0 * cam_last0 + m1 * cam_last1)
     for j in range(9):
@@ -355,21 +381,24 @@
     slot_c = rows_ref[53:54].astype(jnp.int32)
     both = jnp.minimum(slot_a, slot_c) >= 0
     code = jnp.where(both, (slot_a >> 4) * CAM + slot_c, -1)
-    onehot = (lanes_of(code, 256) == iota((256, LANES), 0)).astype(F32).astype(BF)
-    mask = (lanes_of(slot_a & 15, 16) == iota((16, LANES), 0)).astype(F32).astype(BF)
+    onehot = hot(code, 256)
+    mask = hot(slot_a & 15, 16)
     n = GROUP * 144
+    onehot8 = onehot.astype(F8)
     for g in range(9 // GROUP):
-        parts = []
+        parts = [[], []]
         for h in range(2):
             for j in range(g * GROUP, (g + 1) * GROUP):
                 for i in range(9):
-                    parts.append(lanes_of(prod[h, j, i : i + 1], 16).astype(BF) * mask)
-        left = jnp.concatenate(parts, axis=0)
-        got = lax.dot_general(left, onehot, NT, preferred_element_type=F32)
-        acc[e, g * n : (g + 1) * n, :] += got[:n] + got[n:]
-
-
-def assemble(e, read, flag, damp_ref, out_ref, stage, wide_ref):
+                    parts[h].append(lanes_of(prod[h, j, i : i + 1], 16).astype(BF) * mask)
+        high = jnp.concatenate(parts[0], axis=0)
+        low = jnp.concatenate(parts[1], axis=0).astype(F8)
+        got = lax.dot_general(high, onehot, NT, preferred_element_type=F32)
+        rest = lax.dot_general(low, onehot8, NT, preferred_element_type=F32)
+        acc[e, g * n : (g + 1) * n, :] += got + rest
+
+
+def assemble(e, read, undo, flag, damp_ref, out_ref, stage, wide_ref):
     source = iota((640, 640), 0)
     place = iota((640, 640), 1) == 9 * (source % CAM) + source // CAM
     place = (place & (source < TILE)).astype(F32).astype(BF)
@@ -387,7 +416,7 @@
                     odd = pltpu.roll(odd, 64, 1)
                 even = jnp.where(lane < CAM, even, odd)
             tiles.append(even)
-        full = jnp.concatenate(tiles, axis=1)
+        full = jnp.concatenate(tiles, axis=1) * undo
         high = full.astype(BF)
         wide_ref[144 * u : 144 * u + 144] = high
         wide_ref[TILE + 144 * u : TILE + 144 * u + 144] = (full - high.astype(F32)).astype(BF)
@@ -410,7 +439,9 @@
         out_ref[e] += jnp.where(same, jnp.broadcast_to(damp_ref[...], (TILE, TILE)), 0.0)
 
 
-def spread_kernel(flag_ref, rows_ref, damp_ref, behind, out_ref, token, prod, acc, stage, wide_ref):
+def spread_kernel(
+    flag_ref, rows_ref, scale_ref, damp_ref, behind, out_ref, token, prod, acc, stage, wide_ref
+):
     step = pl.program_id(0)
 
     @pl.when(step == 0)
@@ -418,7 +449,7 @@
         acc[...] = jnp.zeros_like(acc)
 
     for e in range(2):
-        add_products(e, rows_ref, prod, acc)
+        add_products(e, rows_ref, scale_ref, prod, acc)
 
     @pl.when(step == pl.num_programs(0) - 1)
     def _():
@@ -427,17 +458,18 @@
             def read(j, base):
                 return acc[e, 144 * j : 144 * j + 144, base : base + 128]
 
-            assemble(e, read, flag_ref[e], damp_ref, out_ref, stage, wide_ref)
+            assemble(e, read, scale_ref[1:2, 0:1], flag_ref[e], damp_ref, out_ref, stage, wide_ref)
         token[...] = jnp.zeros_like(token)
 
 
-def spread(flags, rows, damp, behind):
+def spread(flags, rows, scale, damp, behind):
     return pl.pallas_call(
         spread_kernel,
         grid=(NDEV // SRC,),
         in_specs=[
             pl.BlockSpec(memory_space=pltpu.SMEM),
             pl.BlockSpec((ROWS, LANES), lambda s: (0, s)),
+            whole(8, 128),
             whole(1, TILE),
             ANY,
         ],
@@ -454,7 +486,7 @@
         ],
         name="spread",
         **settings(45, 60),
-    )(flags, rows, damp, behind)
+    )(flags, rows, scale, damp, behind)
 
 
 def finish_kernel(in_ref, behind, step_ref, res_ref, dir_ref):
@@ -517,14 +549,14 @@
     damp = jnp.pad(cam_damp.reshape(CAM, 9).T, ((0, 0), (0, 128 - CAM)), constant_values=1.0)
     zeros = jnp.zeros((8, 128), F32)
     damp = jnp.concatenate([zeros, damp[0:8], zeros[0:1], damp[8:9], zeros[0:6]], axis=0)
-    dense, found = points(
+    packed = pack(
         jac_cam.transpose(1, 0, 2), jac_pt.transpose(1, 0, 2), resid, point_damp, obs_cluster.T,
         obs_slot,
     )
-    incoming = exchange(pack(dense, found).reshape(NDEV, SENT, PTS))
-    rows, share = cg_part(flags, incoming, damp)
+    incoming = exchange(packed.reshape(NDEV, SENT, PTS))
+    rows, share, scale = cg_part(flags, incoming, damp)
     shares = exchange(share)
-    tiles, token = spread(flags, rows, cam_damp, share)
+    tiles, token = spread(flags, rows, scale, cam_damp, share)
     step, residual, direction = finish(shares, token)
     return (tiles[:, None], step.reshape(-1), residual.reshape(-1), direction.reshape(-1))
 

time: 136 us -> 120 us (0.88)
  Pallas kernels: 70.9 us -> 55.5 us
    pallas_call x1, Pallas kernels: 43.6 us -> 36.3 us  [spread(): pl.pallas_call(spread_kernel, grid=(NDEV // SRC,), in_specs=[pl.BlockSpec...]
    pallas_call x2 -> x1, Pallas kernels: 11.1 us -> 6.23 us  [pack(): pl.pallas_call(pack_kernel, grid=(NROW // PAIRS,), in_specs=[whole(*a.sha...]
    pallas_call x1, Pallas kernels: 13.4 us -> 10.1 us  [cg_part(): pl.pallas_call(cg_kernel, grid=(steps,), in_specs=[pl.BlockSpec(memory_sp...]
  transfers between devices with their start and end apart: 2 -> 2, of which waited for: 1 -> 1; matrix products, arithmetic and copies ran while one was open for 2% -> 2% of each run, Pallas kernels for 32% -> 31%
where the time goes in v3:
time: 120 us; the launch traced here: 119 us
  Pallas kernels  55.5 us (46%)
  waiting for transfers between devices  42.9 us (36%)
  starting transfers between devices  16.1 us (13%)
  local copies, waits for them, and re-layouts  3 us (2%)
    all_to_all x2, waiting for transfers between devices, exchange(): return lax.all_to_all(value, AXES, split_axis=0, concat_axis=0, tiled=True)  42.9 us
    pallas_call x1, Pallas kernels, spread(): pl.pallas_call(spread_kernel, grid=(NDEV // SRC,), in_specs=[pl.BlockSpec...  36.3 us
    all_to_all x2, starting transfers between devices, exchange(): return lax.all_to_all(value, AXES, split_axis=0, concat_axis=0, tiled=True)  16.1 us
    pallas_call x1, Pallas kernels, cg_part(): pl.pallas_call(cg_kernel, grid=(steps,), in_specs=[pl.BlockSpec(memory_sp...  10.1 us
    pallas_call x1, Pallas kernels, pack(): pl.pallas_call(pack_kernel, grid=(NROW // PAIRS,), in_specs=[whole(*a.sha...  6.23 us
    pallas_call x1, Pallas kernels, finish(): pl.pallas_call(finish_kernel, grid=(1,), in_specs=[whole(NDEV, 16, 128),...  2.79 us
  transfers between devices with their start and end apart: 2, of which 1 were waited for; matrix products, arithmetic and copies ran while one was open for 2% of the time, Pallas kernels for 31%

profile of v3, /device:TPU:24, one launch (start us, length us, event | category | flops | bytes accessed | tf_op | source)
XLA Modules:
  0.0 118.8 jit_solution(14352828640098485453)
XLA Ops:
  0.6 6.2 %pack.1 = f32[8,16,56,128]{3,2,1,0:T(8,128)} custom-call(f32[18,8,128]{2,1,0:T(8,128)} %bitcast.15, f32[6,8,128]{2,1,0:T(8,128)} %bitcast.16, f32[8,2,128]{2,1,0:T(2,128)} %rs.1, f32[3,128]{1,0:T(4,128)} %damp.1, s32[8,128]{1,0:T(8,128)} %bitcast.17, s32[8,128]{1,0:T(8,128)} %slot.1), custom_call_target="tpu_custom_call" | custom-call | flops 8000000000 | bytes 1000000 | tf_op jit(solution)/shard_map/pack/pallas_call | solution.py:197
  6.9 0.0 copy-start.1
  6.9 10.7 %all-to-all-start = ((f32[128,56,128]{2,1,0:T(8,128)}), f32[128,56,128]{2,1,0:T(8,128)}, u32[]{:S(2)}, u32[]{:S(2)}) async-start(f32[128,56,128]{2,1,0:T(8,128)} %bitcast.12), calls=%async_computation | async-start | bytes 7340032 | tf_op jit(solution)/shard_map/all_to_all | solution.py:215
  17.6 0.0 copy-done.1
  17.6 0.1 reshape.24
  17.7 0.1 copy.12
  17.8 1.8 %concatenate.7.damp_ref = f32[24,128]{1,0:T(8,128)} concatenate(f32[8,128]{1,0:T(8,128)S(1)} %broadcast_in_dim.10, f32[8,128]{1,0:T(8,128)S(1)} %pad_slice_fusion.1, f32[1,128]{1,0:T(1,128)S(1)} %slice.13, f32[1,128]{1,0:T(1,128)S(1)} %pad_slice_fusion, f32[6,128]{1,0:T(8,128)S(1)} %slice.15), dimensions={0} | concatenate | bytes 24576 | tf_op jit(solution)/shard_map/concatenate | solution.py:551
  19.6 0.6 pad_add_fusion.flag_ref
  20.2 42.9 %all-to-all-done.in_ref = f32[128,56,128]{2,1,0:T(8,128)} async-done(((f32[128,56,128]{2,1,0:T(8,128)}), f32[128,56,128]{2,1,0:T(8,128)}, u32[]{:S(2)}, u32[]{:S(2)}) %all-to-all-start) | async-done | bytes 3670048 | tf_op jit(solution)/shard_map/all_to_all | solution.py:215
  63.1 10.1 %cg.1 = (f32[72,12288]{1,0:T(8,128)}, f32[128,16,128]{2,1,0:T(8,128)}, f32[8,128]{1,0:T(8,128)}) custom-call(s32[3]{0:T(128)} %pad_add_fusion.flag_ref, f32[128,56,128]{2,1,0:T(8,128)} %all-to-all-done.in_ref, f32[24,128]{1,0:T(8,128)} %concatenate.7.damp_ref), custom_call_target="tpu_custom_call" | custom-call | flops 6000000000 | bytes 1000000 | tf_op jit(solution)/shard_map/cg/pallas_call | solution.py:326
  73.3 5.4 %all-to-all-start.1 = ((f32[128,16,128]{2,1,0:T(8,128)}), f32[128,16,128]{2,1,0:T(8,128)S(1)}, u32[]{:S(2)}, u32[]{:S(2)}) async-start(f32[128,16,128]{2,1,0:T(8,128)} %get-tuple-element.14.behind), calls=%async_computation.1 | async-start | bytes 2097152 | tf_op jit(solution)/shard_map/all_to_all | solution.py:215
  78.7 36.3 %spread.1 = (f32[2,576,576]{2,1,0:T(8,128)}, f32[8,128]{1,0:T(8,128)}) custom-call(s32[3]{0:T(128)} %pad_add_fusion.flag_ref, f32[72,12288]{1,0:T(8,128)} %get-tuple-element.12.rows_ref, f32[8,128]{1,0:T(8,128)} %get-tuple-element.13.scale_ref, f32[1,576]{1,0:T(1,128)} %damp_ref.1, f32[128,16,128]{2,1,0:T(8,128)} %get-tuple-element.14.behind), custom_call_target="tpu_custom_call" | custom-call | flops 44999999488 | bytes 1000000 | tf_op jit(solution)/shard_map/spread/pallas_call | solution.py:466
  115.0 0.0 all-to-all-done.1.in_ref
  115.0 0.0 copy-start
  115.0 1.0 copy-done
  116.0 2.8 %finish.1 = (f32[72,128]{1,0:T(8,128)}, f32[72,128]{1,0:T(8,128)}, f32[72,128]{1,0:T(8,128)}) custom-call(f32[128,16,128]{2,1,0:T(8,128)} %copy-done, f32[8,128]{1,0:T(8,128)} %get-tuple-element.16.behind), custom_call_target="tpu_custom_call" | custom-call | flops 3000000000 | bytes 1000000 | tf_op jit(solution)/shard_map/finish/pallas_call | solution.py:533
  (7 shorter events, 0.1 us)
Async XLA Ops:
  6.9 10.7 %copy-start.1 = (f32[1,576]{1,0:T(1,128)S(1)}, f32[1,576]{1,0:T(1,128)}, u32[]{:S(2)}) copy-start(f32[1,576]{1,0:T(1,128)} %damp_ref.1) | copy-start | bytes 6916
  6.9 56.3 %all-to-all-start = ((f32[128,56,128]{2,1,0:T(8,128)}), f32[128,56,128]{2,1,0:T(8,128)}, u32[]{:S(2)}, u32[]{:S(2)}) async-start(f32[128,56,128]{2,1,0:T(8,128)} %bitcast.12), calls=%async_computation | async-start | bytes 7340032 | tf_op jit(solution)/shard_map/all_to_all | solution.py:215
  73.3 41.7 %all-to-all-start.1 = ((f32[128,16,128]{2,1,0:T(8,128)}), f32[128,16,128]{2,1,0:T(8,128)S(1)}, u32[]{:S(2)}, u32[]{:S(2)}) async-start(f32[128,16,128]{2,1,0:T(8,128)} %get-tuple-element.14.behind), calls=%async_computation.1 | async-start | bytes 2097152 | tf_op jit(solution)/shard_map/all_to_all | solution.py:215
  115.0 1.0 copy-start

commit v4 on v3

--- a/solution.py
+++ b/solution.py
@@ -150,7 +150,7 @@
     return out
 
 
-def pack_kernel(jc, jp, rs, damp, cl, slot, out_ref, dense, found_ref, fields, kept):
+def pack_kernel(jc, jp, rs, damp, cl, slot, first, second, dense, found_ref, fields, kept):
     step = pl.program_id(0)
 
     @pl.when(step == 0)
@@ -158,13 +158,10 @@
         points_part(jc, jp, rs, damp, cl, slot, dense, found_ref, fields)
 
     for part in range(PAIRS):
-        pack_pair(step * PAIRS + part, part, out_ref, dense, found_ref, kept)
-
-
-def pack_pair(pair, part, out_ref, dense, found_ref, kept):
-    lane = iota((NROW, PTS), 1)
-    zero = jnp.zeros((NROW, PTS), F32)
-    flat = out_ref.reshape(NROW * 2 * PAIRS * SENT, PTS)
+        pack_pair(step * PAIRS + part, part, first, second, dense, found_ref, kept)
+
+
+def pack_pair(pair, part, first, second, dense, found_ref, kept):
     for ec in range(2):
         found = lanes_of(found_ref[ec, pl.ds(pair, 1), :], NROW)
         pick = jnp.minimum(found, PTS - 1)
@@ -177,20 +174,27 @@
             else:
                 kept[2 * part + ec, f] = jnp.take_along_axis(dense[f, ec], pick, axis=1)
         mine = [lanes_of(kept[2 * part + ec, f, pl.ds(pair, 1), :], NROW) for f in range(29)]
-        rows = side[0][0:16] + side[1][0:16] + mine[0:16]
-        rows += [side[0][16], side[1][16], mine[16], side[0][23], side[1][23]]
-        rows.append(jnp.where(found < PTS, mine[23], -1.0))
-        rows += mine[24:26]
-        extra = []
+        middle = []
         for e in range(2):
             same = jnp.where(iota((NROW, PTS), 0) == pair, float(e == ec), 0.0)
-            extra += mixed(side[e], mine, same)
-        extra += mine[26:29]
-        for at, row in enumerate(rows):
-            v, x = at // 16, at % 16
-            rest = pltpu.roll(extra[x], 96 - 32 * v, 1) if v < 3 and x < 11 else zero
-            at = SENT * (2 * part + ec) + at
-            flat[pl.ds(at, NROW, stride=2 * PAIRS * SENT), :] = jnp.where(lane < CAP, row, rest)
+            middle.append(mixed(side[e], mine, same))
+        slot = jnp.where(found < PTS, mine[23], -1.0)
+        extra = [side[0][16], mine[16]] + middle[0] + [side[0][23], slot]
+        store(first, 2 * part + ec, side[0][0:16] + mine[0:16], extra)
+        rows = side[1][0:17] + [side[1][23]] + mine[24:29] + middle[1][0:1]
+        store(second, 2 * part + ec, rows, middle[1][1:4])
+
+
+def store(out_ref, at, rows, extra):
+    lane = iota((NROW, PTS), 1)
+    zero = jnp.zeros((NROW, PTS), F32)
+    sent = len(rows)
+    flat = out_ref.reshape(NROW * 2 * PAIRS * sent, PTS)
+    for r, row in enumerate(rows):
+        v, x = r // 8, r % 8
+        rest = pltpu.roll(extra[x], 96 - 32 * v, 1) if v < 3 and x < len(extra) else zero
+        value = jnp.where(lane < CAP, row, rest)
+        flat[pl.ds(sent * at + r, NROW, stride=2 * PAIRS * sent), :] = value
 
 
 def pack(*args):
@@ -198,8 +202,10 @@
         pack_kernel,
         grid=(NROW // PAIRS,),
         in_specs=[whole(*a.shape) for a in args],
-        out_specs=pl.BlockSpec((NROW, 2 * PAIRS, SENT, PTS), lambda g: (0, g, 0, 0)),
-        out_shape=jax.ShapeDtypeStruct((NROW, NCL, SENT, PTS), F32),
+        out_specs=[
+            pl.BlockSpec((NROW, 2 * PAIRS, n, PTS), lambda g: (0, g, 0, 0)) for n in (FIRST, SECOND)
+        ],
+        out_shape=[jax.ShapeDtypeStruct((NROW, NCL, n, PTS), F32) for n in (FIRST, SECOND)],
         scratch_shapes=[
             pltpu.VMEM((29, 2, NROW, PTS), F32),
             pltpu.VMEM((2, NROW, PTS), jnp.int32),
@@ -215,18 +221,18 @@
     return lax.all_to_all(value, AXES, split_axis=0, concat_axis=0, tiled=True)
 
 
-ROWS = 72
-SENT = 56
+FIRST, SECOND = 32, 24
 
 
 def lay(in_ref, rows_ref):
-    lane = iota((16, PTS), 1)
-    full = iota((ROWS, PTS), 1)
+    lane = iota((8, PTS), 1)
+    full = iota(rows_ref.shape[0:1] + (PTS,), 1)
     for quarter in range(SRC // 4):
         pieces = []
         for s in range(4):
             block = in_ref[quarter * 4 + s]
-            part = [pltpu.roll(block[16 * v : 16 * v + 16], 32 + 32 * v, 1) for v in range(3)]
+            part = [block[8 * v : 8 * v + 8] for v in range(3)]
+            part = [pltpu.roll(p, 32 + 32 * v, 1) for v, p in enumerate(part)]
             rest = jnp.where(lane < 32, part[0], jnp.where(lane < 64, part[1], part[2]))
             pieces.append(jnp.concatenate([block, rest], axis=0))
         r1, r2 = pltpu.roll(pieces[1], 96, 1), pltpu.roll(pieces[2], 64, 1)
@@ -237,31 +243,30 @@
         rows_ref[:, base + 256 : base + 384] = jnp.where(full < 32, r2, r3)
 
 
-def jacobian(rows_ref, which):
-    at = 16 * which
+def jacobian(rows_ref, at, last):
     first = iota((8, LANES), 0) == 0
     a1 = jnp.where(first, 0.0, rows_ref[at + 8 : at + 16])
-    return rows_ref[at : at + 8], a1, rows_ref[at + 8 : at + 9], rows_ref[48 + which : 49 + which]
-
-
-def cg_kernel(
-    flag_ref, in_ref, damp_ref, rows_ref, out_ref, scale_ref, keep, hits, sums, image, largest
-):
+    return rows_ref[at : at + 8], a1, rows_ref[at + 8 : at + 9], rows_ref[last : last + 1]
+
+
+def side_of(e, one, two):
+    if e:
+        return jacobian(two, 0, 16), [two[23 + n : 24 + n] for n in range(4)], two[17:18]
+    return jacobian(one, 0, 32), [one[34 + n : 35 + n] for n in range(4)], one[38:39]
+
+
+def cg_kernel(flag_ref, one, in_ref, damp_ref, two, out_ref, keep1, keep2, hits, sums, image):
     step = pl.program_id(0)
     steps = pl.num_programs(0)
 
     @pl.when(step == 0)
     def _():
         sums[...] = jnp.zeros_like(sums)
-        largest[...] = jnp.zeros_like(largest)
-
-    lay(in_ref, rows_ref)
-    top = [jnp.max(jnp.abs(rows_ref[8 * v : 8 * v + 8]), axis=0, keepdims=True) for v in range(6)]
-    top.append(jnp.max(jnp.abs(rows_ref[48:51]), axis=0, keepdims=True))
-    largest[...] = jnp.maximum(largest[...], functools.reduce(jnp.maximum, top))
-    a0, a1, l0, l1 = jacobian(rows_ref, 2)
-    q0, q1 = rows_ref[54:55], rows_ref[55:56]
-    m0, m1, m2 = rows_ref[64:65], rows_ref[65:66], rows_ref[66:67]
+
+    lay(in_ref, two)
+    a0, a1, l0, l1 = jacobian(one, 16, 33)
+    q0, q1 = two[18:19], two[19:20]
+    m0, m1, m2 = two[20:21], two[21:22], two[22:23]
     terms = [
         a0 * lanes_of(q0, 8) + a1 * lanes_of(q1, 8),
         a0 * a0 * lanes_of(m0, 8) + a0 * a1 * lanes_of(m1, 8) + a1 * a1 * lanes_of(m2, 8),
@@ -269,10 +274,10 @@
         l0 * l0 * m0 + l0 * l1 * m1 + l1 * l1 * m2,
         jnp.zeros((14, LANES), F32),
     ]
-    slot = rows_ref[53:54].astype(jnp.int32)
-    hit = hot(slot, 128)
+    hit = hot(one[39:40].astype(jnp.int32), 128)
     hits[step] = hit
-    keep[step] = rows_ref[...]
+    keep1[step] = one[...]
+    keep2[step] = two[...]
     sums[...] += lax.dot_general(
         three(jnp.concatenate(terms, axis=0)), hit, NT, preferred_element_type=F32
     )
@@ -286,23 +291,20 @@
         x = three(jnp.concatenate([x8, x9, jnp.zeros((7, 128), F32)], axis=0))
         image[...] = jnp.zeros_like(image)
 
-        @pl.loop(0, steps, unroll=4)
-        def _(at):
-            rows = keep.at[at]
+        for at in range(NDEV // SRC):
+            rows1, rows2 = keep1.at[at], keep2.at[at]
             got = jnp.dot(x, hits[at], preferred_element_type=F32)
             got = got[0:16] + got[16:32] + got[32:48]
-            a0, a1, l0, l1 = jacobian(rows, 2)
+            a0, a1, l0, l1 = jacobian(rows1, 16, 33)
             v0 = jnp.sum(a0 * got[0:8], axis=0, keepdims=True) + l0 * got[8:9]
             v1 = jnp.sum(a1 * got[0:8], axis=0, keepdims=True) + l1 * got[8:9]
             for e in range(2):
-                m = [rows[56 + 4 * e + n : 57 + 4 * e + n] for n in range(4)]
+                (a0, a1, l0, l1), m, slot = side_of(e, rows1, rows2)
                 z0, z1 = m[0] * v0 + m[1] * v1, m[2] * v0 + m[3] * v1
-                a0, a1, l0, l1 = jacobian(rows, e)
                 out8 = a0 * lanes_of(z0, 8) + a1 * lanes_of(z1, 8)
                 terms = [out8, l0 * z0 + l1 * z1, jnp.zeros((7, LANES), F32)]
-                slot = rows[51 + e : 52 + e].astype(jnp.int32)
-                slot = jnp.where(slot >= 0, slot + CAM * e, -1)
-                hit = hot(slot, 128)
+                slot = slot.astype(jnp.int32)
+                hit = hot(jnp.where(slot >= 0, slot + CAM * e, -1), 128)
                 image[...] += lax.dot_general(
                     three(jnp.concatenate(terms, axis=0)), hit, NT, preferred_element_type=F32
                 )
@@ -316,56 +318,51 @@
         part = sums[pl.ds(3 * flag_ref[2], 3), :]
         block = jnp.concatenate([y[0:9], part, jnp.zeros((4, 128), F32)], axis=0)
         out_ref[...] = jnp.broadcast_to(block[None], (NDEV, 16, 128))
-        top = jnp.maximum(jnp.max(largest[...], keepdims=True), 1e-15)
-        scale = jnp.broadcast_to(32768.0 / (top * top), (8, 128))
-        scale_ref[...] = jnp.where(iota((8, 128), 0) == 1, 1.0 / scale, scale)
-
-
-def cg_part(flags, incoming, damp):
+
+def cg_part(flags, one, incoming, damp):
     steps = NDEV // SRC
     return pl.pallas_call(
         cg_kernel,
         grid=(steps,),
         in_specs=[
             pl.BlockSpec(memory_space=pltpu.SMEM),
-            pl.BlockSpec((SRC, SENT, PTS), lambda s: (s, 0, 0)),
+            pl.BlockSpec(((FIRST + 8), LANES), lambda s: (0, s)),
+            pl.BlockSpec((SRC, SECOND, PTS), lambda s: (s, 0, 0)),
             whole(24, 128),
         ],
         out_specs=[
-            pl.BlockSpec((ROWS, LANES), lambda s: (0, s)),
+            pl.BlockSpec(((SECOND + 8), LANES), lambda s: (0, s)),
             whole(NDEV, 16, 128),
-            whole(8, 128),
         ],
         out_shape=[
-            jax.ShapeDtypeStruct((ROWS, steps * LANES), F32),
+            jax.ShapeDtypeStruct(((SECOND + 8), steps * LANES), F32),
             jax.ShapeDtypeStruct((NDEV, 16, 128), F32),
-            jax.ShapeDtypeStruct((8, 128), F32),
         ],
         scratch_shapes=[
-            pltpu.VMEM((steps, ROWS, LANES), F32),
+            pltpu.VMEM((steps, (FIRST + 8), LANES), F32),
+            pltpu.VMEM((steps, (SECOND + 8), LANES), F32),
             pltpu.VMEM((steps, 128, LANES), BF),
             pltpu.VMEM((96, 128), F32),
             pltpu.VMEM((48, 128), F32),
-            pltpu.VMEM((1, LANES), F32),
         ],
         name="cg",
         **settings(6, 60),
-    )(flags, incoming, damp)
-
-
-def add_products(e, rows_ref, scale_ref, prod, acc):
-    scale = scale_ref[0:1, 0:1]
-
+    )(flags, one, incoming, damp)
+
+
+SCALE = 2048.0
+
+
+def add_products(e, one, two, prod, acc):
     def split(value):
         high = value.astype(BF).astype(F32)
         return high, value - high
 
-    a0, a1, last0, last1 = jacobian(rows_ref, e)
-    cam0, cam1, cam_last0, cam_last1 = jacobian(rows_ref, 2)
+    (a0, a1, last0, last1), middle, slot_a = side_of(e, one, two)
+    cam0, cam1, cam_last0, cam_last1 = jacobian(one, 16, 33)
     t, t_last = [], []
     for m in range(2):
-        at = 56 + 4 * e + 2 * m
-        m0, m1 = rows_ref[at : at + 1] * scale, rows_ref[at + 1 : at + 2] * scale
+        m0, m1 = middle[2 * m] * SCALE, middle[2 * m + 1] * SCALE
         t.append(lanes_of(m0, 8) * cam0 + lanes_of(m1, 8) * cam1)
         t_last.append(m0 * cam_last0 + m1 * cam_last1)
     for j in range(9):
@@ -377,8 +374,7 @@
         high, low = split(last0 * t0 + last1 * t1)
         prod[0, j, 8:9] = high
         prod[1, j, 8:9] = low
-    slot_a = rows_ref[51 + e : 52 + e].astype(jnp.int32)
-    slot_c = rows_ref[53:54].astype(jnp.int32)
+    slot_a, slot_c = slot_a.astype(jnp.int32), one[39:40].astype(jnp.int32)
     both = jnp.minimum(slot_a, slot_c) >= 0
     code = jnp.where(both, (slot_a >> 4) * CAM + slot_c, -1)
     onehot = hot(code, 256)
@@ -395,10 +391,10 @@
         low = jnp.concatenate(parts[1], axis=0).astype(F8)
         got = lax.dot_general(high, onehot, NT, preferred_element_type=F32)
         rest = lax.dot_general(low, onehot8, NT, preferred_element_type=F32)
-        acc[e, g * n : (g + 1) * n, :] += got + rest
-
-
-def assemble(e, read, undo, flag, damp_ref, out_ref, stage, wide_ref):
+        acc[g * n : (g + 1) * n, :] += got + rest
+
+
+def assemble(read, flag, damp_ref, out_ref, stage, wide_ref):
     source = iota((640, 640), 0)
     place = iota((640, 640), 1) == 9 * (source % CAM) + source // CAM
     place = (place & (source < TILE)).astype(F32).astype(BF)
@@ -416,7 +412,7 @@
                     odd = pltpu.roll(odd, 64, 1)
                 even = jnp.where(lane < CAM, even, odd)
             tiles.append(even)
-        full = jnp.concatenate(tiles, axis=1) * undo
+        full = jnp.concatenate(tiles, axis=1) * (1.0 / SCALE)
         high = full.astype(BF)
         wide_ref[144 * u : 144 * u + 144] = high
         wide_ref[TILE + 144 * u : TILE + 144 * u + 144] = (full - high.astype(F32)).astype(BF)
@@ -431,62 +427,75 @@
     for tile in range(5):
         wide = min(128, TILE - 128 * tile)
         block = stage[TILE * tile : TILE * tile + TILE, 0:wide]
-        out_ref[e, :, 128 * tile : 128 * tile + wide] = block
+        out_ref[0, :, 128 * tile : 128 * tile + wide] = block
 
     @pl.when(flag == 1)
     def _():
         same = iota((TILE, TILE), 0) == iota((TILE, TILE), 1)
-        out_ref[e] += jnp.where(same, jnp.broadcast_to(damp_ref[...], (TILE, TILE)), 0.0)
-
-
-def spread_kernel(
-    flag_ref, rows_ref, scale_ref, damp_ref, behind, out_ref, token, prod, acc, stage, wide_ref
-):
+        out_ref[0] += jnp.where(same, jnp.broadcast_to(damp_ref[...], (TILE, TILE)), 0.0)
+
+
+def spread_kernel(e, flag_ref, damp_ref, *refs):
+    if e:
+        one, two, out_ref, token, prod, acc, stage, wide_ref = refs[0], refs[1], *refs[4:]
+    else:
+        in_ref, out_ref, one, prod, acc, stage, wide_ref = refs
     step = pl.program_id(0)
 
     @pl.when(step == 0)
     def _():
         acc[...] = jnp.zeros_like(acc)
 
-    for e in range(2):
-        add_products(e, rows_ref, scale_ref, prod, acc)
+    if e:
+        add_products(1, one, two, prod, acc)
+    else:
+        lay(in_ref, one)
+        add_products(0, one, None, prod, acc)
 
     @pl.when(step == pl.num_programs(0) - 1)
     def _():
-        for e in range(2):
-
-            def read(j, base):
-                return acc[e, 144 * j : 144 * j + 144, base : base + 128]
-
-            assemble(e, read, scale_ref[1:2, 0:1], flag_ref[e], damp_ref, out_ref, stage, wide_ref)
-        token[...] = jnp.zeros_like(token)
-
-
-def spread(flags, rows, scale, damp, behind):
+        def read(j, base):
+            return acc[144 * j : 144 * j + 144, base : base + 128]
+
+        assemble(read, flag_ref[e], damp_ref, out_ref, stage, wide_ref)
+        if e:
+            token[...] = jnp.zeros_like(token)
+
+
+def spread(e, flags, damp, args):
+    steps = NDEV // SRC
+    in_specs = [pl.BlockSpec(memory_space=pltpu.SMEM), whole(1, TILE)]
+    tile_spec = pl.BlockSpec((1, TILE, TILE), lambda s: (e, 0, 0))
+    tile_shape = jax.ShapeDtypeStruct((2, TILE, TILE), F32)
+    if e:
+        in_specs += [
+            pl.BlockSpec(((FIRST + 8), LANES), lambda s: (0, s)),
+            pl.BlockSpec(((SECOND + 8), LANES), lambda s: (0, s)),
+            ANY,
+            ANY,
+        ]
+        out_specs = [tile_spec, whole(8, 128)]
+        out_shape = [tile_shape, jax.ShapeDtypeStruct((8, 128), F32)]
+    else:
+        in_specs.append(pl.BlockSpec((SRC, FIRST, PTS), lambda s: (s, 0, 0)))
+        out_specs = [tile_spec, pl.BlockSpec(((FIRST + 8), LANES), lambda s: (0, s))]
+        out_shape = [tile_shape, jax.ShapeDtypeStruct(((FIRST + 8), steps * LANES), F32)]
     return pl.pallas_call(
-        spread_kernel,
-        grid=(NDEV // SRC,),
-        in_specs=[
-            pl.BlockSpec(memory_space=pltpu.SMEM),
-            pl.BlockSpec((ROWS, LANES), lambda s: (0, s)),
-            whole(8, 128),
-            whole(1, TILE),
-            ANY,
-        ],
-        out_specs=[whole(2, TILE, TILE), whole(8, 128)],
-        out_shape=[
-            jax.ShapeDtypeStruct((2, TILE, TILE), F32),
-            jax.ShapeDtypeStruct((8, 128), F32),
-        ],
+        functools.partial(spread_kernel, e),
+        grid=(steps,),
+        in_specs=in_specs,
+        out_specs=out_specs,
+        out_shape=out_shape,
         scratch_shapes=[
             pltpu.VMEM((2, 9, 16, LANES), F32),
-            pltpu.VMEM((2, 1296, 256), F32),
+            pltpu.VMEM((1296, 256), F32),
             pltpu.VMEM((5 * TILE, 128), F32),
             pltpu.VMEM((2 * TILE, 640), BF),
         ],
+        input_output_aliases={4: 0} if e else {},
         name="spread",
-        **settings(45, 60),
-    )(flags, rows, scale, damp, behind)
+        **settings(20, 60),
+    )(flags, damp, *args)
 
 
 def finish_kernel(in_ref, behind, step_ref, res_ref, dir_ref):
@@ -549,14 +558,16 @@
     damp = jnp.pad(cam_damp.reshape(CAM, 9).T, ((0, 0), (0, 128 - CAM)), constant_values=1.0)
     zeros = jnp.zeros((8, 128), F32)
     damp = jnp.concatenate([zeros, damp[0:8], zeros[0:1], damp[8:9], zeros[0:6]], axis=0)
-    packed = pack(
+    first, second = pack(
         jac_cam.transpose(1, 0, 2), jac_pt.transpose(1, 0, 2), resid, point_damp, obs_cluster.T,
         obs_slot,
     )
-    incoming = exchange(packed.reshape(NDEV, SENT, PTS))
-    rows, share, scale = cg_part(flags, incoming, damp)
+    first = exchange(first.reshape(NDEV, FIRST, PTS))
+    second = exchange(second.reshape(NDEV, SECOND, PTS))
+    tiles, one = spread(0, flags, cam_damp, (first,))
+    two, share = cg_part(flags, one, second, damp)
     shares = exchange(share)
-    tiles, token = spread(flags, rows, scale, cam_damp, share)
+    tiles, token = spread(1, flags, cam_damp, (one, two, tiles, share))
     step, residual, direction = finish(shares, token)
     return (tiles[:, None], step.reshape(-1), residual.reshape(-1), direction.reshape(-1))
 

time: 120 us -> 115 us (0.958)
  waiting for transfers between devices: 42.9 us -> 29.4 us
  starting transfers between devices: 16.1 us -> 23.3 us
    all_to_all x2 -> x3, waiting for transfers between devices: 42.9 us -> 29.4 us  [exchange(): return lax.all_to_all(value, AXES, split_axis=0, concat_axis=0, tiled=True)]
    all_to_all x2 -> x3, starting transfers between devices: 16.1 us -> 23.3 us  [exchange(): return lax.all_to_all(value, AXES, split_axis=0, concat_axis=0, tiled=True)]
    pallas_call x1 -> x2, Pallas kernels: 36.3 us -> 39.2 us  [spread(): pl.pallas_call(functools.partial(spread_kernel, e), grid=(steps,), in_spe...]
    pallas_call x1, Pallas kernels: 10.1 us -> 8.43 us  [cg_part(): pl.pallas_call(cg_kernel, grid=(steps,), in_specs=[pl.BlockSpec(memory_sp...]
  transfers between devices with their start and end apart: 2 -> 3, of which waited for: 1 -> 2; matrix products, arithmetic and copies ran while one was open for 2% -> 2% of each run, Pallas kernels for 31% -> 35%
where the time goes in v4:
time: 115 us; the launch traced here: 114 us
  Pallas kernels  56.6 us (49%)
  waiting for transfers between devices  29.4 us (26%)
  starting transfers between devices  23.3 us (20%)
  local copies, waits for them, and re-layouts  3 us (3%)
    pallas_call x2, Pallas kernels, spread(): pl.pallas_call(functools.partial(spread_kernel, e), grid=(steps,), in_spe...  39.2 us
    all_to_all x3, waiting for transfers between devices, exchange(): return lax.all_to_all(value, AXES, split_axis=0, concat_axis=0, tiled=True)  29.4 us
    all_to_all x3, starting transfers between devices, exchange(): return lax.all_to_all(value, AXES, split_axis=0, concat_axis=0, tiled=True)  23.3 us
    pallas_call x1, Pallas kernels, cg_part(): pl.pallas_call(cg_kernel, grid=(steps,), in_specs=[pl.BlockSpec(memory_sp...  8.43 us
    pallas_call x1, Pallas kernels, pack(): pl.pallas_call(pack_kernel, grid=(NROW // PAIRS,), in_specs=[whole(*a.sha...  6.14 us
    pallas_call x1, Pallas kernels, finish(): pl.pallas_call(finish_kernel, grid=(1,), in_specs=[whole(NDEV, 16, 128),...  2.79 us
  transfers between devices with their start and end apart: 3, of which 2 were waited for; matrix products, arithmetic and copies ran while one was open for 2% of the time, Pallas kernels for 35%

profile of v4, /device:TPU:24, one launch (start us, length us, event | category | flops | bytes accessed | tf_op | source)
XLA Modules:
  0.0 113.6 jit_solution(7574765361037846170)
XLA Ops:
  0.6 6.1 %pack.1 = (f32[8,16,32,128]{3,2,1,0:T(8,128)}, f32[8,16,24,128]{3,2,1,0:T(8,128)}) custom-call(f32[18,8,128]{2,1,0:T(8,128)} %bitcast.17, f32[6,8,128]{2,1,0:T(8,128)} %bitcast.18, f32[8,2,128]{2,1,0:T(2,128)} %rs.1, f32[3,128]{1,0:T(4,128)} %damp.1, s32[8,128]{1,0:T(8,128)} %bitcast.19, s32[8,128]{1,0:T(8,128)} %slot.1), custom_call_target="tpu_custom_call" | custom-call | flops 8000000000 | bytes 1000000 | tf_op jit(solution)/shard_map/pack/pallas_call | solution.py:201
  6.8 0.0 copy-start.2
  6.8 10.3 %all-to-all-start = ((f32[128,32,128]{2,1,0:T(8,128)}), f32[128,32,128]{2,1,0:T(8,128)S(1)}, u32[]{:S(2)}, u32[]{:S(2)}) async-start(f32[128,32,128]{2,1,0:T(8,128)} %bitcast.13), calls=%async_computation | async-start | bytes 4194304 | tf_op jit(solution)/shard_map/all_to_all | solution.py:221
  17.1 0.0 copy-done.2
  17.1 0.1 reshape.28
  17.2 0.1 copy.13
  17.4 1.8 %concatenate.7.damp_ref = f32[24,128]{1,0:T(8,128)} concatenate(f32[8,128]{1,0:T(8,128)S(1)} %broadcast_in_dim.10, f32[8,128]{1,0:T(8,128)S(1)} %pad_slice_fusion.1, f32[1,128]{1,0:T(1,128)S(1)} %slice.13, f32[1,128]{1,0:T(1,128)S(1)} %pad_slice_fusion, f32[6,128]{1,0:T(8,128)S(1)} %slice.15), dimensions={0} | concatenate | bytes 24576 | tf_op jit(solution)/shard_map/concatenate | solution.py:560
  19.2 0.6 pad_add_fusion.flag_ref
  19.7 26.3 %all-to-all-done.refs_0_ = f32[128,32,128]{2,1,0:T(8,128)S(1)} async-done(((f32[128,32,128]{2,1,0:T(8,128)}), f32[128,32,128]{2,1,0:T(8,128)S(1)}, u32[]{:S(2)}, u32[]{:S(2)}) %all-to-all-start) | async-done | bytes 2097184 | tf_op jit(solution)/shard_map/all_to_all | solution.py:221
  46.1 0.0 copy-start
  46.1 6.3 %all-to-all-start.1 = ((f32[128,24,128]{2,1,0:T(8,128)}), f32[128,24,128]{2,1,0:T(8,128)}, u32[]{:S(2)}, u32[]{:S(2)}) async-start(f32[128,24,128]{2,1,0:T(8,128)} %bitcast.14), calls=%async_computation.1 | async-start | bytes 3145728 | tf_op jit(solution)/shard_map/all_to_all | solution.py:221
  52.4 0.0 copy-done
  52.5 20.1 %spread.2 = (f32[2,576,576]{2,1,0:T(8,128)}, f32[40,12288]{1,0:T(8,128)}) custom-call(s32[3]{0:T(128)} %pad_add_fusion.flag_ref, f32[1,576]{1,0:T(1,128)} %damp_ref.3, f32[128,32,128]{2,1,0:T(8,128)} %copy-done), custom_call_target="tpu_custom_call" | custom-call | flops 20000000000 | bytes 1000000 | tf_op jit(solution)/shard_map/spread/pallas_call | solution.py:483
  72.5 3.1 %all-to-all-done.1.in_ref = f32[128,24,128]{2,1,0:T(8,128)} async-done(((f32[128,24,128]{2,1,0:T(8,128)}), f32[128,24,128]{2,1,0:T(8,128)}, u32[]{:S(2)}, u32[]{:S(2)}) %all-to-all-start.1) | async-done | bytes 1572896 | tf_op jit(solution)/shard_map/all_to_all | solution.py:221
  75.6 8.4 %cg.1 = (f32[32,12288]{1,0:T(8,128)}, f32[128,16,128]{2,1,0:T(8,128)}) custom-call(s32[3]{0:T(128)} %pad_add_fusion.flag_ref, f32[40,12288]{1,0:T(8,128)} %get-tuple-element.16.one.refs_0_, f32[128,24,128]{2,1,0:T(8,128)} %all-to-all-done.1.in_ref, f32[24,128]{1,0:T(8,128)} %concatenate.7.damp_ref), custom_call_target="tpu_custom_call" | custom-call | flops 6000000000 | bytes 1000000 | tf_op jit(solution)/shard_map/cg/pallas_call | solution.py:324
  84.0 6.7 %all-to-all-start.2 = ((f32[128,16,128]{2,1,0:T(8,128)}), f32[128,16,128]{2,1,0:T(8,128)S(1)}, u32[]{:S(2)}, u32[]{:S(2)}) async-start(f32[128,16,128]{2,1,0:T(8,128)} %get-tuple-element.20.refs_3_), calls=%async_computation.2 | async-start | bytes 2097152 | tf_op jit(solution)/shard_map/all_to_all | solution.py:221
  90.7 19.1 %spread.3 = (f32[2,576,576]{2,1,0:T(8,128)}, f32[8,128]{1,0:T(8,128)}) custom-call(s32[3]{0:T(128)} %pad_add_fusion.flag_ref, f32[1,576]{1,0:T(1,128)} %damp_ref.3, f32[40,12288]{1,0:T(8,128)} %get-tuple-element.16.one.refs_0_, f32[32,12288]{1,0:T(8,128)} %get-tuple-element.18.refs_1_, ...), custom_call_target="tpu_custom_call", output_to_operand_aliasing={{0}: (4, {})} | custom-call | flops 20000000000 | bytes 1000000 | tf_op jit(solution)/shard_map/spread/pallas_call | solution.py:483
  109.9 0.0 all-to-all-done.2.in_ref
  109.9 0.0 copy-start.1
  109.9 1.0 copy-done.1
  110.8 2.8 %finish.1 = (f32[72,128]{1,0:T(8,128)}, f32[72,128]{1,0:T(8,128)}, f32[72,128]{1,0:T(8,128)}) custom-call(f32[128,16,128]{2,1,0:T(8,128)} %copy-done.1, f32[8,128]{1,0:T(8,128)} %get-tuple-element.22.behind), custom_call_target="tpu_custom_call" | custom-call | flops 3000000000 | bytes 1000000 | tf_op jit(solution)/shard_map/finish/pallas_call | solution.py:542
  (7 shorter events, 0.1 us)
Async XLA Ops:
  6.8 10.3 %copy-start.2 = (f32[1,576]{1,0:T(1,128)S(1)}, f32[1,576]{1,0:T(1,128)}, u32[]{:S(2)}) copy-start(f32[1,576]{1,0:T(1,128)} %damp_ref.3) | copy-start | bytes 6916
  6.8 39.3 %all-to-all-start = ((f32[128,32,128]{2,1,0:T(8,128)}), f32[128,32,128]{2,1,0:T(8,128)S(1)}, u32[]{:S(2)}, u32[]{:S(2)}) async-start(f32[128,32,128]{2,1,0:T(8,128)} %bitcast.13), calls=%async_computation | async-start | bytes 4194304 | tf_op jit(solution)/shard_map/all_to_all | solution.py:221
  46.1 6.4 %copy-start = (f32[128,32,128]{2,1,0:T(8,128)}, f32[128,32,128]{2,1,0:T(8,128)S(1)}, u32[]{:S(2)}) copy-start(f32[128,32,128]{2,1,0:T(8,128)S(1)} %all-to-all-done.refs_0_) | copy-start | bytes 6291460
  46.1 29.5 %all-to-all-start.1 = ((f32[128,24,128]{2,1,0:T(8,128)}), f32[128,24,128]{2,1,0:T(8,128)}, u32[]{:S(2)}, u32[]{:S(2)}) async-start(f32[128,24,128]{2,1,0:T(8,128)} %bitcast.14), calls=%async_computation.1 | async-start | bytes 3145728 | tf_op jit(solution)/shard_map/all_to_all | solution.py:221
  84.0 25.8 %all-to-all-start.2 = ((f32[128,16,128]{2,1,0:T(8,128)}), f32[128,16,128]{2,1,0:T(8,128)S(1)}, u32[]{:S(2)}, u32[]{:S(2)}) async-start(f32[128,16,128]{2,1,0:T(8,128)} %get-tuple-element.20.refs_3_), calls=%async_computation.2 | async-start | bytes 2097152 | tf_op jit(solution)/shard_map/all_to_all | solution.py:221
  109.9 1.0 copy-start.1

commit v5 on v4

--- a/solution.py
+++ b/solution.py
@@ -80,11 +80,9 @@
     return jnp.where(codes == ids, jnp.ones((), BF), jnp.zeros((), BF))
 
 
-def three(value):
-    a = value.astype(BF)
-    rest = value - a.astype(F32)
-    b = rest.astype(BF)
-    return jnp.concatenate([a, b, (rest - b.astype(F32)).astype(BF)], axis=0)
+def halves(value):
+    high = value.astype(BF)
+    return jnp.concatenate([high, (value - high.astype(F32)).astype(BF)], axis=0)
 
 
 def chosen(named):
@@ -150,7 +148,27 @@
     return out
 
 
-def pack_kernel(jc, jp, rs, damp, cl, slot, first, second, dense, found_ref, fields, kept):
+def picked(dense, found_ref, pair, ec):
+    found = lanes_of(found_ref[ec, pl.ds(pair, 1), :], NROW)
+    pick = jnp.minimum(found, PTS - 1)
+    same = [jnp.where(iota((NROW, PTS), 0) == pair, float(e == ec), 0.0) for e in range(2)]
+    return found, same, lambda f, e: jnp.take_along_axis(dense[f, e], pick, axis=1)
+
+
+def in_lists(rows, extra, slots):
+    lane = iota((NROW, PTS), 1)
+    rest = [jnp.zeros((NROW, PTS), F32)] * len(rows)
+    for value, places in zip(extra, slots):
+        for v, r in enumerate(places):
+            rest[r] = pltpu.roll(value, 96 - 32 * v, 1)
+    return [jnp.where(lane < CAP, a, b) for a, b in zip(rows, rest)]
+
+
+FIRST_SLOTS = [(x, 8 + x, 16 + x) for x in range(8)] + [(24, 25, 26)]
+SECOND_SLOTS = [(x, 6 + x, 12 + x) for x in range(6)]
+
+
+def pack_first_kernel(jc, jp, rs, damp, cl, slot, out_ref, dense, found_ref, fields, kept):
     step = pl.program_id(0)
 
     @pl.when(step == 0)
@@ -158,83 +176,114 @@
         points_part(jc, jp, rs, damp, cl, slot, dense, found_ref, fields)
 
     for part in range(PAIRS):
-        pack_pair(step * PAIRS + part, part, first, second, dense, found_ref, kept)
-
-
-def pack_pair(pair, part, first, second, dense, found_ref, kept):
-    for ec in range(2):
-        found = lanes_of(found_ref[ec, pl.ds(pair, 1), :], NROW)
-        pick = jnp.minimum(found, PTS - 1)
-        side = [
-            [jnp.take_along_axis(dense[f, e], pick, axis=1) for f in range(24)] for e in range(2)
-        ]
-        for f in range(29):
-            if f < 24:
-                kept[2 * part + ec, f] = side[ec][f]
-            else:
-                kept[2 * part + ec, f] = jnp.take_along_axis(dense[f, ec], pick, axis=1)
-        mine = [lanes_of(kept[2 * part + ec, f, pl.ds(pair, 1), :], NROW) for f in range(29)]
-        middle = []
-        for e in range(2):
-            same = jnp.where(iota((NROW, PTS), 0) == pair, float(e == ec), 0.0)
-            middle.append(mixed(side[e], mine, same))
-        slot = jnp.where(found < PTS, mine[23], -1.0)
-        extra = [side[0][16], mine[16]] + middle[0] + [side[0][23], slot]
-        store(first, 2 * part + ec, side[0][0:16] + mine[0:16], extra)
-        rows = side[1][0:17] + [side[1][23]] + mine[24:29] + middle[1][0:1]
-        store(second, 2 * part + ec, rows, middle[1][1:4])
-
-
-def store(out_ref, at, rows, extra):
-    lane = iota((NROW, PTS), 1)
-    zero = jnp.zeros((NROW, PTS), F32)
-    sent = len(rows)
-    flat = out_ref.reshape(NROW * 2 * PAIRS * sent, PTS)
-    for r, row in enumerate(rows):
-        v, x = r // 8, r % 8
-        rest = pltpu.roll(extra[x], 96 - 32 * v, 1) if v < 3 and x < len(extra) else zero
-        value = jnp.where(lane < CAP, row, rest)
-        flat[pl.ds(sent * at + r, NROW, stride=2 * PAIRS * sent), :] = value
-
-
-def pack(*args):
+        pair = step * PAIRS + part
+        for ec in range(2):
+            found, same, take = picked(dense, found_ref, pair, ec)
+            side = [take(f, 0) for f in range(24)]
+            for f in range(24):
+                kept[2 * part + ec, f] = take(f, 1) if ec else side[f]
+            mine = [lanes_of(kept[2 * part + ec, f, pl.ds(pair, 1), :], NROW) for f in range(24)]
+            list_slot = jnp.where(found < PTS, mine[23], -1.0)
+            extra = [side[16], mine[16]] + mixed(side, mine, same[0]) + [side[23], list_slot]
+            extra.append(take(23, 1))
+            values = in_lists(side[0:16] + mine[0:16], extra, FIRST_SLOTS)
+            for r in range(0, FIRST, 8):
+                block = jnp.swapaxes(jnp.stack(values[r : r + 8], axis=0), 0, 1)
+                out_ref[:, 2 * part + ec, r : r + 8, :] = block
+
+
+def pack_second_kernel(dense, found_ref, out_ref, kept):
+    step = pl.program_id(0)
+    for part in range(PAIRS):
+        pair = step * PAIRS + part
+        for ec in range(2):
+            _, same, take = picked(dense, found_ref, pair, ec)
+            side = [take(f, 1) for f in range(23)]
+            for f in range(17, 29):
+                if f != 23:
+                    kept[2 * part + ec, f] = take(f, ec)
+            mine = {
+                f: lanes_of(kept[2 * part + ec, f, pl.ds(pair, 1), :], NROW)
+                for f in range(17, 29)
+                if f != 23
+            }
+            rows = side[0:17] + [mine[24], mine[25], mine[26]]
+            extra = [mine[27], mine[28]] + mixed(side, mine, same[1])
+            values = in_lists(rows, extra, SECOND_SLOTS)
+            values += values[0:4]
+            for r in range(0, SECOND, 8):
+                block = jnp.swapaxes(jnp.stack(values[r : r + 8], axis=0), 0, 1)
+                out_ref[:, 2 * part + ec, r // 4] = block[:, 0:4]
+                if r + 4 < SECOND:
+                    out_ref[:, 2 * part + ec, r // 4 + 1] = block[:, 4:8]
+
+
+def pack_first(*args):
     return pl.pallas_call(
-        pack_kernel,
+        pack_first_kernel,
         grid=(NROW // PAIRS,),
         in_specs=[whole(*a.shape) for a in args],
         out_specs=[
-            pl.BlockSpec((NROW, 2 * PAIRS, n, PTS), lambda g: (0, g, 0, 0)) for n in (FIRST, SECOND)
-        ],
-        out_shape=[jax.ShapeDtypeStruct((NROW, NCL, n, PTS), F32) for n in (FIRST, SECOND)],
+            pl.BlockSpec((NROW, 2 * PAIRS, FIRST, PTS), lambda g: (0, g, 0, 0)),
+            whole(29, 2, NROW, PTS),
+            whole(2, NROW, PTS),
+        ],
+        out_shape=[
+            jax.ShapeDtypeStruct((NROW, NCL, FIRST, PTS), F32),
+            jax.ShapeDtypeStruct((29, 2, NROW, PTS), F32),
+            jax.ShapeDtypeStruct((2, NROW, PTS), jnp.int32),
+        ],
         scratch_shapes=[
-            pltpu.VMEM((29, 2, NROW, PTS), F32),
-            pltpu.VMEM((2, NROW, PTS), jnp.int32),
             pltpu.VMEM((29, KOBS, PTS), F32),
-            pltpu.VMEM((2 * PAIRS, 29, NROW, PTS), F32),
-        ],
-        name="pack",
-        **settings(8, 60),
+            pltpu.VMEM((2 * PAIRS, 24, NROW, PTS), F32),
+        ],
+        name="pack_first",
+        **settings(5, 60),
     )(*args)
+
+
+def pack_second(dense, found):
+    return pl.pallas_call(
+        pack_second_kernel,
+        grid=(NROW // PAIRS,),
+        in_specs=[whole(29, 2, NROW, PTS), whole(2, NROW, PTS)],
+        out_specs=pl.BlockSpec(
+            (NROW, 2 * PAIRS, SECOND // 4, 4, PTS), lambda g: (0, g, 0, 0, 0)
+        ),
+        out_shape=jax.ShapeDtypeStruct((NROW, NCL, SECOND // 4, 4, PTS), F32),
+        scratch_shapes=[pltpu.VMEM((2 * PAIRS, 29, NROW, PTS), F32)],
+        name="pack_second",
+        **settings(5, 60),
+    )(dense, found)
 
 
 def exchange(value):
     return lax.all_to_all(value, AXES, split_axis=0, concat_axis=0, tiled=True)
 
 
-FIRST, SECOND = 32, 24
+FIRST, FIRST_ROWS = 32, 41
+SECOND, SECOND_ROWS = 20, 26
+
+
+def joined(a, b, c):
+    lane = iota(a.shape, 1)
+    a, b, c = pltpu.roll(a, 32, 1), pltpu.roll(b, 64, 1), pltpu.roll(c, 96, 1)
+    return jnp.where(lane < 32, a, jnp.where(lane < 64, b, c))
 
 
 def lay(in_ref, rows_ref):
-    lane = iota((8, PTS), 1)
     full = iota(rows_ref.shape[0:1] + (PTS,), 1)
     for quarter in range(SRC // 4):
         pieces = []
-        for s in range(4):
-            block = in_ref[quarter * 4 + s]
-            part = [block[8 * v : 8 * v + 8] for v in range(3)]
-            part = [pltpu.roll(p, 32 + 32 * v, 1) for v, p in enumerate(part)]
-            rest = jnp.where(lane < 32, part[0], jnp.where(lane < 64, part[1], part[2]))
-            pieces.append(jnp.concatenate([block, rest], axis=0))
+        for s in range(quarter * 4, quarter * 4 + 4):
+            if len(in_ref.shape) == 3:
+                block = in_ref[s]
+                rest = [joined(block[0:8], block[8:16], block[16:24])]
+                rest.append(joined(block[24:25], block[25:26], block[26:27]))
+            else:
+                block = jnp.concatenate([in_ref[s, k] for k in range(SECOND // 4)], axis=0)
+                rest = [joined(block[0:6], block[6:12], block[12:18])]
+            pieces.append(jnp.concatenate([block] + rest, axis=0))
         r1, r2 = pltpu.roll(pieces[1], 96, 1), pltpu.roll(pieces[2], 64, 1)
         r3 = pltpu.roll(pieces[3], 32, 1)
         base = quarter * 384
@@ -251,11 +300,11 @@
 
 def side_of(e, one, two):
     if e:
-        return jacobian(two, 0, 16), [two[23 + n : 24 + n] for n in range(4)], two[17:18]
+        return jacobian(two, 0, 16), [two[22 + n : 23 + n] for n in range(4)], one[40:41]
     return jacobian(one, 0, 32), [one[34 + n : 35 + n] for n in range(4)], one[38:39]
 
 
-def cg_kernel(flag_ref, one, in_ref, damp_ref, two, out_ref, keep1, keep2, hits, sums, image):
+def cg_kernel(flag_ref, one, in_ref, damp_ref, two, out_ref, keep1, keep2, hits, sums, image, kept):
     step = pl.program_id(0)
     steps = pl.num_programs(0)
 
@@ -265,8 +314,8 @@
 
     lay(in_ref, two)
     a0, a1, l0, l1 = jacobian(one, 16, 33)
-    q0, q1 = two[18:19], two[19:20]
-    m0, m1, m2 = two[20:21], two[21:22], two[22:23]
+    q0, q1 = two[17:18], two[18:19]
+    m0, m1, m2 = two[19:20], two[20:21], two[21:22]
     terms = [
         a0 * lanes_of(q0, 8) + a1 * lanes_of(q1, 8),
         a0 * a0 * lanes_of(m0, 8) + a0 * a1 * lanes_of(m1, 8) + a1 * a1 * lanes_of(m2, 8),
@@ -274,27 +323,27 @@
         l0 * l0 * m0 + l0 * l1 * m1 + l1 * l1 * m2,
         jnp.zeros((14, LANES), F32),
     ]
-    hit = hot(one[39:40].astype(jnp.int32), 128)
+    hit = hot(one[39:40].astype(jnp.int32), CAM)
     hits[step] = hit
     keep1[step] = one[...]
     keep2[step] = two[...]
     sums[...] += lax.dot_general(
-        three(jnp.concatenate(terms, axis=0)), hit, NT, preferred_element_type=F32
+        halves(jnp.concatenate(terms, axis=0)), hit, NT, preferred_element_type=F32
     )
 
     @pl.when(step == steps - 1)
     def _():
         damp = damp_ref[...]
-        total = sums[0:24] + sums[32:56] + sums[64:88] + damp
-        sums[0:24] = total
+        total = sums[0:24] + sums[32:56] + damp
+        kept[...] = jnp.concatenate([total, jnp.zeros_like(total)], axis=1)
         x8, x9 = total[0:8] / total[8:16], total[16:17] / total[17:18]
-        x = three(jnp.concatenate([x8, x9, jnp.zeros((7, 128), F32)], axis=0))
+        x = halves(jnp.concatenate([x8, x9, jnp.zeros((7, CAM), F32)], axis=0))
         image[...] = jnp.zeros_like(image)
 
         for at in range(NDEV // SRC):
             rows1, rows2 = keep1.at[at], keep2.at[at]
             got = jnp.dot(x, hits[at], preferred_element_type=F32)
-            got = got[0:16] + got[16:32] + got[32:48]
+            got = got[0:16] + got[16:32]
             a0, a1, l0, l1 = jacobian(rows1, 16, 33)
             v0 = jnp.sum(a0 * got[0:8], axis=0, keepdims=True) + l0 * got[8:9]
             v1 = jnp.sum(a1 * got[0:8], axis=0, keepdims=True) + l1 * got[8:9]
@@ -303,19 +352,20 @@
                 z0, z1 = m[0] * v0 + m[1] * v1, m[2] * v0 + m[3] * v1
                 out8 = a0 * lanes_of(z0, 8) + a1 * lanes_of(z1, 8)
                 terms = [out8, l0 * z0 + l1 * z1, jnp.zeros((7, LANES), F32)]
-                slot = slot.astype(jnp.int32)
-                hit = hot(jnp.where(slot >= 0, slot + CAM * e, -1), 128)
-                image[...] += lax.dot_general(
-                    three(jnp.concatenate(terms, axis=0)), hit, NT, preferred_element_type=F32
+                image[e] += lax.dot_general(
+                    halves(jnp.concatenate(terms, axis=0)),
+                    hot(slot.astype(jnp.int32), CAM),
+                    NT,
+                    preferred_element_type=F32,
                 )
 
-        y = image[0:16] + image[16:32] + image[32:48]
-        own = iota((16, 128), 1) < CAM
-        extra = jnp.concatenate([damp[8:16] * x8, damp[17:18] * x9, jnp.zeros((7, 128), F32)], axis=0)
-        extra = jnp.where(own, extra, 0.0)
-        y += jnp.where(flag_ref[0] == 1, extra, 0.0)
-        y += jnp.where(flag_ref[1] == 1, pltpu.roll(extra, CAM, 1), 0.0)
-        part = sums[pl.ds(3 * flag_ref[2], 3), :]
+        extra = jnp.concatenate([damp[8:16] * x8, damp[17:18] * x9, jnp.zeros((7, CAM), F32)], axis=0)
+        y = [
+            image[e, 0:16] + image[e, 16:32] + jnp.where(flag_ref[e] == 1, extra, 0.0)
+            for e in range(2)
+        ]
+        y = jnp.concatenate(y, axis=1)
+        part = kept[pl.ds(3 * flag_ref[2], 3), :]
         block = jnp.concatenate([y[0:9], part, jnp.zeros((4, 128), F32)], axis=0)
         out_ref[...] = jnp.broadcast_to(block[None], (NDEV, 16, 128))
 
@@ -326,27 +376,28 @@
         grid=(steps,),
         in_specs=[
             pl.BlockSpec(memory_space=pltpu.SMEM),
-            pl.BlockSpec(((FIRST + 8), LANES), lambda s: (0, s)),
-            pl.BlockSpec((SRC, SECOND, PTS), lambda s: (s, 0, 0)),
-            whole(24, 128),
+            pl.BlockSpec((FIRST_ROWS, LANES), lambda s: (0, s)),
+            pl.BlockSpec((SRC, SECOND // 4, 4, PTS), lambda s: (s, 0, 0, 0)),
+            whole(24, CAM),
         ],
         out_specs=[
-            pl.BlockSpec(((SECOND + 8), LANES), lambda s: (0, s)),
+            pl.BlockSpec((SECOND_ROWS, LANES), lambda s: (0, s)),
             whole(NDEV, 16, 128),
         ],
         out_shape=[
-            jax.ShapeDtypeStruct(((SECOND + 8), steps * LANES), F32),
+            jax.ShapeDtypeStruct((SECOND_ROWS, steps * LANES), F32),
             jax.ShapeDtypeStruct((NDEV, 16, 128), F32),
         ],
         scratch_shapes=[
-            pltpu.VMEM((steps, (FIRST + 8), LANES), F32),
-            pltpu.VMEM((steps, (SECOND + 8), LANES), F32),
-            pltpu.VMEM((steps, 128, LANES), BF),
-            pltpu.VMEM((96, 128), F32),
-            pltpu.VMEM((48, 128), F32),
+            pltpu.VMEM((steps, FIRST_ROWS, LANES), F32),
+            pltpu.VMEM((steps, SECOND_ROWS, LANES), F32),
+            pltpu.VMEM((steps, CAM, LANES), BF),
+            pltpu.VMEM((64, CAM), F32),
+            pltpu.VMEM((2, 32, CAM), F32),
+            pltpu.VMEM((24, 128), F32),
         ],
         name="cg",
-        **settings(6, 60),
+        **settings(6, 63),
     )(flags, one, incoming, damp)
 
 
@@ -469,8 +520,8 @@
     tile_shape = jax.ShapeDtypeStruct((2, TILE, TILE), F32)
     if e:
         in_specs += [
-            pl.BlockSpec(((FIRST + 8), LANES), lambda s: (0, s)),
-            pl.BlockSpec(((SECOND + 8), LANES), lambda s: (0, s)),
+            pl.BlockSpec((FIRST_ROWS, LANES), lambda s: (0, s)),
+            pl.BlockSpec((SECOND_ROWS, LANES), lambda s: (0, s)),
             ANY,
             ANY,
         ]
@@ -478,8 +529,8 @@
         out_shape = [tile_shape, jax.ShapeDtypeStruct((8, 128), F32)]
     else:
         in_specs.append(pl.BlockSpec((SRC, FIRST, PTS), lambda s: (s, 0, 0)))
-        out_specs = [tile_spec, pl.BlockSpec(((FIRST + 8), LANES), lambda s: (0, s))]
-        out_shape = [tile_shape, jax.ShapeDtypeStruct(((FIRST + 8), steps * LANES), F32)]
+        out_specs = [tile_spec, pl.BlockSpec((FIRST_ROWS, LANES), lambda s: (0, s))]
+        out_shape = [tile_shape, jax.ShapeDtypeStruct((FIRST_ROWS, steps * LANES), F32)]
     return pl.pallas_call(
         functools.partial(spread_kernel, e),
         grid=(steps,),
@@ -498,55 +549,61 @@
     )(flags, damp, *args)
 
 
-def finish_kernel(in_ref, behind, step_ref, res_ref, dir_ref):
-    pieces = []
-    for r in range(NROW):
-        pieces.append(jnp.sum(in_ref[NCL * r : NCL * r + NCL], axis=0))
-    lane = iota((16, 128), 1)
-    image = jnp.concatenate([jnp.where(iota((16, 128), 0) < 9, p, 0.0) for p in pieces], axis=1)
-    both = []
-    for c in range(NCL):
-        rows = jnp.concatenate([in_ref[NCL * r + c, 9:12, :] for r in range(6)], axis=0)
-        both.append(rows)
-    wide = iota((18, 128), 1)
-    both = [
-        jnp.where(wide < CAM, both[2 * g], pltpu.roll(both[2 * g + 1], CAM, 1))
-        for g in range(NCL // 2)
-    ]
-    both = jnp.concatenate(both, axis=1)
-    pad = jnp.zeros((7, NCL * CAM), F32)
-    rhs = jnp.concatenate([both[0:8], both[16:17], pad], axis=0)
-    diag = jnp.concatenate([both[8:16], both[17:18], pad + 1.0], axis=0)
-    start = rhs / diag
-    rz = jnp.sum(rhs * start)
-    alpha = rz / jnp.sum(start * image)
-    residual = rhs - alpha * image
-    second = residual / diag
-    beta = jnp.sum(residual * second) / rz
-    values = (alpha * start, residual, second + beta * start)
-    for r in range(9):
-        at = 128 * r + lane
-        camera = at // 9
-        keep = at - 9 * camera == iota((16, 128), 0)
-        camera = camera[0:8]
-        for value, ref in zip(values, (step_ref, res_ref, dir_ref)):
-            for g in range(NCL // 2):
-                part = value[:, 128 * g : 128 * g + 128]
-                top = jnp.take_along_axis(part[0:8], camera, axis=1)
-                low = jnp.take_along_axis(part[8:16], camera, axis=1)
-                found = jnp.where(keep, jnp.concatenate([top, low], axis=0), 0.0)
-                ref[9 * g + r : 9 * g + r + 1, :] = jnp.sum(found, axis=0, keepdims=True)
+def finish_kernel(in_ref, behind, step_ref, res_ref, dir_ref, both, image):
+    step = pl.program_id(0)
+    rows = in_ref.shape[0] // NCL
+    lane = iota((8, 128), 1)
+    flat = in_ref.reshape(NDEV // 2 * 16, 128)
+    for k in range(rows):
+        r = step * rows + k
+        share = jnp.sum(in_ref[NCL * k : NCL * k + NCL], axis=0)
+        image[pl.ds(r, 16, stride=8), :] = share
+        for t in range(3):
+            at = NCL * 16 * k + 9 + t
+            even = flat[pl.ds(at, 8, stride=32), :]
+            odd = flat[pl.ds(at + 16, 8, stride=32), :]
+            both[3 * r + t] = jnp.where(lane < CAM, even, pltpu.roll(odd, CAM, 1))
+
+    @pl.when(step == pl.num_programs(0) - 1)
+    def _():
+        def total(values):
+            return jnp.sum(sum(values), keepdims=True)
+
+        rhs = [both[i] for i in range(8)] + [both[16]]
+        diag = [both[8 + i] for i in range(8)] + [both[17]]
+        product = [image[8 * i : 8 * i + 8] for i in range(9)]
+        start = [a / b for a, b in zip(rhs, diag)]
+        rz = total([a * b for a, b in zip(rhs, start)])
+        alpha = rz / total([a * b for a, b in zip(start, product)])
+        residual = [a - alpha * b for a, b in zip(rhs, product)]
+        second = [a / b for a, b in zip(residual, diag)]
+        beta = total([a * b for a, b in zip(residual, second)]) / rz
+        values = (
+            [alpha * a for a in start],
+            residual,
+            [a + beta * b for a, b in zip(second, start)],
+        )
+        for r in range(9):
+            at = 128 * r + lane
+            camera = at // 9
+            which = at - 9 * camera
+            for value, ref in zip(values, (step_ref, res_ref, dir_ref)):
+                row = jnp.take_along_axis(value[0], camera, axis=1)
+                for i in range(1, 9):
+                    row = jnp.where(which == i, jnp.take_along_axis(value[i], camera, axis=1), row)
+                ref[pl.ds(r, 8, stride=9), :] = row
 
 
 def finish(incoming, behind):
     return pl.pallas_call(
         finish_kernel,
-        grid=(1,),
-        in_specs=[whole(NDEV, 16, 128), ANY],
+        grid=(2,),
+        in_specs=[pl.BlockSpec((NDEV // 2, 16, 128), lambda s: (s, 0, 0)), ANY],
         out_specs=[whole(72, 128)] * 3,
         out_shape=[jax.ShapeDtypeStruct((72, 128), F32)] * 3,
+        scratch_shapes=[pltpu.VMEM((24, 8, 128), F32), pltpu.VMEM((128, 128), F32)],
         name="finish",
-        **settings(3, 60),
+        **settings(3, 63),
     )(incoming, behind)
 
 
@@ -555,15 +612,15 @@
     my_col = lax.axis_index("col")
     flags = (2 * my_row + jnp.arange(2) == my_col).astype(jnp.int32)
     flags = jnp.concatenate([flags, my_row[None].astype(jnp.int32)])
-    damp = jnp.pad(cam_damp.reshape(CAM, 9).T, ((0, 0), (0, 128 - CAM)), constant_values=1.0)
-    zeros = jnp.zeros((8, 128), F32)
+    damp = cam_damp.reshape(CAM, 9).T
+    zeros = jnp.zeros((8, CAM), F32)
     damp = jnp.concatenate([zeros, damp[0:8], zeros[0:1], damp[8:9], zeros[0:6]], axis=0)
-    first, second = pack(
+    first, dense, found = pack_first(
         jac_cam.transpose(1, 0, 2), jac_pt.transpose(1, 0, 2), resid, point_damp, obs_cluster.T,
         obs_slot,
     )
     first = exchange(first.reshape(NDEV, FIRST, PTS))
-    second = exchange(second.reshape(NDEV, SECOND, PTS))
+    second = exchange(pack_second(dense, found).reshape(NDEV, SECOND // 4, 4, PTS))
     tiles, one = spread(0, flags, cam_damp, (first,))
     two, share = cg_part(flags, one, second, damp)
     shares = exchange(share)

time: 115 us -> 113 us (0.983)
  waiting for transfers between devices: 29.4 us -> 22.6 us
  starting transfers between devices: 23.3 us -> 26.6 us
  Pallas kernels: 56.6 us -> 58.4 us
    all_to_all x3, waiting for transfers between devices: 29.4 us -> 22.6 us  [exchange(): return lax.all_to_all(value, AXES, split_axis=0, concat_axis=0, tiled=True)]
    all_to_all x3, starting transfers between devices: 23.3 us -> 26.6 us  [exchange(): return lax.all_to_all(value, AXES, split_axis=0, concat_axis=0, tiled=True)]
    pallas_call x2 -> x3, Pallas kernels: 8.93 us -> 11.8 us  [the longest x1 5.1 us: pack_first(): pl.pallas_call(pack_first_kernel, grid=(NROW // PAIRS,), in_specs=[whole(...]
  transfers between devices with their start and end apart: 3 -> 3, of which waited for: 2 -> 2; matrix products, arithmetic and copies ran while one was open for 2% -> 2% of each run, Pallas kernels for 35% -> 39%
where the time goes in v5:
time: 113 us; the launch traced here: 111 us
  Pallas kernels  58.4 us (52%)
  starting transfers between devices  26.6 us (24%)
  waiting for transfers between devices  22.6 us (20%)
  local copies, waits for them, and re-layouts  2.02 us (2%)
    pallas_call x2, Pallas kernels, spread(): pl.pallas_call(functools.partial(spread_kernel, e), grid=(steps,), in_spe...  39.3 us
    all_to_all x3, starting transfers between devices, exchange(): return lax.all_to_all(value, AXES, split_axis=0, concat_axis=0, tiled=True)  26.6 us
    all_to_all x3, waiting for transfers between devices, exchange(): return lax.all_to_all(value, AXES, split_axis=0, concat_axis=0, tiled=True)  22.6 us
    pallas_call x1, Pallas kernels, cg_part(): pl.pallas_call(cg_kernel, grid=(steps,), in_specs=[pl.BlockSpec(memory_sp...  7.31 us
    pallas_call x1, Pallas kernels, pack_first(): pl.pallas_call(pack_first_kernel, grid=(NROW // PAIRS,), in_specs=[whole(...  5.1 us
    pallas_call x1, Pallas kernels, pack_second(): pl.pallas_call(pack_second_kernel, grid=(NROW // PAIRS,), in_specs=[whole...  4.05 us
    pallas_call x1, Pallas kernels, finish(): pl.pallas_call(finish_kernel, grid=(2,), in_specs=[pl.BlockSpec((NDEV //...  2.62 us
  transfers between devices with their start and end apart: 3, of which 2 were waited for; matrix products, arithmetic and copies ran while one was open for 2% of the time, Pallas kernels for 39%

profile of v5, /device:TPU:24, one launch (start us, length us, event | category | flops | bytes accessed | tf_op | source)
XLA Modules:
  0.0 110.9 jit_solution(18003468484434138582)
XLA Ops:
  0.6 5.1 %pack_first.1 = (f32[8,16,32,128]{3,2,1,0:T(8,128)}, f32[29,2,8,128]{3,2,1,0:T(8,128)}, s32[2,8,128]{2,1,0:T(8,128)}) custom-call(f32[18,8,128]{2,1,0:T(8,128)} %bitcast.17, f32[6,8,128]{2,1,0:T(8,128)} %bitcast.18, f32[8,2,128]{2,1,0:T(2,128)} %rs.1, f32[3,128]{1,0:T(4,128)} %damp.1, s32[8,128]{1,0:T(8,128)} %bitcast.19, s32[8,128]{1,0:T(8,128)} %slot.1), custom_call_target="tpu_custom_call" | custom-call | flops 5000000000 | bytes 1000000 | tf_op jit(solution)/shard_map/pack_first/pallas_call | solution.py:222
  5.7 0.0 copy-start.1
  5.7 10.3 %all-to-all-start = ((f32[128,32,128]{2,1,0:T(8,128)}), f32[128,32,128]{2,1,0:T(8,128)S(1)}, u32[]{:S(2)}, u32[]{:S(2)}) async-start(f32[128,32,128]{2,1,0:T(8,128)} %bitcast.13), calls=%async_computation | async-start | bytes 4194304 | tf_op jit(solution)/shard_map/all_to_all | solution.py:261
  16.0 0.0 copy-done.1
  16.1 0.1 reshape.28
  16.2 0.1 copy.13
  16.3 1.8 %concatenate.7.damp_ref = f32[24,64]{1,0:T(8,128)} concatenate(f32[8,64]{1,0:T(8,128)S(1)} %broadcast_in_dim.10, f32[8,64]{1,0:T(8,128)S(1)} %slice.16, f32[1,64]{1,0:T(1,128)S(1)} %slice.13, f32[1,64]{1,0:T(1,128)S(1)} %slice.17, f32[6,64]{1,0:T(8,128)S(1)} %slice.15), dimensions={0} | concatenate | bytes 12288 | tf_op jit(solution)/shard_map/concatenate | solution.py:617
  18.1 0.6 pad_add_fusion.flag_ref
  18.7 4.0 %pack_second.1 = f32[8,16,5,4,128]{4,3,2,1,0:T(4,128)} custom-call(f32[29,2,8,128]{3,2,1,0:T(8,128)} %get-tuple-element.18.dense, s32[2,8,128]{2,1,0:T(8,128)} %get-tuple-element.19.found_ref), custom_call_target="tpu_custom_call" | custom-call | flops 5000000000 | bytes 1000000 | tf_op jit(solution)/shard_map/pack_second/pallas_call | solution.py:246
  22.7 22.3 %all-to-all-done.refs_0_ = f32[128,32,128]{2,1,0:T(8,128)S(1)} async-done(((f32[128,32,128]{2,1,0:T(8,128)}), f32[128,32,128]{2,1,0:T(8,128)S(1)}, u32[]{:S(2)}, u32[]{:S(2)}) %all-to-all-start) | async-done | bytes 2097184 | tf_op jit(solution)/shard_map/all_to_all | solution.py:261
  45.1 0.0 copy-start
  45.1 6.3 %all-to-all-start.1 = ((f32[128,5,4,128]{3,2,1,0:T(4,128)}), f32[128,5,4,128]{3,2,1,0:T(4,128)}, u32[]{:S(2)}, u32[]{:S(2)}) async-start(f32[128,5,4,128]{3,2,1,0:T(4,128)} %bitcast.14), calls=%async_computation.1 | async-start | bytes 2621440 | tf_op jit(solution)/shard_map/all_to_all | solution.py:261
  51.4 0.0 copy-done
  51.4 20.1 %spread.2 = (f32[2,576,576]{2,1,0:T(8,128)}, f32[41,12288]{1,0:T(8,128)}) custom-call(s32[3]{0:T(128)} %pad_add_fusion.flag_ref, f32[1,576]{1,0:T(1,128)} %damp_ref.3, f32[128,32,128]{2,1,0:T(8,128)} %copy-done), custom_call_target="tpu_custom_call" | custom-call | flops 20000000000 | bytes 1000000 | tf_op jit(solution)/shard_map/spread/pallas_call | solution.py:534
  71.6 0.3 all-to-all-done.1.in_ref
  71.8 7.3 %cg.1 = (f32[26,12288]{1,0:T(8,128)}, f32[128,16,128]{2,1,0:T(8,128)}) custom-call(s32[3]{0:T(128)} %pad_add_fusion.flag_ref, f32[41,12288]{1,0:T(8,128)} %get-tuple-element.17.one.refs_0_, f32[128,5,4,128]{3,2,1,0:T(4,128)} %all-to-all-done.1.in_ref, f32[24,64]{1,0:T(8,128)} %concatenate.7.damp_ref), custom_call_target="tpu_custom_call" | custom-call | flops 6000000000 | bytes 1000000 | tf_op jit(solution)/shard_map/cg/pallas_call | solution.py:374
  79.1 10.0 %all-to-all-start.2 = ((f32[128,16,128]{2,1,0:T(8,128)}), f32[128,16,128]{2,1,0:T(8,128)}, u32[]{:S(2)}, u32[]{:S(2)}) async-start(f32[128,16,128]{2,1,0:T(8,128)} %get-tuple-element.22.refs_3_), calls=%async_computation.2 | async-start | bytes 2097152 | tf_op jit(solution)/shard_map/all_to_all | solution.py:261
  89.1 19.2 %spread.3 = (f32[2,576,576]{2,1,0:T(8,128)}, f32[8,128]{1,0:T(8,128)}) custom-call(s32[3]{0:T(128)} %pad_add_fusion.flag_ref, f32[1,576]{1,0:T(1,128)} %damp_ref.3, f32[41,12288]{1,0:T(8,128)} %get-tuple-element.17.one.refs_0_, f32[26,12288]{1,0:T(8,128)} %get-tuple-element.20.refs_1_, ...), custom_call_target="tpu_custom_call", output_to_operand_aliasing={{0}: (4, {})} | custom-call | flops 20000000000 | bytes 1000000 | tf_op jit(solution)/shard_map/spread/pallas_call | solution.py:534
  108.3 0.0 all-to-all-done.2.in_ref
  108.3 2.6 %finish.1 = (f32[72,128]{1,0:T(8,128)}, f32[72,128]{1,0:T(8,128)}, f32[72,128]{1,0:T(8,128)}) custom-call(f32[128,16,128]{2,1,0:T(8,128)} %all-to-all-done.2.in_ref, f32[8,128]{1,0:T(8,128)} %get-tuple-element.24.behind), custom_call_target="tpu_custom_call" | custom-call | flops 3000000000 | bytes 1000000 | tf_op jit(solution)/shard_map/finish/pallas_call | solution.py:598
  (7 shorter events, 0.0 us)
Async XLA Ops:
  5.7 10.3 %copy-start.1 = (f32[1,576]{1,0:T(1,128)S(1)}, f32[1,576]{1,0:T(1,128)}, u32[]{:S(2)}) copy-start(f32[1,576]{1,0:T(1,128)} %damp_ref.3) | copy-start | bytes 6916
  5.7 39.3 %all-to-all-start = ((f32[128,32,128]{2,1,0:T(8,128)}), f32[128,32,128]{2,1,0:T(8,128)S(1)}, u32[]{:S(2)}, u32[]{:S(2)}) async-start(f32[128,32,128]{2,1,0:T(8,128)} %bitcast.13), calls=%async_computation | async-start | bytes 4194304 | tf_op jit(solution)/shard_map/all_to_all | solution.py:261
  45.1 6.4 %copy-start = (f32[128,32,128]{2,1,0:T(8,128)}, f32[128,32,128]{2,1,0:T(8,128)S(1)}, u32[]{:S(2)}) copy-start(f32[128,32,128]{2,1,0:T(8,128)S(1)} %all-to-all-done.refs_0_) | copy-start | bytes 6291460
  45.1 26.8 %all-to-all-start.1 = ((f32[128,5,4,128]{3,2,1,0:T(4,128)}), f32[128,5,4,128]{3,2,1,0:T(4,128)}, u32[]{:S(2)}, u32[]{:S(2)}) async-start(f32[128,5,4,128]{3,2,1,0:T(4,128)} %bitcast.14), calls=%async_computation.1 | async-start | bytes 2621440 | tf_op jit(solution)/shard_map/all_to_all | solution.py:261
  79.1 29.2 %all-to-all-start.2 = ((f32[128,16,128]{2,1,0:T(8,128)}), f32[128,16,128]{2,1,0:T(8,128)}, u32[]{:S(2)}, u32[]{:S(2)}) async-start(f32[128,16,128]{2,1,0:T(8,128)} %get-tuple-element.22.refs_3_), calls=%async_computation.2 | async-start | bytes 2097152 | tf_op jit(solution)/shard_map/all_to_all | solution.py:261

commit v6 on v5

--- a/solution.py
+++ b/solution.py
@@ -21,8 +21,8 @@
 F32 = jnp.float32
 NT = (((1,), (1,)), ((), ()))
 MIB = 1 << 20
-SRC = 32
-PAIRS = 2
+SRC = 64
+PAIRS = 8
 LANES = SRC * CAP
 GROUP = 3
 ANY = pl.BlockSpec(memory_space=pl.ANY)
@@ -338,8 +338,7 @@
         kept[...] = jnp.concatenate([total, jnp.zeros_like(total)], axis=1)
         x8, x9 = total[0:8] / total[8:16], total[16:17] / total[17:18]
         x = halves(jnp.concatenate([x8, x9, jnp.zeros((7, CAM), F32)], axis=0))
-        image[...] = jnp.zeros_like(image)
-
+        parts, spots = [[], []], [[], []]
         for at in range(NDEV // SRC):
             rows1, rows2 = keep1.at[at], keep2.at[at]
             got = jnp.dot(x, hits[at], preferred_element_type=F32)
@@ -352,13 +351,16 @@
                 z0, z1 = m[0] * v0 + m[1] * v1, m[2] * v0 + m[3] * v1
                 out8 = a0 * lanes_of(z0, 8) + a1 * lanes_of(z1, 8)
                 terms = [out8, l0 * z0 + l1 * z1, jnp.zeros((7, LANES), F32)]
-                image[e] += lax.dot_general(
-                    halves(jnp.concatenate(terms, axis=0)),
-                    hot(slot.astype(jnp.int32), CAM),
-                    NT,
-                    preferred_element_type=F32,
-                )
-
+                parts[e].append(halves(jnp.concatenate(terms, axis=0)))
+                spots[e].append(hot(slot.astype(jnp.int32), CAM))
+
+        for e in range(2):
+            image[e] = lax.dot_general(
+                jnp.concatenate(parts[e], axis=1),
+                jnp.concatenate(spots[e], axis=1),
+                NT,
+                preferred_element_type=F32,
+            )
         extra = jnp.concatenate([damp[8:16] * x8, damp[17:18] * x9, jnp.zeros((7, CAM), F32)], axis=0)
         y = [
             image[e, 0:16] + image[e, 16:32] + jnp.where(flag_ref[e] == 1, extra, 0.0)

time: 113 us -> 110 us (0.973)
  Pallas kernels: 58.4 us -> 56 us
    pallas_call x1, Pallas kernels: 7.31 us -> 6.05 us  [cg_part(): pl.pallas_call(cg_kernel, grid=(steps,), in_specs=[pl.BlockSpec(memory_sp...]
where the time goes in v6:
time: 110 us; the launch traced here: 108 us
  Pallas kernels  56 us (51%)
  starting transfers between devices  26 us (24%)
  waiting for transfers between devices  23.1 us (21%)
  local copies, waits for them, and re-layouts  2.02 us (2%)
    pallas_call x2, Pallas kernels, spread(): pl.pallas_call(functools.partial(spread_kernel, e), grid=(steps,), in_spe...  38.6 us
    all_to_all x3, starting transfers between devices, exchange(): return lax.all_to_all(value, AXES, split_axis=0, concat_axis=0, tiled=True)  26 us
    all_to_all x3, waiting for transfers between devices, exchange(): return lax.all_to_all(value, AXES, split_axis=0, concat_axis=0, tiled=True)  23.1 us
    pallas_call x1, Pallas kernels, cg_part(): pl.pallas_call(cg_kernel, grid=(steps,), in_specs=[pl.BlockSpec(memory_sp...  6.05 us
    pallas_call x1, Pallas kernels, pack_first(): pl.pallas_call(pack_first_kernel, grid=(NROW // PAIRS,), in_specs=[whole(...  4.6 us
    pallas_call x1, Pallas kernels, pack_second(): pl.pallas_call(pack_second_kernel, grid=(NROW // PAIRS,), in_specs=[whole...  4.14 us
    pallas_call x1, Pallas kernels, finish(): pl.pallas_call(finish_kernel, grid=(2,), in_specs=[pl.BlockSpec((NDEV //...  2.62 us
  transfers between devices with their start and end apart: 3, of which 2 were waited for; matrix products, arithmetic and copies ran while one was open for 2% of the time, Pallas kernels for 39%

profile of v6, /device:TPU:24, one launch (start us, length us, event | category | flops | bytes accessed | tf_op | source)
XLA Modules:
  0.0 108.5 jit_solution(1253513238406843874)
XLA Ops:
  0.6 4.6 %pack_first.1 = (f32[8,16,32,128]{3,2,1,0:T(8,128)}, f32[29,2,8,128]{3,2,1,0:T(8,128)}, s32[2,8,128]{2,1,0:T(8,128)}) custom-call(f32[18,8,128]{2,1,0:T(8,128)} %bitcast.17, f32[6,8,128]{2,1,0:T(8,128)} %bitcast.18, f32[8,2,128]{2,1,0:T(2,128)} %rs.1, f32[3,128]{1,0:T(4,128)} %damp.1, s32[8,128]{1,0:T(8,128)} %bitcast.19, s32[8,128]{1,0:T(8,128)} %slot.1), custom_call_target="tpu_custom_call" | custom-call | flops 5000000000 | bytes 1000000 | tf_op jit(solution)/shard_map/pack_first/pallas_call | solution.py:222
  5.2 0.0 copy-start.1
  5.2 10.3 %all-to-all-start = ((f32[128,32,128]{2,1,0:T(8,128)}), f32[128,32,128]{2,1,0:T(8,128)S(1)}, u32[]{:S(2)}, u32[]{:S(2)}) async-start(f32[128,32,128]{2,1,0:T(8,128)} %bitcast.13), calls=%async_computation | async-start | bytes 4194304 | tf_op jit(solution)/shard_map/all_to_all | solution.py:261
  15.5 0.0 copy-done.1
  15.5 0.1 reshape.28
  15.7 0.1 copy.13
  15.8 1.8 %concatenate.7.damp_ref = f32[24,64]{1,0:T(8,128)} concatenate(f32[8,64]{1,0:T(8,128)S(1)} %broadcast_in_dim.10, f32[8,64]{1,0:T(8,128)S(1)} %slice.16, f32[1,64]{1,0:T(1,128)S(1)} %slice.13, f32[1,64]{1,0:T(1,128)S(1)} %slice.17, f32[6,64]{1,0:T(8,128)S(1)} %slice.15), dimensions={0} | concatenate | bytes 12288 | tf_op jit(solution)/shard_map/concatenate | solution.py:619
  17.6 0.6 pad_add_fusion.flag_ref
  18.2 4.1 %pack_second.1 = f32[8,16,5,4,128]{4,3,2,1,0:T(4,128)} custom-call(f32[29,2,8,128]{3,2,1,0:T(8,128)} %get-tuple-element.18.dense, s32[2,8,128]{2,1,0:T(8,128)} %get-tuple-element.19.found_ref), custom_call_target="tpu_custom_call" | custom-call | flops 5000000000 | bytes 1000000 | tf_op jit(solution)/shard_map/pack_second/pallas_call | solution.py:246
  22.3 22.2 %all-to-all-done.refs_0_ = f32[128,32,128]{2,1,0:T(8,128)S(1)} async-done(((f32[128,32,128]{2,1,0:T(8,128)}), f32[128,32,128]{2,1,0:T(8,128)S(1)}, u32[]{:S(2)}, u32[]{:S(2)}) %all-to-all-start) | async-done | bytes 2097184 | tf_op jit(solution)/shard_map/all_to_all | solution.py:261
  44.6 0.0 copy-start
  44.6 6.4 %all-to-all-start.1 = ((f32[128,5,4,128]{3,2,1,0:T(4,128)}), f32[128,5,4,128]{3,2,1,0:T(4,128)}, u32[]{:S(2)}, u32[]{:S(2)}) async-start(f32[128,5,4,128]{3,2,1,0:T(4,128)} %bitcast.14), calls=%async_computation.1 | async-start | bytes 2621440 | tf_op jit(solution)/shard_map/all_to_all | solution.py:261
  50.9 0.0 copy-done
  50.9 19.5 %spread.2 = (f32[2,576,576]{2,1,0:T(8,128)}, f32[41,12288]{1,0:T(8,128)}) custom-call(s32[3]{0:T(128)} %pad_add_fusion.flag_ref, f32[1,576]{1,0:T(1,128)} %damp_ref.3, f32[128,32,128]{2,1,0:T(8,128)} %copy-done), custom_call_target="tpu_custom_call" | custom-call | flops 20000000000 | bytes 1000000 | tf_op jit(solution)/shard_map/spread/pallas_call | solution.py:536
  70.4 0.9 all-to-all-done.1.in_ref
  71.3 6.0 %cg.1 = (f32[26,12288]{1,0:T(8,128)}, f32[128,16,128]{2,1,0:T(8,128)}) custom-call(s32[3]{0:T(128)} %pad_add_fusion.flag_ref, f32[41,12288]{1,0:T(8,128)} %get-tuple-element.17.one.refs_0_, f32[128,5,4,128]{3,2,1,0:T(4,128)} %all-to-all-done.1.in_ref, f32[24,64]{1,0:T(8,128)} %concatenate.7.damp_ref), custom_call_target="tpu_custom_call" | custom-call | flops 6000000000 | bytes 1000000 | tf_op jit(solution)/shard_map/cg/pallas_call | solution.py:376
  77.4 9.3 %all-to-all-start.2 = ((f32[128,16,128]{2,1,0:T(8,128)}), f32[128,16,128]{2,1,0:T(8,128)}, u32[]{:S(2)}, u32[]{:S(2)}) async-start(f32[128,16,128]{2,1,0:T(8,128)} %get-tuple-element.22.refs_3_), calls=%async_computation.2 | async-start | bytes 2097152 | tf_op jit(solution)/shard_map/all_to_all | solution.py:261
  86.7 19.2 %spread.3 = (f32[2,576,576]{2,1,0:T(8,128)}, f32[8,128]{1,0:T(8,128)}) custom-call(s32[3]{0:T(128)} %pad_add_fusion.flag_ref, f32[1,576]{1,0:T(1,128)} %damp_ref.3, f32[41,12288]{1,0:T(8,128)} %get-tuple-element.17.one.refs_0_, f32[26,12288]{1,0:T(8,128)} %get-tuple-element.20.refs_1_, ...), custom_call_target="tpu_custom_call", output_to_operand_aliasing={{0}: (4, {})} | custom-call | flops 20000000000 | bytes 1000000 | tf_op jit(solution)/shard_map/spread/pallas_call | solution.py:536
  105.9 0.0 all-to-all-done.2.in_ref
  105.9 2.6 %finish.1 = (f32[72,128]{1,0:T(8,128)}, f32[72,128]{1,0:T(8,128)}, f32[72,128]{1,0:T(8,128)}) custom-call(f32[128,16,128]{2,1,0:T(8,128)} %all-to-all-done.2.in_ref, f32[8,128]{1,0:T(8,128)} %get-tuple-element.24.behind), custom_call_target="tpu_custom_call" | custom-call | flops 3000000000 | bytes 1000000 | tf_op jit(solution)/shard_map/finish/pallas_call | solution.py:600
  (7 shorter events, 0.0 us)
Async XLA Ops:
  5.2 10.3 %copy-start.1 = (f32[1,576]{1,0:T(1,128)S(1)}, f32[1,576]{1,0:T(1,128)}, u32[]{:S(2)}) copy-start(f32[1,576]{1,0:T(1,128)} %damp_ref.3) | copy-start | bytes 6916
  5.2 39.3 %all-to-all-start = ((f32[128,32,128]{2,1,0:T(8,128)}), f32[128,32,128]{2,1,0:T(8,128)S(1)}, u32[]{:S(2)}, u32[]{:S(2)}) async-start(f32[128,32,128]{2,1,0:T(8,128)} %bitcast.13), calls=%async_computation | async-start | bytes 4194304 | tf_op jit(solution)/shard_map/all_to_all | solution.py:261
  44.6 6.4 %copy-start = (f32[128,32,128]{2,1,0:T(8,128)}, f32[128,32,128]{2,1,0:T(8,128)S(1)}, u32[]{:S(2)}) copy-start(f32[128,32,128]{2,1,0:T(8,128)S(1)} %all-to-all-done.refs_0_) | copy-start | bytes 6291460
  44.6 26.8 %all-to-all-start.1 = ((f32[128,5,4,128]{3,2,1,0:T(4,128)}), f32[128,5,4,128]{3,2,1,0:T(4,128)}, u32[]{:S(2)}, u32[]{:S(2)}) async-start(f32[128,5,4,128]{3,2,1,0:T(4,128)} %bitcast.14), calls=%async_computation.1 | async-start | bytes 2621440 | tf_op jit(solution)/shard_map/all_to_all | solution.py:261
  77.4 28.5 %all-to-all-start.2 = ((f32[128,16,128]{2,1,0:T(8,128)}), f32[128,16,128]{2,1,0:T(8,128)}, u32[]{:S(2)}, u32[]{:S(2)}) async-start(f32[128,16,128]{2,1,0:T(8,128)} %get-tuple-element.22.refs_3_), calls=%async_computation.2 | async-start | bytes 2097152 | tf_op jit(solution)/shard_map/all_to_all | solution.py:261

commit v7 on v6

--- a/solution.py
+++ b/solution.py
@@ -547,7 +547,7 @@
         ],
         input_output_aliases={4: 0} if e else {},
         name="spread",
-        **settings(20, 60),
+        **settings(20, 44),
     )(flags, damp, *args)
 
 

time: 110 us -> 113 us (1.027)
  local copies, waits for them, and re-layouts: 2.02 us -> 7.12 us
  Pallas kernels: 56 us -> 54.1 us
    unnamed x4 -> x16, local copies, waits for them, and re-layouts: 0.01 us -> 5.11 us
    pallas_call x2, Pallas kernels: 38.6 us -> 36.7 us  [spread(): pl.pallas_call(functools.partial(spread_kernel, e), grid=(steps,), in_spe...]
  transfers between devices with their start and end apart: 3 -> 3, of which waited for: 2 -> 2; matrix products, arithmetic and copies ran while one was open for 2% -> 2% of each run, Pallas kernels for 39% -> 37%
where the time goes in v7:
time: 113 us; the launch traced here: 112 us
  Pallas kernels  54.1 us (48%)
  starting transfers between devices  26.3 us (23%)
  waiting for transfers between devices  23.3 us (21%)
  local copies, waits for them, and re-layouts  7.12 us (6%)
    pallas_call x2, Pallas kernels, spread(): pl.pallas_call(functools.partial(spread_kernel, e), grid=(steps,), in_spe...  36.7 us
    all_to_all x3, starting transfers between devices, exchange(): return lax.all_to_all(value, AXES, split_axis=0, concat_axis=0, tiled=True)  26.3 us
    all_to_all x3, waiting for transfers between devices, exchange(): return lax.all_to_all(value, AXES, split_axis=0, concat_axis=0, tiled=True)  23.3 us
    pallas_call x1, Pallas kernels, cg_part(): pl.pallas_call(cg_kernel, grid=(steps,), in_specs=[pl.BlockSpec(memory_sp...  6.04 us
    unnamed x16, local copies, waits for them, and re-layouts  5.11 us
    pallas_call x1, Pallas kernels, pack_first(): pl.pallas_call(pack_first_kernel, grid=(NROW // PAIRS,), in_specs=[whole(...  4.6 us
    pallas_call x1, Pallas kernels, pack_second(): pl.pallas_call(pack_second_kernel, grid=(NROW // PAIRS,), in_specs=[whole...  4.14 us
    pallas_call x1, Pallas kernels, finish(): pl.pallas_call(finish_kernel, grid=(2,), in_specs=[pl.BlockSpec((NDEV //...  2.61 us
  transfers between devices with their start and end apart: 3, of which 2 were waited for; matrix products, arithmetic and copies ran while one was open for 2% of the time, Pallas kernels for 37%

profile of v7, /device:TPU:24, one launch (start us, length us, event | category | flops | bytes accessed | tf_op | source)
XLA Modules:
  0.0 111.7 jit_solution(489916627729332806)
XLA Ops:
  0.6 4.6 %pack_first.1 = (f32[8,16,32,128]{3,2,1,0:T(8,128)}, f32[29,2,8,128]{3,2,1,0:T(8,128)}, s32[2,8,128]{2,1,0:T(8,128)}) custom-call(f32[18,8,128]{2,1,0:T(8,128)} %bitcast.17, f32[6,8,128]{2,1,0:T(8,128)} %bitcast.18, f32[8,2,128]{2,1,0:T(2,128)} %rs.1, f32[3,128]{1,0:T(4,128)} %damp.1, s32[8,128]{1,0:T(8,128)} %bitcast.19, s32[8,128]{1,0:T(8,128)} %slot.1), custom_call_target="tpu_custom_call" | custom-call | flops 5000000000 | bytes 1000000 | tf_op jit(solution)/shard_map/pack_first/pallas_call | solution.py:222
  5.2 0.0 copy-start.1
  5.2 10.3 %all-to-all-start = ((f32[128,32,128]{2,1,0:T(8,128)}), f32[128,32,128]{2,1,0:T(8,128)S(1)}, u32[]{:S(2)}, u32[]{:S(2)}) async-start(f32[128,32,128]{2,1,0:T(8,128)} %bitcast.13), calls=%async_computation | async-start | bytes 4194304 | tf_op jit(solution)/shard_map/all_to_all | solution.py:261
  15.5 0.0 copy-done.1
  15.6 0.1 reshape.28
  15.7 0.1 copy.13
  15.8 1.8 %concatenate.7.damp_ref = f32[24,64]{1,0:T(8,128)} concatenate(f32[8,64]{1,0:T(8,128)S(1)} %broadcast_in_dim.10, f32[8,64]{1,0:T(8,128)S(1)} %slice.16, f32[1,64]{1,0:T(1,128)S(1)} %slice.13, f32[1,64]{1,0:T(1,128)S(1)} %slice.17, f32[6,64]{1,0:T(8,128)S(1)} %slice.15), dimensions={0} | concatenate | bytes 12288 | tf_op jit(solution)/shard_map/concatenate | solution.py:619
  17.6 0.1 pad_add_fusion.flag_ref
  17.7 0.0 copy-start.2
  17.7 4.1 %pack_second.1 = f32[8,16,5,4,128]{4,3,2,1,0:T(4,128)} custom-call(f32[29,2,8,128]{3,2,1,0:T(8,128)} %get-tuple-element.18.dense, s32[2,8,128]{2,1,0:T(8,128)} %get-tuple-element.19.found_ref), custom_call_target="tpu_custom_call" | custom-call | flops 5000000000 | bytes 1000000 | tf_op jit(solution)/shard_map/pack_second/pallas_call | solution.py:246
  21.8 22.7 %all-to-all-done.refs_0_ = f32[128,32,128]{2,1,0:T(8,128)S(1)} async-done(((f32[128,32,128]{2,1,0:T(8,128)}), f32[128,32,128]{2,1,0:T(8,128)S(1)}, u32[]{:S(2)}, u32[]{:S(2)}) %all-to-all-start) | async-done | bytes 2097184 | tf_op jit(solution)/shard_map/all_to_all | solution.py:261
  44.6 6.3 %all-to-all-start.1 = ((f32[128,5,4,128]{3,2,1,0:T(4,128)}), f32[128,5,4,128]{3,2,1,0:T(4,128)}, u32[]{:S(2)}, u32[]{:S(2)}) async-start(f32[128,5,4,128]{3,2,1,0:T(4,128)} %bitcast.14), calls=%async_computation.1 | async-start | bytes 2621440 | tf_op jit(solution)/shard_map/all_to_all | solution.py:261
  50.9 0.0 copy-done.2
  50.9 18.4 %spread.2 = (f32[2,576,576]{2,1,0:T(8,128)}, f32[41,12288]{1,0:T(8,128)S(1)}) custom-call(s32[3]{0:T(128)S(1)} %pad_add_fusion.flag_ref, f32[1,576]{1,0:T(1,128)S(1)} %copy-done.1, f32[128,32,128]{2,1,0:T(8,128)S(1)} %all-to-all-done.refs_0_), custom_call_target="tpu_custom_call" | custom-call | flops 20000000000 | bytes 1000000 | tf_op jit(solution)/shard_map/spread/pallas_call | solution.py:536
  69.3 0.0 copy-start.4
  69.3 1.4 %copy-done.4 = f32[41,12288]{1,0:T(8,128)} copy-done((f32[41,12288]{1,0:T(8,128)}, f32[41,12288]{1,0:T(8,128)S(1)}, u32[]{:S(2)}) %copy-start.4) | copy-done | bytes 2015256
  70.8 0.5 all-to-all-done.1.in_ref
  71.3 6.0 %cg.1 = (f32[26,12288]{1,0:T(8,128)}, f32[128,16,128]{2,1,0:T(8,128)}) custom-call(s32[3]{0:T(128)} %copy-done.2, f32[41,12288]{1,0:T(8,128)} %copy-done.4, f32[128,5,4,128]{3,2,1,0:T(4,128)} %all-to-all-done.1.in_ref, f32[24,64]{1,0:T(8,128)} %concatenate.7.damp_ref), custom_call_target="tpu_custom_call" | custom-call | flops 6000000000 | bytes 1000000 | tf_op jit(solution)/shard_map/cg/pallas_call | solution.py:376
  77.3 0.0 copy-start
  77.3 0.0 copy-start.3
  77.3 9.8 %all-to-all-start.2 = ((f32[128,16,128]{2,1,0:T(8,128)}), f32[128,16,128]{2,1,0:T(8,128)}, u32[]{:S(2)}, u32[]{:S(2)}) async-start(f32[128,16,128]{2,1,0:T(8,128)} %get-tuple-element.22.refs_3_), calls=%async_computation.2 | async-start | bytes 2097152 | tf_op jit(solution)/shard_map/all_to_all | solution.py:261
  87.1 0.0 copy-done
  87.1 0.0 copy-done.3
  87.1 0.0 copy-start.5
  87.1 1.7 %copy-done.5 = f32[41,12288]{1,0:T(8,128)S(1)} copy-done((f32[41,12288]{1,0:T(8,128)S(1)}, f32[41,12288]{1,0:T(8,128)}, u32[]{:S(2)}) %copy-start.5) | copy-done | bytes 2015256
  88.8 0.0 copy-start.6
  88.8 1.4 %copy-done.6 = f32[26,12288]{1,0:T(8,128)S(1)} copy-done((f32[26,12288]{1,0:T(8,128)S(1)}, f32[26,12288]{1,0:T(8,128)}, u32[]{:S(2)}) %copy-start.6) | copy-done | bytes 1277976
  90.2 18.3 %spread.3 = (f32[2,576,576]{2,1,0:T(8,128)}, f32[8,128]{1,0:T(8,128)S(1)}) custom-call(s32[3]{0:T(128)S(1)} %copy-done.3, f32[1,576]{1,0:T(1,128)S(1)} %copy-done.1, f32[41,12288]{1,0:T(8,128)S(1)} %copy-done.5, f32[26,12288]{1,0:T(8,128)S(1)} %copy-done.6, f32[2,576,576]{2,1,0:T(8,128)} %get-tuple-element.21.refs_2_, ...), custom_call_target="tpu_custom_call", output_to_operand_aliasing={{0}: (4, {})} | custom-call | flops 20000000000 | bytes 1000000 | tf_op jit(solution)/shard_map/spread/pallas_call | solution.py:536
  108.5 0.0 copy-start.7
  108.5 0.6 copy-done.7
  109.1 0.0 all-to-all-done.2.in_ref
  109.1 2.6 %finish.1 = (f32[72,128]{1,0:T(8,128)}, f32[72,128]{1,0:T(8,128)}, f32[72,128]{1,0:T(8,128)}) custom-call(f32[128,16,128]{2,1,0:T(8,128)} %all-to-all-done.2.in_ref, f32[8,128]{1,0:T(8,128)} %copy-done.7), custom_call_target="tpu_custom_call" | custom-call | flops 3000000000 | bytes 1000000 | tf_op jit(solution)/shard_map/finish/pallas_call | solution.py:600
  (7 shorter events, 0.0 us)
Async XLA Ops:
  5.2 10.3 %copy-start.1 = (f32[1,576]{1,0:T(1,128)S(1)}, f32[1,576]{1,0:T(1,128)}, u32[]{:S(2)}) copy-start(f32[1,576]{1,0:T(1,128)} %damp_ref.3) | copy-start | bytes 6916
  5.2 39.3 %all-to-all-start = ((f32[128,32,128]{2,1,0:T(8,128)}), f32[128,32,128]{2,1,0:T(8,128)S(1)}, u32[]{:S(2)}, u32[]{:S(2)}) async-start(f32[128,32,128]{2,1,0:T(8,128)} %bitcast.13), calls=%async_computation | async-start | bytes 4194304 | tf_op jit(solution)/shard_map/all_to_all | solution.py:261
  17.7 33.2 %copy-start.2 = (s32[3]{0:T(128)}, s32[3]{0:T(128)S(1)}, u32[]{:S(2)}) copy-start(s32[3]{0:T(128)S(1)} %pad_add_fusion.flag_ref) | copy-start | bytes 40
  44.6 26.7 %all-to-all-start.1 = ((f32[128,5,4,128]{3,2,1,0:T(4,128)}), f32[128,5,4,128]{3,2,1,0:T(4,128)}, u32[]{:S(2)}, u32[]{:S(2)}) async-start(f32[128,5,4,128]{3,2,1,0:T(4,128)} %bitcast.14), calls=%async_computation.1 | async-start | bytes 2621440 | tf_op jit(solution)/shard_map/all_to_all | solution.py:261
  69.3 1.4 %copy-start.4 = (f32[41,12288]{1,0:T(8,128)}, f32[41,12288]{1,0:T(8,128)S(1)}, u32[]{:S(2)}) copy-start(f32[41,12288]{1,0:T(8,128)S(1)} %get-tuple-element.17.one.refs_0_) | copy-start | bytes 6045700
  77.3 9.8 %copy-start = (f32[128,16,128]{2,1,0:T(8,128)S(1)}, f32[128,16,128]{2,1,0:T(8,128)}, u32[]{:S(2)}) copy-start(f32[128,16,128]{2,1,0:T(8,128)} %get-tuple-element.22.refs_3_) | copy-start | bytes 3145732
  77.3 9.8 %copy-start.3 = (s32[3]{0:T(128)S(1)}, s32[3]{0:T(128)}, u32[]{:S(2)}) copy-start(s32[3]{0:T(128)} %copy-done.2) | copy-start | bytes 40
  77.3 31.8 %all-to-all-start.2 = ((f32[128,16,128]{2,1,0:T(8,128)}), f32[128,16,128]{2,1,0:T(8,128)}, u32[]{:S(2)}, u32[]{:S(2)}) async-start(f32[128,16,128]{2,1,0:T(8,128)} %get-tuple-element.22.refs_3_), calls=%async_computation.2 | async-start | bytes 2097152 | tf_op jit(solution)/shard_map/all_to_all | solution.py:261
  87.1 1.7 %copy-start.5 = (f32[41,12288]{1,0:T(8,128)S(1)}, f32[41,12288]{1,0:T(8,128)}, u32[]{:S(2)}) copy-start(f32[41,12288]{1,0:T(8,128)} %copy-done.4) | copy-start | bytes 6045700
  88.8 1.4 %copy-start.6 = (f32[26,12288]{1,0:T(8,128)S(1)}, f32[26,12288]{1,0:T(8,128)}, u32[]{:S(2)}) copy-start(f32[26,12288]{1,0:T(8,128)} %get-tuple-element.20.refs_1_) | copy-start | bytes 3833860
  108.5 0.6 copy-start.7
